TPU v7x, 32 devices: a whole 2x2x4 slice. The times are simulated.
32 devices in a mesh: dp: 4 (over x, core), tensor: 8 (over z, y).
Axes of the slice: x: 2, y: 2, z: 4, core: 2. Of those that a mesh axis runs over, the one named last changes fastest.
Arguments:
- hidden: bfloat16 [768, 14336], P('dp', 'tensor'), parts along dimension 0, may hold values from -6 to 6
- down_weight: bfloat16 [14336, 8192], P('tensor'), may hold values from -0.046875 to 0.046875
- residual: bfloat16 [768, 8192], P('dp', 'tensor'), parts along dimension 0, may hold values from -100 to 100
- norm_gain: float32 [8192], replicated, may hold values from 0.1 to 1.9
- qkv_weight: bfloat16 [8192, 5120], P(None, 'tensor'), may hold values from -0.0625 to 0.0625
Outputs:
- stream: bfloat16 [768, 8192], P('dp', 'tensor'), parts along dimension 0
- qkv: bfloat16 [768, 5120], P('dp', 'tensor'), parts along dimension 0
There are 4 independent parts, one for each index of `dp`. A program takes and returns all parts, laid end to end along the dimension named above; an argument that names none is the same for every part. Nothing has to cross between parts.
All inputs are finite; a program needn't handle non-finite values.
Results may differ from a plain program's by a relative error of at most 0.02.
Values may be sent and summed in bfloat16 or wider, within the bound.
No kernel may reach another device: no remote copies, remote signals or barrier semaphores. Data moves between devices by JAX's collectives and lax.ppermute only.
A program may use at most 128 MiB of HBM per device.

v0:
```python
import jax
import jax.numpy as jnp
from jax import lax
from jax.sharding import PartitionSpec as P

epsilon = 1e-05


def shards(hidden, down_weight, residual, norm_gain, qkv_weight):
    partial_sum = lax.psum_scatter(
        jnp.dot(hidden, down_weight, preferred_element_type=jnp.float32).astype(jnp.bfloat16),
        "tensor",
        scatter_dimension=0,
        tiled=True,
    ).astype(jnp.float32)
    res_rows = lax.all_to_all(residual, "tensor", split_axis=0, concat_axis=1, tiled=True)
    summed = partial_sum + res_rows.astype(jnp.float32)
    scale = jnp.sqrt(jnp.mean(summed * summed, axis=1, keepdims=True) + epsilon)
    normed = (summed / scale * norm_gain[None, :]).astype(jnp.bfloat16)
    stream = lax.all_to_all(
        summed.astype(jnp.bfloat16), "tensor", split_axis=1, concat_axis=0, tiled=True
    )
    qkv = jnp.dot(
        lax.all_gather(normed, "tensor", axis=0, tiled=True),
        qkv_weight,
        preferred_element_type=jnp.float32,
    ).astype(jnp.bfloat16)
    return (stream, qkv)


def solution(mesh):
    in_specs = (P("dp", "tensor"), P("tensor", None), P("dp", "tensor"), P(), P(None, "tensor"))
    out_specs = (P("dp", "tensor"), P("dp", "tensor"))
    return jax.shard_map(shards, mesh=mesh, in_specs=in_specs, out_specs=out_specs, check_vma=False)
```

profile of v0, /device:TPU:0, one launch (start us, length us, event | category | flops | bytes accessed | tf_op | source)
XLA Modules:
  0.0 188.3 jit_solution(2668836416267155932)
XLA Ops:
  7.2 0.0 copy-start
  7.2 0.0 copy-start.1
  7.2 0.0 copy-start.2
  7.2 0.0 reduce-scatter.2.cloned.1.call-start
  7.2 1.0 copy-done
  8.3 13.9 %convolution_convert_fusion = bf16[192,8192]{1,0:T(8,128)(2,1)} fusion(bf16[192,1792]{1,0:T(8,128)(2,1)S(1)} %copy-done, bf16[1792,8192]{1,0:T(8,128)(2,1)} %param.6), kind=kOutput, calls=%fused_computation | convolution fusion | flops 5638717440 | bytes 33193984 | tf_op jit(solution)/shard_map/dot_general | solution.py:11
  22.2 0.0 reduce-scatter.2.cloned.1.call-update
  22.2 0.0 all-gather.2.cloned.1.call-start
  22.3 0.0 copy-done.1
  22.3 28.0 %all_to_all.32 = bf16[8,24,1024]{2,1,0:T(8,128)(2,1)S(1)} all-to-all(bf16[8,24,1024]{2,1,0:T(8,128)(2,1)S(1)} %bitcast.21), channel_id=1, replica_groups=mesh['dp'=4,'tensor'=8] {'tensor'}, dimensions={0} | all-to-all | bytes 786432 | tf_op jit(solution)/shard_map/all_to_all | solution.py:16
  50.3 0.1 convert_bitcast_fusion
  50.4 0.1 copy.12
  50.5 55.4 %reduce-scatter.2.cloned.1.call-done = bf16[24,8192]{1,0:T(8,128)(2,1)} async-done(((bf16[192,8192]{1,0:T(8,128)(2,1)}), bf16[24,8192]{1,0:T(8,128)(2,1)}) %reduce-scatter.2.cloned.1.call-update) | async-done | bytes 393232 | tf_op jit(solution)/shard_map/reduce_scatter | solution.py:10
  105.9 1.2 multiply_reduce_fusion
  107.1 0.0 copy-done.2
  107.1 1.9 %multiply_convert_fusion = (bf16[24,8192]{1,0:T(8,128)(2,1)}, bf16[24,8192]{1,0:T(8,128)(2,1)S(1)}) fusion(f32[8192]{0:T(1024)S(1)} %copy-done.2, f32[24]{0:T(128)S(1)} %add_sqrt_fusion, f32[24,8192]{1,0:T(8,128)S(1)} %bitcast.17, bf16[24,8192]{1,0:T(8,128)(2,1)} %reduce-scatter.2.cloned.1.call-done), kind=kLoop, calls=%fused_computation.3 | loop fusion | flops 1179648 | bytes 1998944 | tf_op jit(solution)/shard_map/convert_element_type | solution.py:19
  109.0 0.0 all-gather.2.cloned.1.call-update
  109.0 22.0 %all_to_all.33 = bf16[24,8,1024]{2,0,1:T(8,128)(2,1)S(1)} all-to-all(bf16[24,8,1024]{2,0,1:T(8,128)(2,1)S(1)} %bitcast.19), channel_id=1, replica_groups=mesh['dp'=4,'tensor'=8] {'tensor'}, dimensions={1} | all-to-all | bytes 786432 | tf_op jit(solution)/shard_map/all_to_all | solution.py:20
  131.0 41.4 %all-gather.2.cloned.1.call-done = bf16[192,8192]{1,0:T(8,128)(2,1)} async-done(((bf16[24,8192]{1,0:T(8,128)(2,1)}), bf16[192,8192]{1,0:T(8,128)(2,1)}) %all-gather.2.cloned.1.call-update) | async-done | bytes 3145744 | tf_op jit(solution)/shard_map/all_gather | solution.py:24
  172.5 8.2 %convolution_convert_fusion.1 = bf16[192,640]{1,0:T(8,128)(2,1)} fusion(bf16[192,8192]{1,0:T(8,128)(2,1)} %all-gather.2.cloned.1.call-done, bf16[8192,640]{1,0:T(8,128)(2,1)} %param.9), kind=kOutput, calls=%fused_computation.1 | convolution fusion | flops 2013388800 | bytes 13877248 | tf_op jit(solution)/shard_map/dot_general | solution.py:23
  180.7 0.7 copy.16
  (2 shorter events, 0.0 us)
Async XLA Ops:
  7.2 1.1 copy-start
  7.2 15.1 %copy-start.1 = (bf16[192,1024]{1,0:T(8,128)(2,1)S(1)}, bf16[192,1024]{1,0:T(8,128)(2,1)}, u32[]{:S(2)}) copy-start(bf16[192,1024]{1,0:T(8,128)(2,1)} %param.7) | copy-start | bytes 1179652
  7.2 99.9 %copy-start.2 = (f32[8192]{0:T(1024)S(1)}, f32[8192]{0:T(1024)}, u32[]{:S(2)}) copy-start(f32[8192]{0:T(1024)} %param.8) | copy-start | bytes 98308
  7.2 98.7 %reduce-scatter.2.cloned.1.call-start = ((), (), s32[]{:S(2)}) async-start(), calls=%async_computation.3 | async-start | bytes 3538944 | tf_op jit(solution)/shard_map/reduce_scatter | solution.py:10
  22.2 150.2 %all-gather.2.cloned.1.call-start = ((), (), s32[]{:S(2)}) async-start(), calls=%async_computation.4 | async-start | bytes 3538944 | tf_op jit(solution)/shard_map/all_gather | solution.py:24
Sparse Core Ops, SparseCore 0:
  22.4 83.4 reduce-scatter.1
  109.1 63.2 all-gather.1
where the time goes:
time: 189 us; the launch traced here: 188 us
  waiting for transfers between devices  96.8 us (51%)
  blocking collectives  50 us (26%)
  matrix products  22.2 us (12%)
  between operations  14.1 us (7%)
  other arithmetic  3.18 us (2%)
    reduce_scatter x1, waiting for transfers between devices, shards(): lax.psum_scatter(jnp.dot(hidden, down_weight, preferred_element_type=jnp....  55.4 us
    all_gather x1, waiting for transfers between devices, shards(): lax.all_gather(normed, 'tensor', axis=0, tiled=True)  41.4 us
    all_to_all x1, blocking collectives, shards(): lax.all_to_all(residual, 'tensor', split_axis=0, concat_axis=1, tiled=True)  28 us
    all_to_all x1, blocking collectives, shards(): lax.all_to_all(summed.astype(jnp.bfloat16), 'tensor', split_axis=1, conca...  22 us
    dot_general x1, matrix products, shards(): jnp.dot(hidden, down_weight, preferred_element_type=jnp.float32)  13.9 us
    dot_general x1, matrix products, shards(): jnp.dot(lax.all_gather(normed, 'tensor', axis=0, tiled=True), qkv_weight,...  8.25 us
  transfers between devices with their start and end apart: 2, of which 2 were waited for; matrix products, arithmetic and copies ran while one was open for 0% of the time, Pallas kernels for 0%

commit v1 on v0

v1 whole, which is shorter than its diff:
```python
import functools

import jax
import jax.numpy as jnp
from jax import lax
from jax.experimental import pallas as pl
from jax.experimental.pallas import tpu as pltpu
from jax.sharding import PartitionSpec as P

epsilon = 1e-05
f32, bf16 = jnp.float32, jnp.bfloat16
MIB = 1024 * 1024


def ring_order(n):
    return list(range(0, n, 2)) + list(range(n - 1, 0, -2))


def owner(n, offset):
    me = lax.axis_index("tensor")
    place = jnp.where(me % 2 == 0, me // 2, n - 1 - me // 2)
    place = (place + (offset + n)) % n
    return jnp.where(place < n // 2, 2 * place, 2 * (n - 1 - place) + 1)


def down_kernel(n, parts, x_ref, w_ref, *rest):
    outs, rest = rest[: len(parts)], list(rest[len(parts) :])
    buf, sems = rest[-2:]
    if len(rest) > 2:
        x_out, x_sem = rest[:2]
        x_copy = pltpu.make_async_copy(x_ref, x_out, x_sem)
        x_copy.start()
    else:
        x_out, x_copy = x_ref, None
    sub = outs[0].shape[1]
    per, (count, pieces) = sub // buf.shape[2], sems.shape
    tile, deep = buf.shape[2], buf.shape[1] // pieces

    def copies(i, begin, j):
        at = i * per + j
        columns = pl.ds(pl.multiple_of(begin + j * tile, tile), tile)
        for p in range(pieces):
            rows = pl.ds(p * deep, deep)
            yield pltpu.make_async_copy(w_ref.at[rows, columns], buf.at[at, rows], sems.at[at, p])

    begins = [owner(n, offset) * (2 * sub) + half * sub for offset, half in parts]
    for i in range(len(parts)):
        for j in range(per):
            for copy in copies(i, begins[i], j):
                copy.start()
    if x_copy is not None:
        x_copy.wait()
    for i, out in enumerate(outs):

        def step(j, carry):
            for copy in copies(i, begins[i], j):
                copy.wait()
            part = jnp.dot(x_out[...], buf[i * per + j], preferred_element_type=f32)
            out[:, pl.ds(pl.multiple_of(j * tile, tile), tile)] = part.astype(bf16)
            return carry

        lax.fori_loop(0, per, step, 0)


def down(n, parts, hidden, down_weight, sub, first=False):
    rows, inner = hidden.shape
    vmem, hbm = pl.BlockSpec(memory_space=pltpu.VMEM), pl.BlockSpec(memory_space=pltpu.HBM)
    pieces = max(p for p in (1, 2, 4) if inner % (16 * p) == 0)
    tile = sub
    count = len(parts) * (sub // tile)
    weight = pltpu.with_memory_space_constraint(down_weight, pltpu.HBM)
    out_shape = [pltpu.VMEM((rows, sub), bf16)] * len(parts)
    scratch = [pltpu.VMEM((count, inner, tile), bf16), pltpu.SemaphoreType.DMA((count, pieces))]
    if first:
        hidden = pltpu.with_memory_space_constraint(hidden, pltpu.HBM)
        out_shape = out_shape + [pltpu.VMEM(hidden.shape, bf16)]
        scratch = [pltpu.SemaphoreType.DMA] + scratch
    return pl.pallas_call(
        functools.partial(down_kernel, n, parts),
        out_shape=out_shape,
        in_specs=[hbm if first else vmem, hbm],
        out_specs=[vmem] * len(out_shape),
        scratch_shapes=scratch,
        compiler_params=pltpu.CompilerParams(vmem_limit_bytes=14 * MIB),
        cost_estimate=pl.CostEstimate(
            flops=2 * rows * inner * sub * len(parts),
            bytes_accessed=2 * inner * sub * len(parts),
            transcendentals=0,
        ),
    )(hidden, weight)


def add_kernel(own_ref, x_ref, hidden_ref, out, hidden_out):
    out[...] = (own_ref[...].astype(f32) + x_ref[...].astype(f32)).astype(bf16)


def add_step(own, x, hidden):
    vmem = pl.BlockSpec(memory_space=pltpu.VMEM)
    return pl.pallas_call(
        add_kernel,
        out_shape=[pltpu.VMEM(x.shape, bf16), pltpu.VMEM(hidden.shape, bf16)],
        in_specs=[vmem] * 3,
        out_specs=[vmem] * 2,
        input_output_aliases={2: 1},
        compiler_params=pltpu.CompilerParams(vmem_limit_bytes=12 * MIB),
        cost_estimate=pl.CostEstimate(flops=x.size, bytes_accessed=6 * x.size, transcendentals=0),
    )(own, x, hidden)


def finish_kernel(half, own_ref, residual_ref, x_ref, y_ref, out):
    sub = out.shape[1]
    total = own_ref[...].astype(f32) + residual_ref[:, half * sub : (half + 1) * sub].astype(f32)
    out[...] = (total + x_ref[...].astype(f32) + y_ref[...].astype(f32)).astype(bf16)


def finish(half, own, residual, x, y):
    vmem = pl.BlockSpec(memory_space=pltpu.VMEM)
    return pl.pallas_call(
        functools.partial(finish_kernel, half),
        out_shape=[pltpu.VMEM(own.shape, bf16)],
        in_specs=[vmem] * 4,
        out_specs=[vmem],
        compiler_params=pltpu.CompilerParams(vmem_limit_bytes=12 * MIB),
        cost_estimate=pl.CostEstimate(flops=4 * own.size, bytes_accessed=10 * own.size, transcendentals=0),
    )(own, residual, x, y)[0]


def qkv_kernel(n, parts, first, last, joins, total_features, *refs):
    count = len(parts)
    xs, (gain_ref, w_ref), rest = refs[:count], refs[count : count + 2], refs[count + 2 :]
    sub = xs[0].shape[-1]
    if not first:
        total_in, squares_in, rest = rest[0], rest[1], rest[2:]
    if joins:
        for i, x_ref in enumerate(xs[-2:]):
            rest[2][:, i * sub : (i + 1) * sub] = x_ref[...]
    columns = w_ref.shape[1]
    scaled, rows_at = [], []
    squares = None if first else squares_in[...]
    for x_ref, (offset, half) in zip(xs, parts):
        row = pl.multiple_of(owner(n, offset) * (2 * sub) + half * sub, sub)
        x = x_ref[...].astype(f32)
        scaled.append((x * gain_ref[:, pl.ds(row, sub)]).astype(bf16))
        rows_at.append(row)
        for c in range(0, sub, 128):
            piece = x[:, c : c + 128]
            squares = piece * piece if squares is None else squares + piece * piece
    if last:
        mean = jnp.sum(squares, axis=1, keepdims=True) / total_features
        scale = jnp.sqrt(mean + epsilon)
        inverse = 1.0 / scale
    else:
        rest[1][...] = squares
    for c in range(0, columns, 256):
        wide = min(256, columns - c)
        acc = None if first else total_in[:, c : c + wide]
        for x, row in zip(scaled, rows_at):
            more = jnp.dot(x, w_ref[pl.ds(row, sub), c : c + wide], preferred_element_type=f32)
            acc = more if acc is None else acc + more
        if last:
            rest[0][:, c : c + wide] = (acc * inverse).astype(bf16)
        else:
            rest[0][:, c : c + wide] = acc


def qkv_step(n, parts, xs, gain, weight, state, last=False, hand_on=False, joins=False):
    rows, sub = xs[0].shape
    columns = weight.shape[1]
    vmem = pl.BlockSpec(memory_space=pltpu.VMEM)
    if last:
        out_shape = [jax.ShapeDtypeStruct((rows, columns), bf16)]
    else:
        out_shape = [pltpu.VMEM((rows, columns), f32), pltpu.VMEM((rows, 128), f32)]
    aliases = {}
    if joins:
        out_shape.append(jax.ShapeDtypeStruct((rows, 2 * sub), bf16))
    if hand_on:
        aliases = {len(xs) - 1: len(out_shape)}
        out_shape.append(pltpu.VMEM((rows, sub), bf16))
    operands = (*xs, gain, weight, *state)
    return pl.pallas_call(
        functools.partial(qkv_kernel, n, parts, not state, last, joins, float(weight.shape[0])),
        out_shape=out_shape,
        in_specs=[vmem] * len(operands),
        out_specs=[vmem] * len(out_shape),
        input_output_aliases=aliases,
        compiler_params=pltpu.CompilerParams(vmem_limit_bytes=16 * MIB),
        cost_estimate=pl.CostEstimate(
            flops=2 * rows * sub * columns * len(parts),
            bytes_accessed=2 * sub * columns * len(parts),
            transcendentals=0,
        ),
    )(*operands)


def make_shards(n):
    order = ring_order(n)
    right = [(order[p], order[(p + 1) % n]) for p in range(n)]
    left = [(order[p], order[(p - 1) % n]) for p in range(n)]
    half = n // 2
    plan = [((half, 0), (half, 1))]
    for k in range(half - 1, 0, -1):
        plan += [((k, 1), (-k, 0)), ((k, 0), (-k, 1))]

    def shards(hidden, down_weight, residual, norm_gain, qkv_weight):
        rows, width = residual.shape
        sub = width // 2

        def send(x, pairs):
            return lax.ppermute(x, "tensor", pairs)

        *own, hidden = down(n, plan[0], hidden, down_weight, sub, first=True)
        arrived = [(send(own[0], right), send(own[1], left))]
        for step in range(1, n - 1, 2):
            own = down(n, [*plan[step], *plan[step + 1]], hidden, down_weight, sub)
            for i in range(2):
                up, down_ = own[2 * i : 2 * i + 2]
                if step + i > 1:
                    from_left, from_right = arrived[-2]
                    down_, hidden = add_step(down_, from_right, hidden)
                    up, hidden = add_step(up, from_left, hidden)
                arrived.append((send(up, right), send(down_, left)))
        own = down(n, [(0, 0), (0, 1)], hidden, down_weight, sub)
        (left_b, right_a), (left_a, right_b) = arrived[-2:]
        halves = [finish(0, own[0], residual, left_a, right_a), finish(1, own[1], residual, left_b, right_b)]

        gain = norm_gain[None, :]
        arrived = [(send(halves[0], right), send(halves[1], left))]
        arrived.append((send(halves[1], right), send(halves[0], left)))
        state, parts, xs = (), [], []
        for step in range(n - 1):
            x, y = arrived[step]
            k = step // 2 + 1
            parts += [(k, 1 - step % 2), (-k, step % 2)]
            xs += [y, x]
            if step in (n - 4, n - 5):
                arrived.append((send(x, right), send(y, left)))
            elif step == n - 3:
                state = qkv_step(n, parts, xs, gain, qkv_weight, state)
                *state, stream = qkv_step(n, [(0, 0), (0, 1)], halves, gain, qkv_weight, state, joins=True)
                parts, xs = [], []
            elif step == n - 2:
                state = qkv_step(n, parts[:1], xs[:1], gain, qkv_weight, state)
                (qkv,) = qkv_step(n, parts[1:], xs[1:], gain, qkv_weight, state, last=True)
            else:
                *state, x = qkv_step(n, parts, xs, gain, qkv_weight, state, hand_on=True)
                arrived.append((send(x, right), send(y, left)))
                parts, xs = [], []
        return stream, qkv

    return shards


def solution(mesh):
    in_specs = (P("dp", "tensor"), P("tensor", None), P("dp", "tensor"), P(), P(None, "tensor"))
    out_specs = (P("dp", "tensor"), P("dp", "tensor"))
    return jax.shard_map(
        make_shards(mesh.shape["tensor"]),
        mesh=mesh,
        in_specs=in_specs,
        out_specs=out_specs,
        check_vma=False,
    )
```

time: 189 us -> 71.2 us (0.38)
  waiting for transfers between devices: 96.8 us -> 16.9 us
  blocking collectives: 50 us -> 0 us
  starting transfers between devices: 0.08 us -> 30.3 us
  Pallas kernels: 0 us -> 23 us
  matrix products: 22.2 us -> 0 us
  between operations: 14.1 us -> 0.82 us
  other arithmetic: 3.18 us -> 0.01 us
    reduce_scatter x1 -> x0, waiting for transfers between devices: 55.4 us -> none  [shards(): lax.psum_scatter(jnp.dot(hidden, down_weight, preferred_element_type=jnp....]
    all_to_all x2 -> x0, blocking collectives: 50 us -> none  [the longest x1 28 us: shards(): lax.all_to_all(residual, 'tensor', split_axis=0, concat_axis=1, tiled=True)]
    all_gather x1 -> x0, waiting for transfers between devices: 41.4 us -> none  [shards(): lax.all_gather(normed, 'tensor', axis=0, tiled=True)]
    ppermute x0 -> x28, starting transfers between devices: none -> 30.3 us  [send(): return lax.ppermute(x, 'tensor', pairs)]
    pallas_call x0 -> x24, Pallas kernels: none -> 23 us  [the longest x5 17.1 us: down(): pl.pallas_call(functools.partial(down_kernel, n, parts), out_shape=out_sh...]
    dot_general x2 -> x0, matrix products: 22.2 us -> none  [the longest x1 13.9 us: shards(): jnp.dot(hidden, down_weight, preferred_element_type=jnp.float32)]
    ppermute x0 -> x28, waiting for transfers between devices: none -> 16.9 us  [send(): return lax.ppermute(x, 'tensor', pairs)]
  transfers between devices with their start and end apart: 2 -> 28, of which waited for: 2 -> 11; matrix products, arithmetic and copies ran while one was open for 0% -> 0% of each run, Pallas kernels for 0% -> 27%
where the time goes in v1:
time: 71.2 us; the launch traced here: 71.1 us
  starting transfers between devices  30.3 us (43%)
  Pallas kernels  23 us (32%)
  waiting for transfers between devices  16.9 us (24%)
  between operations  0.82 us (1%)
    ppermute x28, starting transfers between devices, send(): return lax.ppermute(x, 'tensor', pairs)  30.3 us
    pallas_call x5, Pallas kernels, down(): pl.pallas_call(functools.partial(down_kernel, n, parts), out_shape=out_sh...  17.1 us
    ppermute x28, waiting for transfers between devices, send(): return lax.ppermute(x, 'tensor', pairs)  16.9 us
    pallas_call x7, Pallas kernels, qkv_step(): pl.pallas_call(functools.partial(qkv_kernel, n, parts, not state, last, j...  5.17 us
  transfers between devices with their start and end apart: 28, of which 11 were waited for; matrix products, arithmetic and copies ran while one was open for 0% of the time, Pallas kernels for 27%

profile of v1, /device:TPU:0, one launch (start us, length us, event | category | flops | bytes accessed | tf_op | source)
XLA Modules:
  0.0 71.1 jit_solution(3910596820291207028)
XLA Ops:
  0.6 2.8 %shard_map.68 = (bf16[192,512]{1,0:T(8,128)(2,1)S(1)}, bf16[192,512]{1,0:T(8,128)(2,1)S(1)}, bf16[192,1792]{1,0:T(8,128)(2,1)S(1)}) custom-call(bf16[192,1792]{1,0:T(8,128)(2,1)} %x_ref.1, bf16[1792,8192]{1,0:T(8,128)(2,1)} %w_ref.9), custom_call_target="tpu_custom_call" | custom-call | flops 704643072 | bytes 3670016 | tf_op jit(solution)/shard_map/pallas_call | solution.py:78
  3.5 3.0 %collective-permute-start.1 = (bf16[192,512]{1,0:T(8,128)(2,1)S(1)}, bf16[192,512]{1,0:T(8,128)(2,1)S(1)}, u32[]{:S(2)}, u32[]{:S(2)}) collective-permute-start(bf16[192,512]{1,0:T(8,128)(2,1)S(1)} %get-tuple-element.59), channel_id=1, source_target_pairs={{0,1},{2,0},{4,2},{6,4},{7,6},{5,7},{3,5},{1,3},{8,9},{10,8},{12,1... | collective-permute-start | bytes 589832 | tf_op jit(solution)/shard_map/ppermute | solution.py:210
  6.6 3.8 %shard_map.69 = (bf16[192,512]{1,0:T(8,128)(2,1)S(1)}, bf16[192,512]{1,0:T(8,128)(2,1)S(1)}, bf16[192,512]{1,0:T(8,128)(2,1)S(1)}, bf16[192,512]{1,0:T(8,128)(2,1)S(1)}) custom-call(bf16[192,1792]{1,0:T(8,128)(2,1)S(1)} %get-tuple-element.55.x_ref.hidden_ref, bf16[1792,8192]{1,0:T(8,128)(2,1)} %w_ref.9), custom_call_target="tpu_custom_call" | custom-call | flops 1409286144 | bytes 7340032 | tf_op jit(solution)/shard_map/pallas_call | solution.py:78
  10.4 2.0 %collective-permute-start.5 = (bf16[192,512]{1,0:T(8,128)(2,1)S(1)}, bf16[192,512]{1,0:T(8,128)(2,1)S(1)}, u32[]{:S(2)}, u32[]{:S(2)}) collective-permute-start(bf16[192,512]{1,0:T(8,128)(2,1)S(1)} %get-tuple-element.69), channel_id=1, source_target_pairs={{0,1},{2,0},{4,2},{6,4},{7,6},{5,7},{3,5},{1,3},{8,9},{10,8},{12,1... | collective-permute-start | bytes 589832 | tf_op jit(solution)/shard_map/ppermute | solution.py:210
  12.5 2.0 %collective-permute-start.3 = (bf16[192,512]{1,0:T(8,128)(2,1)S(1)}, bf16[192,512]{1,0:T(8,128)(2,1)S(1)}, u32[]{:S(2)}, u32[]{:S(2)}) collective-permute-start(bf16[192,512]{1,0:T(8,128)(2,1)S(1)} %get-tuple-element.65), channel_id=1, source_target_pairs={{0,1},{2,0},{4,2},{6,4},{7,6},{5,7},{3,5},{1,3},{8,9},{10,8},{12,1... | collective-permute-start | bytes 589832 | tf_op jit(solution)/shard_map/ppermute | solution.py:210
  14.6 0.2 collective-permute-start.2
  14.7 3.8 %shard_map.72 = (bf16[192,512]{1,0:T(8,128)(2,1)S(1)}, bf16[192,512]{1,0:T(8,128)(2,1)S(1)}, bf16[192,512]{1,0:T(8,128)(2,1)S(1)}, bf16[192,512]{1,0:T(8,128)(2,1)S(1)}) custom-call(bf16[192,1792]{1,0:T(8,128)(2,1)S(1)} %get-tuple-element.61.x_ref.hidden_ref, bf16[1792,8192]{1,0:T(8,128)(2,1)} %w_ref.9), custom_call_target="tpu_custom_call" | custom-call | flops 1409286144 | bytes 7340032 | tf_op jit(solution)/shard_map/pallas_call | solution.py:78
  18.6 2.0 %collective-permute-start.9 = (bf16[192,512]{1,0:T(8,128)(2,1)S(1)}, bf16[192,512]{1,0:T(8,128)(2,1)S(1)}, u32[]{:S(2)}, u32[]{:S(2)}) collective-permute-start(bf16[192,512]{1,0:T(8,128)(2,1)S(1)} %get-tuple-element.81), channel_id=1, source_target_pairs={{0,1},{2,0},{4,2},{6,4},{7,6},{5,7},{3,5},{1,3},{8,9},{10,8},{12,1... | collective-permute-start | bytes 589832 | tf_op jit(solution)/shard_map/ppermute | solution.py:210
  20.8 1.5 %collective-permute-done.3.x_ref = bf16[192,512]{1,0:T(8,128)(2,1)S(1)} collective-permute-done((bf16[192,512]{1,0:T(8,128)(2,1)S(1)}, bf16[192,512]{1,0:T(8,128)(2,1)S(1)}, u32[]{:S(2)}, u32[]{:S(2)}) %collective-permute-start.3) | collective-permute-done | bytes 196640 | tf_op jit(solution)/shard_map/ppermute | solution.py:210
  22.4 1.7 %collective-permute-start.7 = (bf16[192,512]{1,0:T(8,128)(2,1)S(1)}, bf16[192,512]{1,0:T(8,128)(2,1)S(1)}, u32[]{:S(2)}, u32[]{:S(2)}) collective-permute-start(bf16[192,512]{1,0:T(8,128)(2,1)S(1)} %get-tuple-element.77), channel_id=1, source_target_pairs={{0,1},{2,0},{4,2},{6,4},{7,6},{5,7},{3,5},{1,3},{8,9},{10,8},{12,1... | collective-permute-start | bytes 589832 | tf_op jit(solution)/shard_map/ppermute | solution.py:210
  24.1 0.5 collective-permute-start.6
  24.6 4.0 %shard_map.77 = (bf16[192,512]{1,0:T(8,128)(2,1)S(1)}, bf16[192,512]{1,0:T(8,128)(2,1)S(1)}, bf16[192,512]{1,0:T(8,128)(2,1)S(1)}, bf16[192,512]{1,0:T(8,128)(2,1)S(1)}) custom-call(bf16[192,1792]{1,0:T(8,128)(2,1)S(1)} %get-tuple-element.73.x_ref.hidden_ref, bf16[1792,8192]{1,0:T(8,128)(2,1)} %w_ref.9), custom_call_target="tpu_custom_call" | custom-call | flops 1409286144 | bytes 7340032 | tf_op jit(solution)/shard_map/pallas_call | solution.py:78
  28.6 1.7 %collective-permute-start.11 = (bf16[192,512]{1,0:T(8,128)(2,1)S(1)}, bf16[192,512]{1,0:T(8,128)(2,1)S(1)}, u32[]{:S(2)}, u32[]{:S(2)}) collective-permute-start(bf16[192,512]{1,0:T(8,128)(2,1)S(1)} %get-tuple-element.88), channel_id=1, source_target_pairs={{0,1},{2,0},{4,2},{6,4},{7,6},{5,7},{3,5},{1,3},{8,9},{10,8},{12,1... | collective-permute-start | bytes 589832 | tf_op jit(solution)/shard_map/ppermute | solution.py:210
  30.3 0.5 collective-permute-start.12
  30.9 1.9 %collective-permute-start.13 = (bf16[192,512]{1,0:T(8,128)(2,1)S(1)}, bf16[192,512]{1,0:T(8,128)(2,1)S(1)}, u32[]{:S(2)}, u32[]{:S(2)}) collective-permute-start(bf16[192,512]{1,0:T(8,128)(2,1)S(1)} %get-tuple-element.91), channel_id=1, source_target_pairs={{0,1},{2,0},{4,2},{6,4},{7,6},{5,7},{3,5},{1,3},{8,9},{10,8},{12,1... | collective-permute-start | bytes 589832 | tf_op jit(solution)/shard_map/ppermute | solution.py:210
  32.8 0.3 collective-permute-start.10
  33.0 2.8 %shard_map.82 = (bf16[192,512]{1,0:T(8,128)(2,1)S(1)}, bf16[192,512]{1,0:T(8,128)(2,1)S(1)}) custom-call(bf16[192,1792]{1,0:T(8,128)(2,1)S(1)} %get-tuple-element.85.x_ref, bf16[1792,8192]{1,0:T(8,128)(2,1)} %w_ref.9), custom_call_target="tpu_custom_call" | custom-call | flops 704643072 | bytes 3670016 | tf_op jit(solution)/shard_map/pallas_call | solution.py:78
  35.8 1.3 %collective-permute-done.12.x_ref = bf16[192,512]{1,0:T(8,128)(2,1)S(1)} collective-permute-done((bf16[192,512]{1,0:T(8,128)(2,1)S(1)}, bf16[192,512]{1,0:T(8,128)(2,1)S(1)}, u32[]{:S(2)}, u32[]{:S(2)}) %collective-permute-start.12) | collective-permute-done | bytes 196640 | tf_op jit(solution)/shard_map/ppermute | solution.py:210
  37.1 0.8 %collective-permute-done.13.y_ref = bf16[192,512]{1,0:T(8,128)(2,1)S(1)} collective-permute-done((bf16[192,512]{1,0:T(8,128)(2,1)S(1)}, bf16[192,512]{1,0:T(8,128)(2,1)S(1)}, u32[]{:S(2)}, u32[]{:S(2)}) %collective-permute-start.13) | collective-permute-done | bytes 196640 | tf_op jit(solution)/shard_map/ppermute | solution.py:210
  38.0 1.7 %collective-permute-start.17 = (bf16[192,512]{1,0:T(8,128)(2,1)S(1)}, bf16[192,512]{1,0:T(8,128)(2,1)S(1)}, u32[]{:S(2)}, u32[]{:S(2)}) collective-permute-start(bf16[192,512]{1,0:T(8,128)(2,1)S(1)} %shard_map.84.refs_1_), channel_id=1, source_target_pairs={{0,1},{2,0},{4,2},{6,4},{7,6},{5,7},{3,5},{1,3},{8,9},{10,8},{12,1... | collective-permute-start | bytes 589832 | tf_op jit(solution)/shard_map/ppermute | solution.py:210
  39.8 0.5 collective-permute-start.18
  40.2 1.6 %collective-permute-start.14 = (bf16[192,512]{1,0:T(8,128)(2,1)S(1)}, bf16[192,512]{1,0:T(8,128)(2,1)S(1)}, u32[]{:S(2)}, u32[]{:S(2)}) collective-permute-start(bf16[192,512]{1,0:T(8,128)(2,1)S(1)} %shard_map.83.refs_0_), channel_id=1, source_target_pairs={{0,1},{2,0},{4,2},{6,4},{7,6},{5,7},{3,5},{1,3},{8,9},{10,8},{12,1... | collective-permute-start | bytes 589832 | tf_op jit(solution)/shard_map/ppermute | solution.py:210
  41.9 0.4 collective-permute-start.16
  42.3 3.6 %collective-permute-done.17.refs_0_ = bf16[192,512]{1,0:T(8,128)(2,1)S(1)} collective-permute-done((bf16[192,512]{1,0:T(8,128)(2,1)S(1)}, bf16[192,512]{1,0:T(8,128)(2,1)S(1)}, u32[]{:S(2)}, u32[]{:S(2)}) %collective-permute-start.17) | collective-permute-done | bytes 196640 | tf_op jit(solution)/shard_map/ppermute | solution.py:210
  45.9 1.6 %collective-permute-start.20 = (bf16[192,512]{1,0:T(8,128)(2,1)S(1)}, bf16[192,512]{1,0:T(8,128)(2,1)S(1)}, u32[]{:S(2)}, u32[]{:S(2)}) collective-permute-start(bf16[192,512]{1,0:T(8,128)(2,1)S(1)} %collective-permute-done.17.refs_0_), channel_id=1, source_target_pairs={{0,1},{2,0},{4,2},{6,4},{7,6},{5,7},{3,5},{1,3},{8,9},{10,8},{12,1... | collective-permute-start | bytes 589832 | tf_op jit(solution)/shard_map/ppermute | solution.py:210
  47.5 0.5 shard_map.85
  48.1 0.5 collective-permute-start.22
  48.5 1.6 %collective-permute-done.14.refs_0_ = bf16[192,512]{1,0:T(8,128)(2,1)S(1)} collective-permute-done((bf16[192,512]{1,0:T(8,128)(2,1)S(1)}, bf16[192,512]{1,0:T(8,128)(2,1)S(1)}, u32[]{:S(2)}, u32[]{:S(2)}) %collective-permute-start.14) | collective-permute-done | bytes 196640 | tf_op jit(solution)/shard_map/ppermute | solution.py:210
  50.1 1.6 %collective-permute-start.15 = (bf16[192,512]{1,0:T(8,128)(2,1)S(1)}, bf16[192,512]{1,0:T(8,128)(2,1)S(1)}, u32[]{:S(2)}, u32[]{:S(2)}) collective-permute-start(bf16[192,512]{1,0:T(8,128)(2,1)S(1)} %collective-permute-done.14.refs_0_), channel_id=1, source_target_pairs={{0,1},{2,0},{4,2},{6,4},{7,6},{5,7},{3,5},{1,3},{8,9},{10,8},{12,1... | collective-permute-start | bytes 589832 | tf_op jit(solution)/shard_map/ppermute | solution.py:210
  51.7 0.5 shard_map.86
  52.2 0.4 collective-permute-start.19
  52.7 1.6 %collective-permute-done.20.refs_0_ = bf16[192,512]{1,0:T(8,128)(2,1)S(1)} collective-permute-done((bf16[192,512]{1,0:T(8,128)(2,1)S(1)}, bf16[192,512]{1,0:T(8,128)(2,1)S(1)}, u32[]{:S(2)}, u32[]{:S(2)}) %collective-permute-start.20) | collective-permute-done | bytes 196640 | tf_op jit(solution)/shard_map/ppermute | solution.py:210
  54.3 1.6 %collective-permute-start.21 = (bf16[192,512]{1,0:T(8,128)(2,1)S(1)}, bf16[192,512]{1,0:T(8,128)(2,1)S(1)}, u32[]{:S(2)}, u32[]{:S(2)}) collective-permute-start(bf16[192,512]{1,0:T(8,128)(2,1)S(1)} %collective-permute-done.20.refs_0_), channel_id=1, source_target_pairs={{0,1},{2,0},{4,2},{6,4},{7,6},{5,7},{3,5},{1,3},{8,9},{10,8},{12,1... | collective-permute-start | bytes 589832 | tf_op jit(solution)/shard_map/ppermute | solution.py:210
  56.0 0.5 shard_map.87
  56.5 0.5 collective-permute-start.23
  56.9 1.6 %collective-permute-done.15.refs_0_ = bf16[192,512]{1,0:T(8,128)(2,1)S(1)} collective-permute-done((bf16[192,512]{1,0:T(8,128)(2,1)S(1)}, bf16[192,512]{1,0:T(8,128)(2,1)S(1)}, u32[]{:S(2)}, u32[]{:S(2)}) %collective-permute-start.15) | collective-permute-done | bytes 196640 | tf_op jit(solution)/shard_map/ppermute | solution.py:210
  58.5 1.6 %collective-permute-start.24 = (bf16[192,512]{1,0:T(8,128)(2,1)S(1)}, bf16[192,512]{1,0:T(8,128)(2,1)S(1)}, u32[]{:S(2)}, u32[]{:S(2)}) collective-permute-start(bf16[192,512]{1,0:T(8,128)(2,1)S(1)} %collective-permute-done.15.refs_0_), channel_id=1, source_target_pairs={{0,1},{2,0},{4,2},{6,4},{7,6},{5,7},{3,5},{1,3},{8,9},{10,8},{12,1... | collective-permute-start | bytes 589832 | tf_op jit(solution)/shard_map/ppermute | solution.py:210
  60.2 0.4 collective-permute-start.25
  60.6 2.2 %collective-permute-done.21.refs_2_ = bf16[192,512]{1,0:T(8,128)(2,1)S(1)} collective-permute-done((bf16[192,512]{1,0:T(8,128)(2,1)S(1)}, bf16[192,512]{1,0:T(8,128)(2,1)S(1)}, u32[]{:S(2)}, u32[]{:S(2)}) %collective-permute-start.21) | collective-permute-done | bytes 196640 | tf_op jit(solution)/shard_map/ppermute | solution.py:210
  62.7 1.6 %collective-permute-start.27 = (bf16[192,512]{1,0:T(8,128)(2,1)S(1)}, bf16[192,512]{1,0:T(8,128)(2,1)S(1)}, u32[]{:S(2)}, u32[]{:S(2)}) collective-permute-start(bf16[192,512]{1,0:T(8,128)(2,1)S(1)} %collective-permute-done.21.refs_2_), channel_id=1, source_target_pairs={{0,1},{2,0},{4,2},{6,4},{7,6},{5,7},{3,5},{1,3},{8,9},{10,8},{12,1... | collective-permute-start | bytes 589832 | tf_op jit(solution)/shard_map/ppermute | solution.py:210
  64.4 0.4 collective-permute-start.26
  64.8 0.5 collective-permute-done.24.refs_4_
  65.3 1.5 %collective-permute-done.25.refs_5_ = bf16[192,512]{1,0:T(8,128)(2,1)S(1)} collective-permute-done((bf16[192,512]{1,0:T(8,128)(2,1)S(1)}, bf16[192,512]{1,0:T(8,128)(2,1)S(1)}, u32[]{:S(2)}, u32[]{:S(2)}) %collective-permute-start.25) | collective-permute-done | bytes 196640 | tf_op jit(solution)/shard_map/ppermute | solution.py:210
  66.8 1.1 %shard_map.88 = (f32[192,640]{1,0:T(8,128)S(1)}, f32[192,128]{1,0:T(8,128)S(1)}) custom-call(bf16[192,512]{1,0:T(8,128)(2,1)S(1)} %collective-permute-done.15.refs_0_, bf16[192,512]{1,0:T(8,128)(2,1)S(1)} %collective-permute-done.19.refs_1_, bf16[192,512]{1,0:T(8,128)(2,1)S(1)} %collective-permute-done.21.refs_2_, ...), custom_call_target="tpu_custom_call" | custom-call | flops 754974720 | bytes 3932160 | tf_op jit(solution)/shard_map/pallas_call | solution.py:181
  67.9 1.2 %shard_map.89 = (f32[192,640]{1,0:T(8,128)S(1)}, f32[192,128]{1,0:T(8,128)S(1)}, bf16[192,1024]{1,0:T(8,128)(2,1)}) custom-call(bf16[192,512]{1,0:T(8,128)(2,1)S(1)} %shard_map.83.refs_0_, bf16[192,512]{1,0:T(8,128)(2,1)S(1)} %shard_map.84.refs_1_, f32[1,8192]{1,0:T(1,128)S(1)} %bitcast.7, bf16[8192,640]{1,0:T(8,128)(2,1)S(1)} %bitcast.2, ...), custom_call_target="tpu_custom_call" | custom-call | flops 251658240 | bytes 1310720 | tf_op jit(solution)/shard_map/pallas_call | solution.py:181
  69.1 0.3 shard_map.90
  69.5 0.6 collective-permute-done.26.refs_0_
  70.1 1.0 %shard_map.91 = bf16[192,640]{1,0:T(8,128)(2,1)} custom-call(bf16[192,512]{1,0:T(8,128)(2,1)S(1)} %collective-permute-done.26.refs_0_, f32[1,8192]{1,0:T(1,128)S(1)} %bitcast.9, bf16[8192,640]{1,0:T(8,128)(2,1)S(1)} %bitcast.2, f32[192,640]{1,0:T(8,128)S(1)} %get-tuple-element.106.refs_3_, f32[192,128]{1,0:T(8,128)S(1)} %get-tuple-element.107.refs_4_), custom_call_target="tpu_custom_call" | custom-call | flops 125829120 | bytes 655360 | tf_op jit(solution)/shard_map/pallas_call | solution.py:181
  (43 shorter events, 1.2 us)
Async XLA Ops:
  3.5 9.0 %collective-permute-start.1 = (bf16[192,512]{1,0:T(8,128)(2,1)S(1)}, bf16[192,512]{1,0:T(8,128)(2,1)S(1)}, u32[]{:S(2)}, u32[]{:S(2)}) collective-permute-start(bf16[192,512]{1,0:T(8,128)(2,1)S(1)} %get-tuple-element.59), channel_id=1, source_target_pairs={{0,1},{2,0},{4,2},{6,4},{7,6},{5,7},{3,5},{1,3},{8,9},{10,8},{12,1... | collective-permute-start | bytes 589832 | tf_op jit(solution)/shard_map/ppermute | solution.py:210
  6.5 8.0 %collective-permute-start = (bf16[192,512]{1,0:T(8,128)(2,1)S(1)}, bf16[192,512]{1,0:T(8,128)(2,1)S(1)}, u32[]{:S(2)}, u32[]{:S(2)}) collective-permute-start(bf16[192,512]{1,0:T(8,128)(2,1)S(1)} %get-tuple-element.57), channel_id=1, source_target_pairs={{0,2},{2,4},{4,6},{6,7},{7,5},{5,3},{3,1},{1,0},{8,10},{10,12},{12... | collective-permute-start | bytes 589832 | tf_op jit(solution)/shard_map/ppermute | solution.py:210
  10.4 8.1 %collective-permute-start.5 = (bf16[192,512]{1,0:T(8,128)(2,1)S(1)}, bf16[192,512]{1,0:T(8,128)(2,1)S(1)}, u32[]{:S(2)}, u32[]{:S(2)}) collective-permute-start(bf16[192,512]{1,0:T(8,128)(2,1)S(1)} %get-tuple-element.69), channel_id=1, source_target_pairs={{0,1},{2,0},{4,2},{6,4},{7,6},{5,7},{3,5},{1,3},{8,9},{10,8},{12,1... | collective-permute-start | bytes 589832 | tf_op jit(solution)/shard_map/ppermute | solution.py:210
  12.4 8.2 %collective-permute-start.4 = (bf16[192,512]{1,0:T(8,128)(2,1)S(1)}, bf16[192,512]{1,0:T(8,128)(2,1)S(1)}, u32[]{:S(2)}, u32[]{:S(2)}) collective-permute-start(bf16[192,512]{1,0:T(8,128)(2,1)S(1)} %get-tuple-element.67), channel_id=1, source_target_pairs={{0,2},{2,4},{4,6},{6,7},{7,5},{5,3},{3,1},{1,0},{8,10},{10,12},{12... | collective-permute-start | bytes 589832 | tf_op jit(solution)/shard_map/ppermute | solution.py:210
  12.5 9.8 %collective-permute-start.3 = (bf16[192,512]{1,0:T(8,128)(2,1)S(1)}, bf16[192,512]{1,0:T(8,128)(2,1)S(1)}, u32[]{:S(2)}, u32[]{:S(2)}) collective-permute-start(bf16[192,512]{1,0:T(8,128)(2,1)S(1)} %get-tuple-element.65), channel_id=1, source_target_pairs={{0,1},{2,0},{4,2},{6,4},{7,6},{5,7},{3,5},{1,3},{8,9},{10,8},{12,1... | collective-permute-start | bytes 589832 | tf_op jit(solution)/shard_map/ppermute | solution.py:210
  14.6 9.5 %collective-permute-start.2 = (bf16[192,512]{1,0:T(8,128)(2,1)S(1)}, bf16[192,512]{1,0:T(8,128)(2,1)S(1)}, u32[]{:S(2)}, u32[]{:S(2)}) collective-permute-start(bf16[192,512]{1,0:T(8,128)(2,1)S(1)} %get-tuple-element.63), channel_id=1, source_target_pairs={{0,2},{2,4},{4,6},{6,7},{7,5},{5,3},{3,1},{1,0},{8,10},{10,12},{12... | collective-permute-start | bytes 589832 | tf_op jit(solution)/shard_map/ppermute | solution.py:210
  18.6 10.0 %collective-permute-start.9 = (bf16[192,512]{1,0:T(8,128)(2,1)S(1)}, bf16[192,512]{1,0:T(8,128)(2,1)S(1)}, u32[]{:S(2)}, u32[]{:S(2)}) collective-permute-start(bf16[192,512]{1,0:T(8,128)(2,1)S(1)} %get-tuple-element.81), channel_id=1, source_target_pairs={{0,1},{2,0},{4,2},{6,4},{7,6},{5,7},{3,5},{1,3},{8,9},{10,8},{12,1... | collective-permute-start | bytes 589832 | tf_op jit(solution)/shard_map/ppermute | solution.py:210
  20.6 9.7 %collective-permute-start.8 = (bf16[192,512]{1,0:T(8,128)(2,1)S(1)}, bf16[192,512]{1,0:T(8,128)(2,1)S(1)}, u32[]{:S(2)}, u32[]{:S(2)}) collective-permute-start(bf16[192,512]{1,0:T(8,128)(2,1)S(1)} %get-tuple-element.79), channel_id=1, source_target_pairs={{0,2},{2,4},{4,6},{6,7},{7,5},{5,3},{3,1},{1,0},{8,10},{10,12},{12... | collective-permute-start | bytes 589832 | tf_op jit(solution)/shard_map/ppermute | solution.py:210
  22.4 8.4 %collective-permute-start.7 = (bf16[192,512]{1,0:T(8,128)(2,1)S(1)}, bf16[192,512]{1,0:T(8,128)(2,1)S(1)}, u32[]{:S(2)}, u32[]{:S(2)}) collective-permute-start(bf16[192,512]{1,0:T(8,128)(2,1)S(1)} %get-tuple-element.77), channel_id=1, source_target_pairs={{0,1},{2,0},{4,2},{6,4},{7,6},{5,7},{3,5},{1,3},{8,9},{10,8},{12,1... | collective-permute-start | bytes 589832 | tf_op jit(solution)/shard_map/ppermute | solution.py:210
  24.1 8.6 %collective-permute-start.6 = (bf16[192,512]{1,0:T(8,128)(2,1)S(1)}, bf16[192,512]{1,0:T(8,128)(2,1)S(1)}, u32[]{:S(2)}, u32[]{:S(2)}) collective-permute-start(bf16[192,512]{1,0:T(8,128)(2,1)S(1)} %get-tuple-element.75), channel_id=1, source_target_pairs={{0,2},{2,4},{4,6},{6,7},{7,5},{5,3},{3,1},{1,0},{8,10},{10,12},{12... | collective-permute-start | bytes 589832 | tf_op jit(solution)/shard_map/ppermute | solution.py:210
  24.6 13.3 %copy-start.1 = (bf16[192,1024]{1,0:T(8,128)(2,1)S(1)}, bf16[192,1024]{1,0:T(8,128)(2,1)}, u32[]{:S(2)}) copy-start(bf16[192,1024]{1,0:T(8,128)(2,1)} %residual_ref.3) | copy-start | bytes 1179652
  24.6 22.9 %slice-start = ((s8[10485760]{0:T(1024)(128)(4,1)}), s8[4194304]{0:T(1024)(128)(4,1)S(1)}, s32[]{:S(2)}) async-start(s8[10485760]{0:T(1024)(128)(4,1)} %bitcast.1), calls=%async_computation | async-start | bytes 8388608
  24.6 22.9 %slice-start.1 = ((s8[10485760]{0:T(1024)(128)(4,1)}), s8[4194304]{0:T(1024)(128)(4,1)S(1)}, s32[]{:S(2)}) async-start(s8[10485760]{0:T(1024)(128)(4,1)} %bitcast.1), calls=%async_computation.1 | async-start | bytes 8388608
  24.6 22.9 %copy-start = (f32[8192]{0:T(1024)S(1)}, f32[8192]{0:T(1024)}, u32[]{:S(2)}) copy-start(f32[8192]{0:T(1024)} %param.8) | copy-start | bytes 98308
  28.6 11.1 %collective-permute-start.11 = (bf16[192,512]{1,0:T(8,128)(2,1)S(1)}, bf16[192,512]{1,0:T(8,128)(2,1)S(1)}, u32[]{:S(2)}, u32[]{:S(2)}) collective-permute-start(bf16[192,512]{1,0:T(8,128)(2,1)S(1)} %get-tuple-element.88), channel_id=1, source_target_pairs={{0,1},{2,0},{4,2},{6,4},{7,6},{5,7},{3,5},{1,3},{8,9},{10,8},{12,1... | collective-permute-start | bytes 589832 | tf_op jit(solution)/shard_map/ppermute | solution.py:210
  30.3 6.8 %collective-permute-start.12 = (bf16[192,512]{1,0:T(8,128)(2,1)S(1)}, bf16[192,512]{1,0:T(8,128)(2,1)S(1)}, u32[]{:S(2)}, u32[]{:S(2)}) collective-permute-start(bf16[192,512]{1,0:T(8,128)(2,1)S(1)} %get-tuple-element.90), channel_id=1, source_target_pairs={{0,2},{2,4},{4,6},{6,7},{7,5},{5,3},{3,1},{1,0},{8,10},{10,12},{12... | collective-permute-start | bytes 589832 | tf_op jit(solution)/shard_map/ppermute | solution.py:210
  30.9 7.0 %collective-permute-start.13 = (bf16[192,512]{1,0:T(8,128)(2,1)S(1)}, bf16[192,512]{1,0:T(8,128)(2,1)S(1)}, u32[]{:S(2)}, u32[]{:S(2)}) collective-permute-start(bf16[192,512]{1,0:T(8,128)(2,1)S(1)} %get-tuple-element.91), channel_id=1, source_target_pairs={{0,1},{2,0},{4,2},{6,4},{7,6},{5,7},{3,5},{1,3},{8,9},{10,8},{12,1... | collective-permute-start | bytes 589832 | tf_op jit(solution)/shard_map/ppermute | solution.py:210
  32.8 6.9 %collective-permute-start.10 = (bf16[192,512]{1,0:T(8,128)(2,1)S(1)}, bf16[192,512]{1,0:T(8,128)(2,1)S(1)}, u32[]{:S(2)}, u32[]{:S(2)}) collective-permute-start(bf16[192,512]{1,0:T(8,128)(2,1)S(1)} %get-tuple-element.87), channel_id=1, source_target_pairs={{0,2},{2,4},{4,6},{6,7},{7,5},{5,3},{3,1},{1,0},{8,10},{10,12},{12... | collective-permute-start | bytes 589832 | tf_op jit(solution)/shard_map/ppermute | solution.py:210
  33.0 14.5 %slice-start.2 = ((s8[10485760]{0:T(1024)(128)(4,1)}), s8[2097152]{0:T(1024)(128)(4,1)S(1)}, s32[]{:S(2)}) async-start(s8[10485760]{0:T(1024)(128)(4,1)} %bitcast.1), calls=%async_computation.2 | async-start | bytes 4194304
  38.0 7.9 %collective-permute-start.17 = (bf16[192,512]{1,0:T(8,128)(2,1)S(1)}, bf16[192,512]{1,0:T(8,128)(2,1)S(1)}, u32[]{:S(2)}, u32[]{:S(2)}) collective-permute-start(bf16[192,512]{1,0:T(8,128)(2,1)S(1)} %shard_map.84.refs_1_), channel_id=1, source_target_pairs={{0,1},{2,0},{4,2},{6,4},{7,6},{5,7},{3,5},{1,3},{8,9},{10,8},{12,1... | collective-permute-start | bytes 589832 | tf_op jit(solution)/shard_map/ppermute | solution.py:210
  39.8 7.7 %collective-permute-start.18 = (bf16[192,512]{1,0:T(8,128)(2,1)S(1)}, bf16[192,512]{1,0:T(8,128)(2,1)S(1)}, u32[]{:S(2)}, u32[]{:S(2)}) collective-permute-start(bf16[192,512]{1,0:T(8,128)(2,1)S(1)} %shard_map.83.refs_0_), channel_id=1, source_target_pairs={{0,2},{2,4},{4,6},{6,7},{7,5},{5,3},{3,1},{1,0},{8,10},{10,12},{12... | collective-permute-start | bytes 589832 | tf_op jit(solution)/shard_map/ppermute | solution.py:210
  40.2 9.9 %collective-permute-start.14 = (bf16[192,512]{1,0:T(8,128)(2,1)S(1)}, bf16[192,512]{1,0:T(8,128)(2,1)S(1)}, u32[]{:S(2)}, u32[]{:S(2)}) collective-permute-start(bf16[192,512]{1,0:T(8,128)(2,1)S(1)} %shard_map.83.refs_0_), channel_id=1, source_target_pairs={{0,1},{2,0},{4,2},{6,4},{7,6},{5,7},{3,5},{1,3},{8,9},{10,8},{12,1... | collective-permute-start | bytes 589832 | tf_op jit(solution)/shard_map/ppermute | solution.py:210
  41.9 9.9 %collective-permute-start.16 = (bf16[192,512]{1,0:T(8,128)(2,1)S(1)}, bf16[192,512]{1,0:T(8,128)(2,1)S(1)}, u32[]{:S(2)}, u32[]{:S(2)}) collective-permute-start(bf16[192,512]{1,0:T(8,128)(2,1)S(1)} %shard_map.84.refs_1_), channel_id=1, source_target_pairs={{0,2},{2,4},{4,6},{6,7},{7,5},{5,3},{3,1},{1,0},{8,10},{10,12},{12... | collective-permute-start | bytes 589832 | tf_op jit(solution)/shard_map/ppermute | solution.py:210
  45.9 8.4 %collective-permute-start.20 = (bf16[192,512]{1,0:T(8,128)(2,1)S(1)}, bf16[192,512]{1,0:T(8,128)(2,1)S(1)}, u32[]{:S(2)}, u32[]{:S(2)}) collective-permute-start(bf16[192,512]{1,0:T(8,128)(2,1)S(1)} %collective-permute-done.17.refs_0_), channel_id=1, source_target_pairs={{0,1},{2,0},{4,2},{6,4},{7,6},{5,7},{3,5},{1,3},{8,9},{10,8},{12,1... | collective-permute-start | bytes 589832 | tf_op jit(solution)/shard_map/ppermute | solution.py:210
  48.1 7.9 %collective-permute-start.22 = (bf16[192,512]{1,0:T(8,128)(2,1)S(1)}, bf16[192,512]{1,0:T(8,128)(2,1)S(1)}, u32[]{:S(2)}, u32[]{:S(2)}) collective-permute-start(bf16[192,512]{1,0:T(8,128)(2,1)S(1)} %get-tuple-element.95), channel_id=1, source_target_pairs={{0,2},{2,4},{4,6},{6,7},{7,5},{5,3},{3,1},{1,0},{8,10},{10,12},{12... | collective-permute-start | bytes 589832 | tf_op jit(solution)/shard_map/ppermute | solution.py:210
  50.1 8.4 %collective-permute-start.15 = (bf16[192,512]{1,0:T(8,128)(2,1)S(1)}, bf16[192,512]{1,0:T(8,128)(2,1)S(1)}, u32[]{:S(2)}, u32[]{:S(2)}) collective-permute-start(bf16[192,512]{1,0:T(8,128)(2,1)S(1)} %collective-permute-done.14.refs_0_), channel_id=1, source_target_pairs={{0,1},{2,0},{4,2},{6,4},{7,6},{5,7},{3,5},{1,3},{8,9},{10,8},{12,1... | collective-permute-start | bytes 589832 | tf_op jit(solution)/shard_map/ppermute | solution.py:210
  52.2 7.9 %collective-permute-start.19 = (bf16[192,512]{1,0:T(8,128)(2,1)S(1)}, bf16[192,512]{1,0:T(8,128)(2,1)S(1)}, u32[]{:S(2)}, u32[]{:S(2)}) collective-permute-start(bf16[192,512]{1,0:T(8,128)(2,1)S(1)} %get-tuple-element.94), channel_id=1, source_target_pairs={{0,2},{2,4},{4,6},{6,7},{7,5},{5,3},{3,1},{1,0},{8,10},{10,12},{12... | collective-permute-start | bytes 589832 | tf_op jit(solution)/shard_map/ppermute | solution.py:210
  54.3 8.4 %collective-permute-start.21 = (bf16[192,512]{1,0:T(8,128)(2,1)S(1)}, bf16[192,512]{1,0:T(8,128)(2,1)S(1)}, u32[]{:S(2)}, u32[]{:S(2)}) collective-permute-start(bf16[192,512]{1,0:T(8,128)(2,1)S(1)} %collective-permute-done.20.refs_0_), channel_id=1, source_target_pairs={{0,1},{2,0},{4,2},{6,4},{7,6},{5,7},{3,5},{1,3},{8,9},{10,8},{12,1... | collective-permute-start | bytes 589832 | tf_op jit(solution)/shard_map/ppermute | solution.py:210
  56.5 7.9 %collective-permute-start.23 = (bf16[192,512]{1,0:T(8,128)(2,1)S(1)}, bf16[192,512]{1,0:T(8,128)(2,1)S(1)}, u32[]{:S(2)}, u32[]{:S(2)}) collective-permute-start(bf16[192,512]{1,0:T(8,128)(2,1)S(1)} %get-tuple-element.98), channel_id=1, source_target_pairs={{0,2},{2,4},{4,6},{6,7},{7,5},{5,3},{3,1},{1,0},{8,10},{10,12},{12... | collective-permute-start | bytes 589832 | tf_op jit(solution)/shard_map/ppermute | solution.py:210
  58.5 6.8 %collective-permute-start.24 = (bf16[192,512]{1,0:T(8,128)(2,1)S(1)}, bf16[192,512]{1,0:T(8,128)(2,1)S(1)}, u32[]{:S(2)}, u32[]{:S(2)}) collective-permute-start(bf16[192,512]{1,0:T(8,128)(2,1)S(1)} %collective-permute-done.15.refs_0_), channel_id=1, source_target_pairs={{0,1},{2,0},{4,2},{6,4},{7,6},{5,7},{3,5},{1,3},{8,9},{10,8},{12,1... | collective-permute-start | bytes 589832 | tf_op jit(solution)/shard_map/ppermute | solution.py:210
  60.2 6.6 %collective-permute-start.25 = (bf16[192,512]{1,0:T(8,128)(2,1)S(1)}, bf16[192,512]{1,0:T(8,128)(2,1)S(1)}, u32[]{:S(2)}, u32[]{:S(2)}) collective-permute-start(bf16[192,512]{1,0:T(8,128)(2,1)S(1)} %collective-permute-done.19.refs_1_), channel_id=1, source_target_pairs={{0,2},{2,4},{4,6},{6,7},{7,5},{5,3},{3,1},{1,0},{8,10},{10,12},{12... | collective-permute-start | bytes 589832 | tf_op jit(solution)/shard_map/ppermute | solution.py:210
  62.7 6.4 %collective-permute-start.27 = (bf16[192,512]{1,0:T(8,128)(2,1)S(1)}, bf16[192,512]{1,0:T(8,128)(2,1)S(1)}, u32[]{:S(2)}, u32[]{:S(2)}) collective-permute-start(bf16[192,512]{1,0:T(8,128)(2,1)S(1)} %collective-permute-done.21.refs_2_), channel_id=1, source_target_pairs={{0,1},{2,0},{4,2},{6,4},{7,6},{5,7},{3,5},{1,3},{8,9},{10,8},{12,1... | collective-permute-start | bytes 589832 | tf_op jit(solution)/shard_map/ppermute | solution.py:210
  64.4 5.7 %collective-permute-start.26 = (bf16[192,512]{1,0:T(8,128)(2,1)S(1)}, bf16[192,512]{1,0:T(8,128)(2,1)S(1)}, u32[]{:S(2)}, u32[]{:S(2)}) collective-permute-start(bf16[192,512]{1,0:T(8,128)(2,1)S(1)} %collective-permute-done.23.refs_3_), channel_id=1, source_target_pairs={{0,2},{2,4},{4,6},{6,7},{7,5},{5,3},{3,1},{1,0},{8,10},{10,12},{12... | collective-permute-start | bytes 589832 | tf_op jit(solution)/shard_map/ppermute | solution.py:210

commit v2 on v1

--- a/solution.py
+++ b/solution.py
@@ -65,7 +65,7 @@
 def down(n, parts, hidden, down_weight, sub, first=False):
     rows, inner = hidden.shape
     vmem, hbm = pl.BlockSpec(memory_space=pltpu.VMEM), pl.BlockSpec(memory_space=pltpu.HBM)
-    pieces = max(p for p in (1, 2, 4) if inner % (16 * p) == 0)
+    pieces = max(p for p in (1, 2) if inner % (16 * p) == 0)
     tile = sub
     count = len(parts) * (sub // tile)
     weight = pltpu.with_memory_space_constraint(down_weight, pltpu.HBM)

time: 71.2 us -> 71.2 us (level)
  no operation moved by 1% of the time
where the time goes in v2:
time: 71.2 us; the launch traced here: 71 us
  starting transfers between devices  30.3 us (43%)
  Pallas kernels  22.8 us (32%)
  waiting for transfers between devices  17.1 us (24%)
  between operations  0.82 us (1%)
    ppermute x28, starting transfers between devices, send(): return lax.ppermute(x, 'tensor', pairs)  30.3 us
    ppermute x28, waiting for transfers between devices, send(): return lax.ppermute(x, 'tensor', pairs)  17.1 us
    pallas_call x5, Pallas kernels, down(): pl.pallas_call(functools.partial(down_kernel, n, parts), out_shape=out_sh...  17 us
    pallas_call x7, Pallas kernels, qkv_step(): pl.pallas_call(functools.partial(qkv_kernel, n, parts, not state, last, j...  5.16 us
  transfers between devices with their start and end apart: 28, of which 11 were waited for; matrix products, arithmetic and copies ran while one was open for 0% of the time, Pallas kernels for 27%

profile of v2, /device:TPU:0, one launch (start us, length us, event | category | flops | bytes accessed | tf_op | source)
XLA Modules:
  0.0 71.0 jit_solution(10582514900977236235)
XLA Ops:
  0.6 2.8 %shard_map.68 = (bf16[192,512]{1,0:T(8,128)(2,1)S(1)}, bf16[192,512]{1,0:T(8,128)(2,1)S(1)}, bf16[192,1792]{1,0:T(8,128)(2,1)S(1)}) custom-call(bf16[192,1792]{1,0:T(8,128)(2,1)} %x_ref.1, bf16[1792,8192]{1,0:T(8,128)(2,1)} %w_ref.9), custom_call_target="tpu_custom_call" | custom-call | flops 704643072 | bytes 3670016 | tf_op jit(solution)/shard_map/pallas_call | solution.py:78
  3.4 3.0 %collective-permute-start.1 = (bf16[192,512]{1,0:T(8,128)(2,1)S(1)}, bf16[192,512]{1,0:T(8,128)(2,1)S(1)}, u32[]{:S(2)}, u32[]{:S(2)}) collective-permute-start(bf16[192,512]{1,0:T(8,128)(2,1)S(1)} %get-tuple-element.59), channel_id=1, source_target_pairs={{0,1},{2,0},{4,2},{6,4},{7,6},{5,7},{3,5},{1,3},{8,9},{10,8},{12,1... | collective-permute-start | bytes 589832 | tf_op jit(solution)/shard_map/ppermute | solution.py:210
  6.6 3.7 %shard_map.69 = (bf16[192,512]{1,0:T(8,128)(2,1)S(1)}, bf16[192,512]{1,0:T(8,128)(2,1)S(1)}, bf16[192,512]{1,0:T(8,128)(2,1)S(1)}, bf16[192,512]{1,0:T(8,128)(2,1)S(1)}) custom-call(bf16[192,1792]{1,0:T(8,128)(2,1)S(1)} %get-tuple-element.55.x_ref.hidden_ref, bf16[1792,8192]{1,0:T(8,128)(2,1)} %w_ref.9), custom_call_target="tpu_custom_call" | custom-call | flops 1409286144 | bytes 7340032 | tf_op jit(solution)/shard_map/pallas_call | solution.py:78
  10.3 2.0 %collective-permute-start.5 = (bf16[192,512]{1,0:T(8,128)(2,1)S(1)}, bf16[192,512]{1,0:T(8,128)(2,1)S(1)}, u32[]{:S(2)}, u32[]{:S(2)}) collective-permute-start(bf16[192,512]{1,0:T(8,128)(2,1)S(1)} %get-tuple-element.69), channel_id=1, source_target_pairs={{0,1},{2,0},{4,2},{6,4},{7,6},{5,7},{3,5},{1,3},{8,9},{10,8},{12,1... | collective-permute-start | bytes 589832 | tf_op jit(solution)/shard_map/ppermute | solution.py:210
  12.5 2.0 %collective-permute-start.3 = (bf16[192,512]{1,0:T(8,128)(2,1)S(1)}, bf16[192,512]{1,0:T(8,128)(2,1)S(1)}, u32[]{:S(2)}, u32[]{:S(2)}) collective-permute-start(bf16[192,512]{1,0:T(8,128)(2,1)S(1)} %get-tuple-element.65), channel_id=1, source_target_pairs={{0,1},{2,0},{4,2},{6,4},{7,6},{5,7},{3,5},{1,3},{8,9},{10,8},{12,1... | collective-permute-start | bytes 589832 | tf_op jit(solution)/shard_map/ppermute | solution.py:210
  14.7 3.7 %shard_map.72 = (bf16[192,512]{1,0:T(8,128)(2,1)S(1)}, bf16[192,512]{1,0:T(8,128)(2,1)S(1)}, bf16[192,512]{1,0:T(8,128)(2,1)S(1)}, bf16[192,512]{1,0:T(8,128)(2,1)S(1)}) custom-call(bf16[192,1792]{1,0:T(8,128)(2,1)S(1)} %get-tuple-element.61.x_ref.hidden_ref, bf16[1792,8192]{1,0:T(8,128)(2,1)} %w_ref.9), custom_call_target="tpu_custom_call" | custom-call | flops 1409286144 | bytes 7340032 | tf_op jit(solution)/shard_map/pallas_call | solution.py:78
  18.5 1.9 %collective-permute-start.9 = (bf16[192,512]{1,0:T(8,128)(2,1)S(1)}, bf16[192,512]{1,0:T(8,128)(2,1)S(1)}, u32[]{:S(2)}, u32[]{:S(2)}) collective-permute-start(bf16[192,512]{1,0:T(8,128)(2,1)S(1)} %get-tuple-element.81), channel_id=1, source_target_pairs={{0,1},{2,0},{4,2},{6,4},{7,6},{5,7},{3,5},{1,3},{8,9},{10,8},{12,1... | collective-permute-start | bytes 589832 | tf_op jit(solution)/shard_map/ppermute | solution.py:210
  20.5 0.2 collective-permute-start.8
  20.7 1.6 %collective-permute-done.3.x_ref = bf16[192,512]{1,0:T(8,128)(2,1)S(1)} collective-permute-done((bf16[192,512]{1,0:T(8,128)(2,1)S(1)}, bf16[192,512]{1,0:T(8,128)(2,1)S(1)}, u32[]{:S(2)}, u32[]{:S(2)}) %collective-permute-start.3) | collective-permute-done | bytes 196640 | tf_op jit(solution)/shard_map/ppermute | solution.py:210
  22.4 1.7 %collective-permute-start.7 = (bf16[192,512]{1,0:T(8,128)(2,1)S(1)}, bf16[192,512]{1,0:T(8,128)(2,1)S(1)}, u32[]{:S(2)}, u32[]{:S(2)}) collective-permute-start(bf16[192,512]{1,0:T(8,128)(2,1)S(1)} %get-tuple-element.77), channel_id=1, source_target_pairs={{0,1},{2,0},{4,2},{6,4},{7,6},{5,7},{3,5},{1,3},{8,9},{10,8},{12,1... | collective-permute-start | bytes 589832 | tf_op jit(solution)/shard_map/ppermute | solution.py:210
  24.1 0.5 collective-permute-start.6
  24.6 3.9 %shard_map.77 = (bf16[192,512]{1,0:T(8,128)(2,1)S(1)}, bf16[192,512]{1,0:T(8,128)(2,1)S(1)}, bf16[192,512]{1,0:T(8,128)(2,1)S(1)}, bf16[192,512]{1,0:T(8,128)(2,1)S(1)}) custom-call(bf16[192,1792]{1,0:T(8,128)(2,1)S(1)} %get-tuple-element.73.x_ref.hidden_ref, bf16[1792,8192]{1,0:T(8,128)(2,1)} %w_ref.9), custom_call_target="tpu_custom_call" | custom-call | flops 1409286144 | bytes 7340032 | tf_op jit(solution)/shard_map/pallas_call | solution.py:78
  28.6 1.7 %collective-permute-start.11 = (bf16[192,512]{1,0:T(8,128)(2,1)S(1)}, bf16[192,512]{1,0:T(8,128)(2,1)S(1)}, u32[]{:S(2)}, u32[]{:S(2)}) collective-permute-start(bf16[192,512]{1,0:T(8,128)(2,1)S(1)} %get-tuple-element.88), channel_id=1, source_target_pairs={{0,1},{2,0},{4,2},{6,4},{7,6},{5,7},{3,5},{1,3},{8,9},{10,8},{12,1... | collective-permute-start | bytes 589832 | tf_op jit(solution)/shard_map/ppermute | solution.py:210
  30.3 0.5 collective-permute-start.12
  30.8 1.8 %collective-permute-start.13 = (bf16[192,512]{1,0:T(8,128)(2,1)S(1)}, bf16[192,512]{1,0:T(8,128)(2,1)S(1)}, u32[]{:S(2)}, u32[]{:S(2)}) collective-permute-start(bf16[192,512]{1,0:T(8,128)(2,1)S(1)} %get-tuple-element.91), channel_id=1, source_target_pairs={{0,1},{2,0},{4,2},{6,4},{7,6},{5,7},{3,5},{1,3},{8,9},{10,8},{12,1... | collective-permute-start | bytes 589832 | tf_op jit(solution)/shard_map/ppermute | solution.py:210
  32.6 0.3 collective-permute-start.10
  33.0 2.7 %shard_map.82 = (bf16[192,512]{1,0:T(8,128)(2,1)S(1)}, bf16[192,512]{1,0:T(8,128)(2,1)S(1)}) custom-call(bf16[192,1792]{1,0:T(8,128)(2,1)S(1)} %get-tuple-element.85.x_ref, bf16[1792,8192]{1,0:T(8,128)(2,1)} %w_ref.9), custom_call_target="tpu_custom_call" | custom-call | flops 704643072 | bytes 3670016 | tf_op jit(solution)/shard_map/pallas_call | solution.py:78
  35.7 1.3 %collective-permute-done.12.x_ref = bf16[192,512]{1,0:T(8,128)(2,1)S(1)} collective-permute-done((bf16[192,512]{1,0:T(8,128)(2,1)S(1)}, bf16[192,512]{1,0:T(8,128)(2,1)S(1)}, u32[]{:S(2)}, u32[]{:S(2)}) %collective-permute-start.12) | collective-permute-done | bytes 196640 | tf_op jit(solution)/shard_map/ppermute | solution.py:210
  37.1 0.8 %collective-permute-done.13.y_ref = bf16[192,512]{1,0:T(8,128)(2,1)S(1)} collective-permute-done((bf16[192,512]{1,0:T(8,128)(2,1)S(1)}, bf16[192,512]{1,0:T(8,128)(2,1)S(1)}, u32[]{:S(2)}, u32[]{:S(2)}) %collective-permute-start.13) | collective-permute-done | bytes 196640 | tf_op jit(solution)/shard_map/ppermute | solution.py:210
  37.9 1.7 %collective-permute-start.17 = (bf16[192,512]{1,0:T(8,128)(2,1)S(1)}, bf16[192,512]{1,0:T(8,128)(2,1)S(1)}, u32[]{:S(2)}, u32[]{:S(2)}) collective-permute-start(bf16[192,512]{1,0:T(8,128)(2,1)S(1)} %shard_map.84.refs_1_), channel_id=1, source_target_pairs={{0,1},{2,0},{4,2},{6,4},{7,6},{5,7},{3,5},{1,3},{8,9},{10,8},{12,1... | collective-permute-start | bytes 589832 | tf_op jit(solution)/shard_map/ppermute | solution.py:210
  39.7 0.5 collective-permute-start.18
  40.2 1.6 %collective-permute-start.14 = (bf16[192,512]{1,0:T(8,128)(2,1)S(1)}, bf16[192,512]{1,0:T(8,128)(2,1)S(1)}, u32[]{:S(2)}, u32[]{:S(2)}) collective-permute-start(bf16[192,512]{1,0:T(8,128)(2,1)S(1)} %shard_map.83.refs_0_), channel_id=1, source_target_pairs={{0,1},{2,0},{4,2},{6,4},{7,6},{5,7},{3,5},{1,3},{8,9},{10,8},{12,1... | collective-permute-start | bytes 589832 | tf_op jit(solution)/shard_map/ppermute | solution.py:210
  41.8 0.4 collective-permute-start.16
  42.2 3.6 %collective-permute-done.17.refs_0_ = bf16[192,512]{1,0:T(8,128)(2,1)S(1)} collective-permute-done((bf16[192,512]{1,0:T(8,128)(2,1)S(1)}, bf16[192,512]{1,0:T(8,128)(2,1)S(1)}, u32[]{:S(2)}, u32[]{:S(2)}) %collective-permute-start.17) | collective-permute-done | bytes 196640 | tf_op jit(solution)/shard_map/ppermute | solution.py:210
  45.8 1.6 %collective-permute-start.20 = (bf16[192,512]{1,0:T(8,128)(2,1)S(1)}, bf16[192,512]{1,0:T(8,128)(2,1)S(1)}, u32[]{:S(2)}, u32[]{:S(2)}) collective-permute-start(bf16[192,512]{1,0:T(8,128)(2,1)S(1)} %collective-permute-done.17.refs_0_), channel_id=1, source_target_pairs={{0,1},{2,0},{4,2},{6,4},{7,6},{5,7},{3,5},{1,3},{8,9},{10,8},{12,1... | collective-permute-start | bytes 589832 | tf_op jit(solution)/shard_map/ppermute | solution.py:210
  47.5 0.5 shard_map.85
  48.0 0.5 collective-permute-start.22
  48.5 1.6 %collective-permute-done.14.refs_0_ = bf16[192,512]{1,0:T(8,128)(2,1)S(1)} collective-permute-done((bf16[192,512]{1,0:T(8,128)(2,1)S(1)}, bf16[192,512]{1,0:T(8,128)(2,1)S(1)}, u32[]{:S(2)}, u32[]{:S(2)}) %collective-permute-start.14) | collective-permute-done | bytes 196640 | tf_op jit(solution)/shard_map/ppermute | solution.py:210
  50.0 1.6 %collective-permute-start.15 = (bf16[192,512]{1,0:T(8,128)(2,1)S(1)}, bf16[192,512]{1,0:T(8,128)(2,1)S(1)}, u32[]{:S(2)}, u32[]{:S(2)}) collective-permute-start(bf16[192,512]{1,0:T(8,128)(2,1)S(1)} %collective-permute-done.14.refs_0_), channel_id=1, source_target_pairs={{0,1},{2,0},{4,2},{6,4},{7,6},{5,7},{3,5},{1,3},{8,9},{10,8},{12,1... | collective-permute-start | bytes 589832 | tf_op jit(solution)/shard_map/ppermute | solution.py:210
  51.7 0.5 shard_map.86
  52.2 0.5 collective-permute-start.19
  52.6 1.6 %collective-permute-done.20.refs_0_ = bf16[192,512]{1,0:T(8,128)(2,1)S(1)} collective-permute-done((bf16[192,512]{1,0:T(8,128)(2,1)S(1)}, bf16[192,512]{1,0:T(8,128)(2,1)S(1)}, u32[]{:S(2)}, u32[]{:S(2)}) %collective-permute-start.20) | collective-permute-done | bytes 196640 | tf_op jit(solution)/shard_map/ppermute | solution.py:210
  54.3 1.6 %collective-permute-start.21 = (bf16[192,512]{1,0:T(8,128)(2,1)S(1)}, bf16[192,512]{1,0:T(8,128)(2,1)S(1)}, u32[]{:S(2)}, u32[]{:S(2)}) collective-permute-start(bf16[192,512]{1,0:T(8,128)(2,1)S(1)} %collective-permute-done.20.refs_0_), channel_id=1, source_target_pairs={{0,1},{2,0},{4,2},{6,4},{7,6},{5,7},{3,5},{1,3},{8,9},{10,8},{12,1... | collective-permute-start | bytes 589832 | tf_op jit(solution)/shard_map/ppermute | solution.py:210
  55.9 0.5 shard_map.87
  56.4 0.5 collective-permute-start.23
  56.9 1.6 %collective-permute-done.15.refs_0_ = bf16[192,512]{1,0:T(8,128)(2,1)S(1)} collective-permute-done((bf16[192,512]{1,0:T(8,128)(2,1)S(1)}, bf16[192,512]{1,0:T(8,128)(2,1)S(1)}, u32[]{:S(2)}, u32[]{:S(2)}) %collective-permute-start.15) | collective-permute-done | bytes 196640 | tf_op jit(solution)/shard_map/ppermute | solution.py:210
  58.5 1.6 %collective-permute-start.24 = (bf16[192,512]{1,0:T(8,128)(2,1)S(1)}, bf16[192,512]{1,0:T(8,128)(2,1)S(1)}, u32[]{:S(2)}, u32[]{:S(2)}) collective-permute-start(bf16[192,512]{1,0:T(8,128)(2,1)S(1)} %collective-permute-done.15.refs_0_), channel_id=1, source_target_pairs={{0,1},{2,0},{4,2},{6,4},{7,6},{5,7},{3,5},{1,3},{8,9},{10,8},{12,1... | collective-permute-start | bytes 589832 | tf_op jit(solution)/shard_map/ppermute | solution.py:210
  60.1 0.4 collective-permute-start.25
  60.5 2.2 %collective-permute-done.21.refs_2_ = bf16[192,512]{1,0:T(8,128)(2,1)S(1)} collective-permute-done((bf16[192,512]{1,0:T(8,128)(2,1)S(1)}, bf16[192,512]{1,0:T(8,128)(2,1)S(1)}, u32[]{:S(2)}, u32[]{:S(2)}) %collective-permute-start.21) | collective-permute-done | bytes 196640 | tf_op jit(solution)/shard_map/ppermute | solution.py:210
  62.7 1.6 %collective-permute-start.27 = (bf16[192,512]{1,0:T(8,128)(2,1)S(1)}, bf16[192,512]{1,0:T(8,128)(2,1)S(1)}, u32[]{:S(2)}, u32[]{:S(2)}) collective-permute-start(bf16[192,512]{1,0:T(8,128)(2,1)S(1)} %collective-permute-done.21.refs_2_), channel_id=1, source_target_pairs={{0,1},{2,0},{4,2},{6,4},{7,6},{5,7},{3,5},{1,3},{8,9},{10,8},{12,1... | collective-permute-start | bytes 589832 | tf_op jit(solution)/shard_map/ppermute | solution.py:210
  64.3 0.4 collective-permute-start.26
  64.7 0.5 collective-permute-done.24.refs_4_
  65.2 1.5 %collective-permute-done.25.refs_5_ = bf16[192,512]{1,0:T(8,128)(2,1)S(1)} collective-permute-done((bf16[192,512]{1,0:T(8,128)(2,1)S(1)}, bf16[192,512]{1,0:T(8,128)(2,1)S(1)}, u32[]{:S(2)}, u32[]{:S(2)}) %collective-permute-start.25) | collective-permute-done | bytes 196640 | tf_op jit(solution)/shard_map/ppermute | solution.py:210
  66.7 1.1 %shard_map.88 = (f32[192,640]{1,0:T(8,128)S(1)}, f32[192,128]{1,0:T(8,128)S(1)}) custom-call(bf16[192,512]{1,0:T(8,128)(2,1)S(1)} %collective-permute-done.15.refs_0_, bf16[192,512]{1,0:T(8,128)(2,1)S(1)} %collective-permute-done.19.refs_1_, bf16[192,512]{1,0:T(8,128)(2,1)S(1)} %collective-permute-done.21.refs_2_, ...), custom_call_target="tpu_custom_call" | custom-call | flops 754974720 | bytes 3932160 | tf_op jit(solution)/shard_map/pallas_call | solution.py:181
  67.8 1.2 %shard_map.89 = (f32[192,640]{1,0:T(8,128)S(1)}, f32[192,128]{1,0:T(8,128)S(1)}, bf16[192,1024]{1,0:T(8,128)(2,1)}) custom-call(bf16[192,512]{1,0:T(8,128)(2,1)S(1)} %shard_map.83.refs_0_, bf16[192,512]{1,0:T(8,128)(2,1)S(1)} %shard_map.84.refs_1_, f32[1,8192]{1,0:T(1,128)S(1)} %bitcast.7, bf16[8192,640]{1,0:T(8,128)(2,1)S(1)} %bitcast.2, ...), custom_call_target="tpu_custom_call" | custom-call | flops 251658240 | bytes 1310720 | tf_op jit(solution)/shard_map/pallas_call | solution.py:181
  69.1 0.3 shard_map.90
  69.4 0.6 collective-permute-done.26.refs_0_
  70.0 1.0 %shard_map.91 = bf16[192,640]{1,0:T(8,128)(2,1)} custom-call(bf16[192,512]{1,0:T(8,128)(2,1)S(1)} %collective-permute-done.26.refs_0_, f32[1,8192]{1,0:T(1,128)S(1)} %bitcast.9, bf16[8192,640]{1,0:T(8,128)(2,1)S(1)} %bitcast.2, f32[192,640]{1,0:T(8,128)S(1)} %get-tuple-element.106.refs_3_, f32[192,128]{1,0:T(8,128)S(1)} %get-tuple-element.107.refs_4_), custom_call_target="tpu_custom_call" | custom-call | flops 125829120 | bytes 655360 | tf_op jit(solution)/shard_map/pallas_call | solution.py:181
  (43 shorter events, 1.2 us)
Async XLA Ops:
  3.4 9.0 %collective-permute-start.1 = (bf16[192,512]{1,0:T(8,128)(2,1)S(1)}, bf16[192,512]{1,0:T(8,128)(2,1)S(1)}, u32[]{:S(2)}, u32[]{:S(2)}) collective-permute-start(bf16[192,512]{1,0:T(8,128)(2,1)S(1)} %get-tuple-element.59), channel_id=1, source_target_pairs={{0,1},{2,0},{4,2},{6,4},{7,6},{5,7},{3,5},{1,3},{8,9},{10,8},{12,1... | collective-permute-start | bytes 589832 | tf_op jit(solution)/shard_map/ppermute | solution.py:210
  6.5 8.0 %collective-permute-start = (bf16[192,512]{1,0:T(8,128)(2,1)S(1)}, bf16[192,512]{1,0:T(8,128)(2,1)S(1)}, u32[]{:S(2)}, u32[]{:S(2)}) collective-permute-start(bf16[192,512]{1,0:T(8,128)(2,1)S(1)} %get-tuple-element.57), channel_id=1, source_target_pairs={{0,2},{2,4},{4,6},{6,7},{7,5},{5,3},{3,1},{1,0},{8,10},{10,12},{12... | collective-permute-start | bytes 589832 | tf_op jit(solution)/shard_map/ppermute | solution.py:210
  10.3 8.1 %collective-permute-start.5 = (bf16[192,512]{1,0:T(8,128)(2,1)S(1)}, bf16[192,512]{1,0:T(8,128)(2,1)S(1)}, u32[]{:S(2)}, u32[]{:S(2)}) collective-permute-start(bf16[192,512]{1,0:T(8,128)(2,1)S(1)} %get-tuple-element.69), channel_id=1, source_target_pairs={{0,1},{2,0},{4,2},{6,4},{7,6},{5,7},{3,5},{1,3},{8,9},{10,8},{12,1... | collective-permute-start | bytes 589832 | tf_op jit(solution)/shard_map/ppermute | solution.py:210
  12.3 8.1 %collective-permute-start.4 = (bf16[192,512]{1,0:T(8,128)(2,1)S(1)}, bf16[192,512]{1,0:T(8,128)(2,1)S(1)}, u32[]{:S(2)}, u32[]{:S(2)}) collective-permute-start(bf16[192,512]{1,0:T(8,128)(2,1)S(1)} %get-tuple-element.67), channel_id=1, source_target_pairs={{0,2},{2,4},{4,6},{6,7},{7,5},{5,3},{3,1},{1,0},{8,10},{10,12},{12... | collective-permute-start | bytes 589832 | tf_op jit(solution)/shard_map/ppermute | solution.py:210
  12.5 9.8 %collective-permute-start.3 = (bf16[192,512]{1,0:T(8,128)(2,1)S(1)}, bf16[192,512]{1,0:T(8,128)(2,1)S(1)}, u32[]{:S(2)}, u32[]{:S(2)}) collective-permute-start(bf16[192,512]{1,0:T(8,128)(2,1)S(1)} %get-tuple-element.65), channel_id=1, source_target_pairs={{0,1},{2,0},{4,2},{6,4},{7,6},{5,7},{3,5},{1,3},{8,9},{10,8},{12,1... | collective-permute-start | bytes 589832 | tf_op jit(solution)/shard_map/ppermute | solution.py:210
  14.5 9.6 %collective-permute-start.2 = (bf16[192,512]{1,0:T(8,128)(2,1)S(1)}, bf16[192,512]{1,0:T(8,128)(2,1)S(1)}, u32[]{:S(2)}, u32[]{:S(2)}) collective-permute-start(bf16[192,512]{1,0:T(8,128)(2,1)S(1)} %get-tuple-element.63), channel_id=1, source_target_pairs={{0,2},{2,4},{4,6},{6,7},{7,5},{5,3},{3,1},{1,0},{8,10},{10,12},{12... | collective-permute-start | bytes 589832 | tf_op jit(solution)/shard_map/ppermute | solution.py:210
  18.5 10.0 %collective-permute-start.9 = (bf16[192,512]{1,0:T(8,128)(2,1)S(1)}, bf16[192,512]{1,0:T(8,128)(2,1)S(1)}, u32[]{:S(2)}, u32[]{:S(2)}) collective-permute-start(bf16[192,512]{1,0:T(8,128)(2,1)S(1)} %get-tuple-element.81), channel_id=1, source_target_pairs={{0,1},{2,0},{4,2},{6,4},{7,6},{5,7},{3,5},{1,3},{8,9},{10,8},{12,1... | collective-permute-start | bytes 589832 | tf_op jit(solution)/shard_map/ppermute | solution.py:210
  20.5 9.7 %collective-permute-start.8 = (bf16[192,512]{1,0:T(8,128)(2,1)S(1)}, bf16[192,512]{1,0:T(8,128)(2,1)S(1)}, u32[]{:S(2)}, u32[]{:S(2)}) collective-permute-start(bf16[192,512]{1,0:T(8,128)(2,1)S(1)} %get-tuple-element.79), channel_id=1, source_target_pairs={{0,2},{2,4},{4,6},{6,7},{7,5},{5,3},{3,1},{1,0},{8,10},{10,12},{12... | collective-permute-start | bytes 589832 | tf_op jit(solution)/shard_map/ppermute | solution.py:210
  22.4 8.4 %collective-permute-start.7 = (bf16[192,512]{1,0:T(8,128)(2,1)S(1)}, bf16[192,512]{1,0:T(8,128)(2,1)S(1)}, u32[]{:S(2)}, u32[]{:S(2)}) collective-permute-start(bf16[192,512]{1,0:T(8,128)(2,1)S(1)} %get-tuple-element.77), channel_id=1, source_target_pairs={{0,1},{2,0},{4,2},{6,4},{7,6},{5,7},{3,5},{1,3},{8,9},{10,8},{12,1... | collective-permute-start | bytes 589832 | tf_op jit(solution)/shard_map/ppermute | solution.py:210
  24.1 8.5 %collective-permute-start.6 = (bf16[192,512]{1,0:T(8,128)(2,1)S(1)}, bf16[192,512]{1,0:T(8,128)(2,1)S(1)}, u32[]{:S(2)}, u32[]{:S(2)}) collective-permute-start(bf16[192,512]{1,0:T(8,128)(2,1)S(1)} %get-tuple-element.75), channel_id=1, source_target_pairs={{0,2},{2,4},{4,6},{6,7},{7,5},{5,3},{3,1},{1,0},{8,10},{10,12},{12... | collective-permute-start | bytes 589832 | tf_op jit(solution)/shard_map/ppermute | solution.py:210
  24.5 13.3 %copy-start.1 = (bf16[192,1024]{1,0:T(8,128)(2,1)S(1)}, bf16[192,1024]{1,0:T(8,128)(2,1)}, u32[]{:S(2)}) copy-start(bf16[192,1024]{1,0:T(8,128)(2,1)} %residual_ref.3) | copy-start | bytes 1179652
  24.6 22.9 %slice-start = ((s8[10485760]{0:T(1024)(128)(4,1)}), s8[4194304]{0:T(1024)(128)(4,1)S(1)}, s32[]{:S(2)}) async-start(s8[10485760]{0:T(1024)(128)(4,1)} %bitcast.1), calls=%async_computation | async-start | bytes 8388608
  24.6 22.9 %slice-start.1 = ((s8[10485760]{0:T(1024)(128)(4,1)}), s8[4194304]{0:T(1024)(128)(4,1)S(1)}, s32[]{:S(2)}) async-start(s8[10485760]{0:T(1024)(128)(4,1)} %bitcast.1), calls=%async_computation.1 | async-start | bytes 8388608
  24.6 22.9 %copy-start = (f32[8192]{0:T(1024)S(1)}, f32[8192]{0:T(1024)}, u32[]{:S(2)}) copy-start(f32[8192]{0:T(1024)} %param.8) | copy-start | bytes 98308
  28.6 11.0 %collective-permute-start.11 = (bf16[192,512]{1,0:T(8,128)(2,1)S(1)}, bf16[192,512]{1,0:T(8,128)(2,1)S(1)}, u32[]{:S(2)}, u32[]{:S(2)}) collective-permute-start(bf16[192,512]{1,0:T(8,128)(2,1)S(1)} %get-tuple-element.88), channel_id=1, source_target_pairs={{0,1},{2,0},{4,2},{6,4},{7,6},{5,7},{3,5},{1,3},{8,9},{10,8},{12,1... | collective-permute-start | bytes 589832 | tf_op jit(solution)/shard_map/ppermute | solution.py:210
  30.3 6.8 %collective-permute-start.12 = (bf16[192,512]{1,0:T(8,128)(2,1)S(1)}, bf16[192,512]{1,0:T(8,128)(2,1)S(1)}, u32[]{:S(2)}, u32[]{:S(2)}) collective-permute-start(bf16[192,512]{1,0:T(8,128)(2,1)S(1)} %get-tuple-element.90), channel_id=1, source_target_pairs={{0,2},{2,4},{4,6},{6,7},{7,5},{5,3},{3,1},{1,0},{8,10},{10,12},{12... | collective-permute-start | bytes 589832 | tf_op jit(solution)/shard_map/ppermute | solution.py:210
  30.8 7.0 %collective-permute-start.13 = (bf16[192,512]{1,0:T(8,128)(2,1)S(1)}, bf16[192,512]{1,0:T(8,128)(2,1)S(1)}, u32[]{:S(2)}, u32[]{:S(2)}) collective-permute-start(bf16[192,512]{1,0:T(8,128)(2,1)S(1)} %get-tuple-element.91), channel_id=1, source_target_pairs={{0,1},{2,0},{4,2},{6,4},{7,6},{5,7},{3,5},{1,3},{8,9},{10,8},{12,1... | collective-permute-start | bytes 589832 | tf_op jit(solution)/shard_map/ppermute | solution.py:210
  32.6 7.0 %collective-permute-start.10 = (bf16[192,512]{1,0:T(8,128)(2,1)S(1)}, bf16[192,512]{1,0:T(8,128)(2,1)S(1)}, u32[]{:S(2)}, u32[]{:S(2)}) collective-permute-start(bf16[192,512]{1,0:T(8,128)(2,1)S(1)} %get-tuple-element.87), channel_id=1, source_target_pairs={{0,2},{2,4},{4,6},{6,7},{7,5},{5,3},{3,1},{1,0},{8,10},{10,12},{12... | collective-permute-start | bytes 589832 | tf_op jit(solution)/shard_map/ppermute | solution.py:210
  33.0 14.5 %slice-start.2 = ((s8[10485760]{0:T(1024)(128)(4,1)}), s8[2097152]{0:T(1024)(128)(4,1)S(1)}, s32[]{:S(2)}) async-start(s8[10485760]{0:T(1024)(128)(4,1)} %bitcast.1), calls=%async_computation.2 | async-start | bytes 4194304
  37.9 7.9 %collective-permute-start.17 = (bf16[192,512]{1,0:T(8,128)(2,1)S(1)}, bf16[192,512]{1,0:T(8,128)(2,1)S(1)}, u32[]{:S(2)}, u32[]{:S(2)}) collective-permute-start(bf16[192,512]{1,0:T(8,128)(2,1)S(1)} %shard_map.84.refs_1_), channel_id=1, source_target_pairs={{0,1},{2,0},{4,2},{6,4},{7,6},{5,7},{3,5},{1,3},{8,9},{10,8},{12,1... | collective-permute-start | bytes 589832 | tf_op jit(solution)/shard_map/ppermute | solution.py:210
  39.7 7.7 %collective-permute-start.18 = (bf16[192,512]{1,0:T(8,128)(2,1)S(1)}, bf16[192,512]{1,0:T(8,128)(2,1)S(1)}, u32[]{:S(2)}, u32[]{:S(2)}) collective-permute-start(bf16[192,512]{1,0:T(8,128)(2,1)S(1)} %shard_map.83.refs_0_), channel_id=1, source_target_pairs={{0,2},{2,4},{4,6},{6,7},{7,5},{5,3},{3,1},{1,0},{8,10},{10,12},{12... | collective-permute-start | bytes 589832 | tf_op jit(solution)/shard_map/ppermute | solution.py:210
  40.2 9.9 %collective-permute-start.14 = (bf16[192,512]{1,0:T(8,128)(2,1)S(1)}, bf16[192,512]{1,0:T(8,128)(2,1)S(1)}, u32[]{:S(2)}, u32[]{:S(2)}) collective-permute-start(bf16[192,512]{1,0:T(8,128)(2,1)S(1)} %shard_map.83.refs_0_), channel_id=1, source_target_pairs={{0,1},{2,0},{4,2},{6,4},{7,6},{5,7},{3,5},{1,3},{8,9},{10,8},{12,1... | collective-permute-start | bytes 589832 | tf_op jit(solution)/shard_map/ppermute | solution.py:210
  41.8 9.9 %collective-permute-start.16 = (bf16[192,512]{1,0:T(8,128)(2,1)S(1)}, bf16[192,512]{1,0:T(8,128)(2,1)S(1)}, u32[]{:S(2)}, u32[]{:S(2)}) collective-permute-start(bf16[192,512]{1,0:T(8,128)(2,1)S(1)} %shard_map.84.refs_1_), channel_id=1, source_target_pairs={{0,2},{2,4},{4,6},{6,7},{7,5},{5,3},{3,1},{1,0},{8,10},{10,12},{12... | collective-permute-start | bytes 589832 | tf_op jit(solution)/shard_map/ppermute | solution.py:210
  45.8 8.4 %collective-permute-start.20 = (bf16[192,512]{1,0:T(8,128)(2,1)S(1)}, bf16[192,512]{1,0:T(8,128)(2,1)S(1)}, u32[]{:S(2)}, u32[]{:S(2)}) collective-permute-start(bf16[192,512]{1,0:T(8,128)(2,1)S(1)} %collective-permute-done.17.refs_0_), channel_id=1, source_target_pairs={{0,1},{2,0},{4,2},{6,4},{7,6},{5,7},{3,5},{1,3},{8,9},{10,8},{12,1... | collective-permute-start | bytes 589832 | tf_op jit(solution)/shard_map/ppermute | solution.py:210
  48.0 7.9 %collective-permute-start.22 = (bf16[192,512]{1,0:T(8,128)(2,1)S(1)}, bf16[192,512]{1,0:T(8,128)(2,1)S(1)}, u32[]{:S(2)}, u32[]{:S(2)}) collective-permute-start(bf16[192,512]{1,0:T(8,128)(2,1)S(1)} %get-tuple-element.95), channel_id=1, source_target_pairs={{0,2},{2,4},{4,6},{6,7},{7,5},{5,3},{3,1},{1,0},{8,10},{10,12},{12... | collective-permute-start | bytes 589832 | tf_op jit(solution)/shard_map/ppermute | solution.py:210
  50.0 8.4 %collective-permute-start.15 = (bf16[192,512]{1,0:T(8,128)(2,1)S(1)}, bf16[192,512]{1,0:T(8,128)(2,1)S(1)}, u32[]{:S(2)}, u32[]{:S(2)}) collective-permute-start(bf16[192,512]{1,0:T(8,128)(2,1)S(1)} %collective-permute-done.14.refs_0_), channel_id=1, source_target_pairs={{0,1},{2,0},{4,2},{6,4},{7,6},{5,7},{3,5},{1,3},{8,9},{10,8},{12,1... | collective-permute-start | bytes 589832 | tf_op jit(solution)/shard_map/ppermute | solution.py:210
  52.2 7.9 %collective-permute-start.19 = (bf16[192,512]{1,0:T(8,128)(2,1)S(1)}, bf16[192,512]{1,0:T(8,128)(2,1)S(1)}, u32[]{:S(2)}, u32[]{:S(2)}) collective-permute-start(bf16[192,512]{1,0:T(8,128)(2,1)S(1)} %get-tuple-element.94), channel_id=1, source_target_pairs={{0,2},{2,4},{4,6},{6,7},{7,5},{5,3},{3,1},{1,0},{8,10},{10,12},{12... | collective-permute-start | bytes 589832 | tf_op jit(solution)/shard_map/ppermute | solution.py:210
  54.3 8.4 %collective-permute-start.21 = (bf16[192,512]{1,0:T(8,128)(2,1)S(1)}, bf16[192,512]{1,0:T(8,128)(2,1)S(1)}, u32[]{:S(2)}, u32[]{:S(2)}) collective-permute-start(bf16[192,512]{1,0:T(8,128)(2,1)S(1)} %collective-permute-done.20.refs_0_), channel_id=1, source_target_pairs={{0,1},{2,0},{4,2},{6,4},{7,6},{5,7},{3,5},{1,3},{8,9},{10,8},{12,1... | collective-permute-start | bytes 589832 | tf_op jit(solution)/shard_map/ppermute | solution.py:210
  56.4 7.9 %collective-permute-start.23 = (bf16[192,512]{1,0:T(8,128)(2,1)S(1)}, bf16[192,512]{1,0:T(8,128)(2,1)S(1)}, u32[]{:S(2)}, u32[]{:S(2)}) collective-permute-start(bf16[192,512]{1,0:T(8,128)(2,1)S(1)} %get-tuple-element.98), channel_id=1, source_target_pairs={{0,2},{2,4},{4,6},{6,7},{7,5},{5,3},{3,1},{1,0},{8,10},{10,12},{12... | collective-permute-start | bytes 589832 | tf_op jit(solution)/shard_map/ppermute | solution.py:210
  58.5 6.8 %collective-permute-start.24 = (bf16[192,512]{1,0:T(8,128)(2,1)S(1)}, bf16[192,512]{1,0:T(8,128)(2,1)S(1)}, u32[]{:S(2)}, u32[]{:S(2)}) collective-permute-start(bf16[192,512]{1,0:T(8,128)(2,1)S(1)} %collective-permute-done.15.refs_0_), channel_id=1, source_target_pairs={{0,1},{2,0},{4,2},{6,4},{7,6},{5,7},{3,5},{1,3},{8,9},{10,8},{12,1... | collective-permute-start | bytes 589832 | tf_op jit(solution)/shard_map/ppermute | solution.py:210
  60.1 6.6 %collective-permute-start.25 = (bf16[192,512]{1,0:T(8,128)(2,1)S(1)}, bf16[192,512]{1,0:T(8,128)(2,1)S(1)}, u32[]{:S(2)}, u32[]{:S(2)}) collective-permute-start(bf16[192,512]{1,0:T(8,128)(2,1)S(1)} %collective-permute-done.19.refs_1_), channel_id=1, source_target_pairs={{0,2},{2,4},{4,6},{6,7},{7,5},{5,3},{3,1},{1,0},{8,10},{10,12},{12... | collective-permute-start | bytes 589832 | tf_op jit(solution)/shard_map/ppermute | solution.py:210
  62.7 6.4 %collective-permute-start.27 = (bf16[192,512]{1,0:T(8,128)(2,1)S(1)}, bf16[192,512]{1,0:T(8,128)(2,1)S(1)}, u32[]{:S(2)}, u32[]{:S(2)}) collective-permute-start(bf16[192,512]{1,0:T(8,128)(2,1)S(1)} %collective-permute-done.21.refs_2_), channel_id=1, source_target_pairs={{0,1},{2,0},{4,2},{6,4},{7,6},{5,7},{3,5},{1,3},{8,9},{10,8},{12,1... | collective-permute-start | bytes 589832 | tf_op jit(solution)/shard_map/ppermute | solution.py:210
  64.3 5.7 %collective-permute-start.26 = (bf16[192,512]{1,0:T(8,128)(2,1)S(1)}, bf16[192,512]{1,0:T(8,128)(2,1)S(1)}, u32[]{:S(2)}, u32[]{:S(2)}) collective-permute-start(bf16[192,512]{1,0:T(8,128)(2,1)S(1)} %collective-permute-done.23.refs_3_), channel_id=1, source_target_pairs={{0,2},{2,4},{4,6},{6,7},{7,5},{5,3},{3,1},{1,0},{8,10},{10,12},{12... | collective-permute-start | bytes 589832 | tf_op jit(solution)/shard_map/ppermute | solution.py:210

commit v3 on v2

--- a/solution.py
+++ b/solution.py
@@ -211,11 +211,11 @@
 
         *own, hidden = down(n, plan[0], hidden, down_weight, sub, first=True)
         arrived = [(send(own[0], right), send(own[1], left))]
-        for step in range(1, n - 1, 2):
-            own = down(n, [*plan[step], *plan[step + 1]], hidden, down_weight, sub)
-            for i in range(2):
-                up, down_ = own[2 * i : 2 * i + 2]
-                if step + i > 1:
+        for group in [plan[1:2], plan[2:3]] + [plan[s : s + 2] for s in range(3, n - 1, 2)]:
+            own = down(n, [part for pair in group for part in pair], hidden, down_weight, sub)
+            for i in range(0, len(own), 2):
+                up, down_ = own[i : i + 2]
+                if len(arrived) > 1:
                     from_left, from_right = arrived[-2]
                     down_, hidden = add_step(down_, from_right, hidden)
                     up, hidden = add_step(up, from_left, hidden)

time: 71.2 us -> 71.2 us (level)
  waiting for transfers between devices: 17.1 us -> 15.7 us
  Pallas kernels: 22.8 us -> 24.2 us
    pallas_call x5 -> x6, Pallas kernels: 17 us -> 18.4 us  [down(): pl.pallas_call(functools.partial(down_kernel, n, parts), out_shape=out_sh...]
    ppermute x28, waiting for transfers between devices: 17.1 us -> 15.7 us  [send(): return lax.ppermute(x, 'tensor', pairs)]
  transfers between devices with their start and end apart: 28 -> 28, of which waited for: 11 -> 11; matrix products, arithmetic and copies ran while one was open for 0% -> 0% of each run, Pallas kernels for 27% -> 29%
where the time goes in v3:
time: 71.2 us; the launch traced here: 71.1 us
  starting transfers between devices  30.3 us (43%)
  Pallas kernels  24.2 us (34%)
  waiting for transfers between devices  15.7 us (22%)
  between operations  0.84 us (1%)
    ppermute x28, starting transfers between devices, send(): return lax.ppermute(x, 'tensor', pairs)  30.3 us
    pallas_call x6, Pallas kernels, down(): pl.pallas_call(functools.partial(down_kernel, n, parts), out_shape=out_sh...  18.4 us
    ppermute x28, waiting for transfers between devices, send(): return lax.ppermute(x, 'tensor', pairs)  15.7 us
    pallas_call x7, Pallas kernels, qkv_step(): pl.pallas_call(functools.partial(qkv_kernel, n, parts, not state, last, j...  5.18 us
  transfers between devices with their start and end apart: 28, of which 11 were waited for; matrix products, arithmetic and copies ran while one was open for 0% of the time, Pallas kernels for 29%

profile of v3, /device:TPU:0, one launch (start us, length us, event | category | flops | bytes accessed | tf_op | source)
XLA Modules:
  0.0 71.1 jit_solution(16769323286521714001)
XLA Ops:
  0.6 2.8 %shard_map.68 = (bf16[192,512]{1,0:T(8,128)(2,1)S(1)}, bf16[192,512]{1,0:T(8,128)(2,1)S(1)}, bf16[192,1792]{1,0:T(8,128)(2,1)S(1)}) custom-call(bf16[192,1792]{1,0:T(8,128)(2,1)} %x_ref.1, bf16[1792,8192]{1,0:T(8,128)(2,1)} %w_ref.11), custom_call_target="tpu_custom_call" | custom-call | flops 704643072 | bytes 3670016 | tf_op jit(solution)/shard_map/pallas_call | solution.py:78
  3.4 3.0 %collective-permute-start.1 = (bf16[192,512]{1,0:T(8,128)(2,1)S(1)}, bf16[192,512]{1,0:T(8,128)(2,1)S(1)}, u32[]{:S(2)}, u32[]{:S(2)}) collective-permute-start(bf16[192,512]{1,0:T(8,128)(2,1)S(1)} %get-tuple-element.59), channel_id=1, source_target_pairs={{0,1},{2,0},{4,2},{6,4},{7,6},{5,7},{3,5},{1,3},{8,9},{10,8},{12,1... | collective-permute-start | bytes 589832 | tf_op jit(solution)/shard_map/ppermute | solution.py:210
  6.6 2.6 %shard_map.73 = (bf16[192,512]{1,0:T(8,128)(2,1)S(1)}, bf16[192,512]{1,0:T(8,128)(2,1)S(1)}) custom-call(bf16[192,1792]{1,0:T(8,128)(2,1)S(1)} %get-tuple-element.55.x_ref.hidden_ref, bf16[1792,8192]{1,0:T(8,128)(2,1)} %w_ref.11), custom_call_target="tpu_custom_call" | custom-call | flops 704643072 | bytes 3670016 | tf_op jit(solution)/shard_map/pallas_call | solution.py:78
  9.2 2.0 %collective-permute-start.4 = (bf16[192,512]{1,0:T(8,128)(2,1)S(1)}, bf16[192,512]{1,0:T(8,128)(2,1)S(1)}, u32[]{:S(2)}, u32[]{:S(2)}) collective-permute-start(bf16[192,512]{1,0:T(8,128)(2,1)S(1)} %get-tuple-element.67), channel_id=1, source_target_pairs={{0,2},{2,4},{4,6},{6,7},{7,5},{5,3},{3,1},{1,0},{8,10},{10,12},{12... | collective-permute-start | bytes 589832 | tf_op jit(solution)/shard_map/ppermute | solution.py:210
  11.3 2.6 %shard_map.69 = (bf16[192,512]{1,0:T(8,128)(2,1)S(1)}, bf16[192,512]{1,0:T(8,128)(2,1)S(1)}) custom-call(bf16[192,1792]{1,0:T(8,128)(2,1)S(1)} %get-tuple-element.55.x_ref.hidden_ref, bf16[1792,8192]{1,0:T(8,128)(2,1)} %w_ref.11), custom_call_target="tpu_custom_call" | custom-call | flops 704643072 | bytes 3670016 | tf_op jit(solution)/shard_map/pallas_call | solution.py:78
  13.9 2.0 %collective-permute-start.3 = (bf16[192,512]{1,0:T(8,128)(2,1)S(1)}, bf16[192,512]{1,0:T(8,128)(2,1)S(1)}, u32[]{:S(2)}, u32[]{:S(2)}) collective-permute-start(bf16[192,512]{1,0:T(8,128)(2,1)S(1)} %get-tuple-element.65), channel_id=1, source_target_pairs={{0,1},{2,0},{4,2},{6,4},{7,6},{5,7},{3,5},{1,3},{8,9},{10,8},{12,1... | collective-permute-start | bytes 589832 | tf_op jit(solution)/shard_map/ppermute | solution.py:210
  16.1 3.7 %shard_map.72 = (bf16[192,512]{1,0:T(8,128)(2,1)S(1)}, bf16[192,512]{1,0:T(8,128)(2,1)S(1)}, bf16[192,512]{1,0:T(8,128)(2,1)S(1)}, bf16[192,512]{1,0:T(8,128)(2,1)S(1)}) custom-call(bf16[192,1792]{1,0:T(8,128)(2,1)S(1)} %get-tuple-element.61.x_ref.hidden_ref, bf16[1792,8192]{1,0:T(8,128)(2,1)} %w_ref.11), custom_call_target="tpu_custom_call" | custom-call | flops 1409286144 | bytes 7340032 | tf_op jit(solution)/shard_map/pallas_call | solution.py:78
  19.9 2.0 %collective-permute-start.9 = (bf16[192,512]{1,0:T(8,128)(2,1)S(1)}, bf16[192,512]{1,0:T(8,128)(2,1)S(1)}, u32[]{:S(2)}, u32[]{:S(2)}) collective-permute-start(bf16[192,512]{1,0:T(8,128)(2,1)S(1)} %get-tuple-element.81), channel_id=1, source_target_pairs={{0,1},{2,0},{4,2},{6,4},{7,6},{5,7},{3,5},{1,3},{8,9},{10,8},{12,1... | collective-permute-start | bytes 589832 | tf_op jit(solution)/shard_map/ppermute | solution.py:210
  21.9 0.2 collective-permute-start.8
  22.2 2.0 %collective-permute-start.7 = (bf16[192,512]{1,0:T(8,128)(2,1)S(1)}, bf16[192,512]{1,0:T(8,128)(2,1)S(1)}, u32[]{:S(2)}, u32[]{:S(2)}) collective-permute-start(bf16[192,512]{1,0:T(8,128)(2,1)S(1)} %get-tuple-element.77), channel_id=1, source_target_pairs={{0,1},{2,0},{4,2},{6,4},{7,6},{5,7},{3,5},{1,3},{8,9},{10,8},{12,1... | collective-permute-start | bytes 589832 | tf_op jit(solution)/shard_map/ppermute | solution.py:210
  24.2 0.2 collective-permute-start.6
  24.4 3.9 %shard_map.78 = (bf16[192,512]{1,0:T(8,128)(2,1)S(1)}, bf16[192,512]{1,0:T(8,128)(2,1)S(1)}, bf16[192,512]{1,0:T(8,128)(2,1)S(1)}, bf16[192,512]{1,0:T(8,128)(2,1)S(1)}) custom-call(bf16[192,1792]{1,0:T(8,128)(2,1)S(1)} %get-tuple-element.73.x_ref.hidden_ref, bf16[1792,8192]{1,0:T(8,128)(2,1)} %w_ref.11), custom_call_target="tpu_custom_call" | custom-call | flops 1409286144 | bytes 7340032 | tf_op jit(solution)/shard_map/pallas_call | solution.py:78
  28.4 2.0 %collective-permute-start.11 = (bf16[192,512]{1,0:T(8,128)(2,1)S(1)}, bf16[192,512]{1,0:T(8,128)(2,1)S(1)}, u32[]{:S(2)}, u32[]{:S(2)}) collective-permute-start(bf16[192,512]{1,0:T(8,128)(2,1)S(1)} %get-tuple-element.88), channel_id=1, source_target_pairs={{0,1},{2,0},{4,2},{6,4},{7,6},{5,7},{3,5},{1,3},{8,9},{10,8},{12,1... | collective-permute-start | bytes 589832 | tf_op jit(solution)/shard_map/ppermute | solution.py:210
  30.5 0.3 collective-permute-done.7.x_ref
  30.9 1.6 %collective-permute-start.13 = (bf16[192,512]{1,0:T(8,128)(2,1)S(1)}, bf16[192,512]{1,0:T(8,128)(2,1)S(1)}, u32[]{:S(2)}, u32[]{:S(2)}) collective-permute-start(bf16[192,512]{1,0:T(8,128)(2,1)S(1)} %get-tuple-element.91), channel_id=1, source_target_pairs={{0,1},{2,0},{4,2},{6,4},{7,6},{5,7},{3,5},{1,3},{8,9},{10,8},{12,1... | collective-permute-start | bytes 589832 | tf_op jit(solution)/shard_map/ppermute | solution.py:210
  32.6 0.5 collective-permute-start.10
  33.1 2.7 %shard_map.83 = (bf16[192,512]{1,0:T(8,128)(2,1)S(1)}, bf16[192,512]{1,0:T(8,128)(2,1)S(1)}) custom-call(bf16[192,1792]{1,0:T(8,128)(2,1)S(1)} %get-tuple-element.85.x_ref, bf16[1792,8192]{1,0:T(8,128)(2,1)} %w_ref.11), custom_call_target="tpu_custom_call" | custom-call | flops 704643072 | bytes 3670016 | tf_op jit(solution)/shard_map/pallas_call | solution.py:78
  35.9 1.3 %collective-permute-done.12.x_ref = bf16[192,512]{1,0:T(8,128)(2,1)S(1)} collective-permute-done((bf16[192,512]{1,0:T(8,128)(2,1)S(1)}, bf16[192,512]{1,0:T(8,128)(2,1)S(1)}, u32[]{:S(2)}, u32[]{:S(2)}) %collective-permute-start.12) | collective-permute-done | bytes 196640 | tf_op jit(solution)/shard_map/ppermute | solution.py:210
  37.2 0.9 %collective-permute-done.13.y_ref = bf16[192,512]{1,0:T(8,128)(2,1)S(1)} collective-permute-done((bf16[192,512]{1,0:T(8,128)(2,1)S(1)}, bf16[192,512]{1,0:T(8,128)(2,1)S(1)}, u32[]{:S(2)}, u32[]{:S(2)}) %collective-permute-start.13) | collective-permute-done | bytes 196640 | tf_op jit(solution)/shard_map/ppermute | solution.py:210
  38.2 1.5 %collective-permute-start.17 = (bf16[192,512]{1,0:T(8,128)(2,1)S(1)}, bf16[192,512]{1,0:T(8,128)(2,1)S(1)}, u32[]{:S(2)}, u32[]{:S(2)}) collective-permute-start(bf16[192,512]{1,0:T(8,128)(2,1)S(1)} %shard_map.85.refs_1_), channel_id=1, source_target_pairs={{0,1},{2,0},{4,2},{6,4},{7,6},{5,7},{3,5},{1,3},{8,9},{10,8},{12,1... | collective-permute-start | bytes 589832 | tf_op jit(solution)/shard_map/ppermute | solution.py:210
  39.8 0.7 collective-permute-start.18
  40.4 1.4 %collective-permute-start.14 = (bf16[192,512]{1,0:T(8,128)(2,1)S(1)}, bf16[192,512]{1,0:T(8,128)(2,1)S(1)}, u32[]{:S(2)}, u32[]{:S(2)}) collective-permute-start(bf16[192,512]{1,0:T(8,128)(2,1)S(1)} %shard_map.84.refs_0_), channel_id=1, source_target_pairs={{0,1},{2,0},{4,2},{6,4},{7,6},{5,7},{3,5},{1,3},{8,9},{10,8},{12,1... | collective-permute-start | bytes 589832 | tf_op jit(solution)/shard_map/ppermute | solution.py:210
  41.8 0.6 collective-permute-start.16
  42.4 3.6 %collective-permute-done.17.refs_0_ = bf16[192,512]{1,0:T(8,128)(2,1)S(1)} collective-permute-done((bf16[192,512]{1,0:T(8,128)(2,1)S(1)}, bf16[192,512]{1,0:T(8,128)(2,1)S(1)}, u32[]{:S(2)}, u32[]{:S(2)}) %collective-permute-start.17) | collective-permute-done | bytes 196640 | tf_op jit(solution)/shard_map/ppermute | solution.py:210
  46.1 1.4 %collective-permute-start.20 = (bf16[192,512]{1,0:T(8,128)(2,1)S(1)}, bf16[192,512]{1,0:T(8,128)(2,1)S(1)}, u32[]{:S(2)}, u32[]{:S(2)}) collective-permute-start(bf16[192,512]{1,0:T(8,128)(2,1)S(1)} %collective-permute-done.17.refs_0_), channel_id=1, source_target_pairs={{0,1},{2,0},{4,2},{6,4},{7,6},{5,7},{3,5},{1,3},{8,9},{10,8},{12,1... | collective-permute-start | bytes 589832 | tf_op jit(solution)/shard_map/ppermute | solution.py:210
  47.5 0.5 shard_map.86
  48.1 0.6 collective-permute-start.22
  48.7 1.6 %collective-permute-done.14.refs_0_ = bf16[192,512]{1,0:T(8,128)(2,1)S(1)} collective-permute-done((bf16[192,512]{1,0:T(8,128)(2,1)S(1)}, bf16[192,512]{1,0:T(8,128)(2,1)S(1)}, u32[]{:S(2)}, u32[]{:S(2)}) %collective-permute-start.14) | collective-permute-done | bytes 196640 | tf_op jit(solution)/shard_map/ppermute | solution.py:210
  50.3 1.4 %collective-permute-start.15 = (bf16[192,512]{1,0:T(8,128)(2,1)S(1)}, bf16[192,512]{1,0:T(8,128)(2,1)S(1)}, u32[]{:S(2)}, u32[]{:S(2)}) collective-permute-start(bf16[192,512]{1,0:T(8,128)(2,1)S(1)} %collective-permute-done.14.refs_0_), channel_id=1, source_target_pairs={{0,1},{2,0},{4,2},{6,4},{7,6},{5,7},{3,5},{1,3},{8,9},{10,8},{12,1... | collective-permute-start | bytes 589832 | tf_op jit(solution)/shard_map/ppermute | solution.py:210
  51.7 0.5 shard_map.87
  52.2 0.6 collective-permute-start.19
  52.9 1.6 %collective-permute-done.20.refs_0_ = bf16[192,512]{1,0:T(8,128)(2,1)S(1)} collective-permute-done((bf16[192,512]{1,0:T(8,128)(2,1)S(1)}, bf16[192,512]{1,0:T(8,128)(2,1)S(1)}, u32[]{:S(2)}, u32[]{:S(2)}) %collective-permute-start.20) | collective-permute-done | bytes 196640 | tf_op jit(solution)/shard_map/ppermute | solution.py:210
  54.5 1.4 %collective-permute-start.21 = (bf16[192,512]{1,0:T(8,128)(2,1)S(1)}, bf16[192,512]{1,0:T(8,128)(2,1)S(1)}, u32[]{:S(2)}, u32[]{:S(2)}) collective-permute-start(bf16[192,512]{1,0:T(8,128)(2,1)S(1)} %collective-permute-done.20.refs_0_), channel_id=1, source_target_pairs={{0,1},{2,0},{4,2},{6,4},{7,6},{5,7},{3,5},{1,3},{8,9},{10,8},{12,1... | collective-permute-start | bytes 589832 | tf_op jit(solution)/shard_map/ppermute | solution.py:210
  55.9 0.5 shard_map.88
  56.4 0.7 collective-permute-start.23
  57.1 1.6 %collective-permute-done.15.refs_0_ = bf16[192,512]{1,0:T(8,128)(2,1)S(1)} collective-permute-done((bf16[192,512]{1,0:T(8,128)(2,1)S(1)}, bf16[192,512]{1,0:T(8,128)(2,1)S(1)}, u32[]{:S(2)}, u32[]{:S(2)}) %collective-permute-start.15) | collective-permute-done | bytes 196640 | tf_op jit(solution)/shard_map/ppermute | solution.py:210
  58.7 1.4 %collective-permute-start.24 = (bf16[192,512]{1,0:T(8,128)(2,1)S(1)}, bf16[192,512]{1,0:T(8,128)(2,1)S(1)}, u32[]{:S(2)}, u32[]{:S(2)}) collective-permute-start(bf16[192,512]{1,0:T(8,128)(2,1)S(1)} %collective-permute-done.15.refs_0_), channel_id=1, source_target_pairs={{0,1},{2,0},{4,2},{6,4},{7,6},{5,7},{3,5},{1,3},{8,9},{10,8},{12,1... | collective-permute-start | bytes 589832 | tf_op jit(solution)/shard_map/ppermute | solution.py:210
  60.2 0.6 collective-permute-start.25
  60.8 2.2 %collective-permute-done.21.refs_2_ = bf16[192,512]{1,0:T(8,128)(2,1)S(1)} collective-permute-done((bf16[192,512]{1,0:T(8,128)(2,1)S(1)}, bf16[192,512]{1,0:T(8,128)(2,1)S(1)}, u32[]{:S(2)}, u32[]{:S(2)}) %collective-permute-start.21) | collective-permute-done | bytes 196640 | tf_op jit(solution)/shard_map/ppermute | solution.py:210
  62.9 1.4 %collective-permute-start.27 = (bf16[192,512]{1,0:T(8,128)(2,1)S(1)}, bf16[192,512]{1,0:T(8,128)(2,1)S(1)}, u32[]{:S(2)}, u32[]{:S(2)}) collective-permute-start(bf16[192,512]{1,0:T(8,128)(2,1)S(1)} %collective-permute-done.21.refs_2_), channel_id=1, source_target_pairs={{0,1},{2,0},{4,2},{6,4},{7,6},{5,7},{3,5},{1,3},{8,9},{10,8},{12,1... | collective-permute-start | bytes 589832 | tf_op jit(solution)/shard_map/ppermute | solution.py:210
  64.4 0.6 collective-permute-start.26
  65.0 1.0 %collective-permute-done.24.refs_4_ = bf16[192,512]{1,0:T(8,128)(2,1)S(1)} collective-permute-done((bf16[192,512]{1,0:T(8,128)(2,1)S(1)}, bf16[192,512]{1,0:T(8,128)(2,1)S(1)}, u32[]{:S(2)}, u32[]{:S(2)}) %collective-permute-start.24) | collective-permute-done | bytes 196640 | tf_op jit(solution)/shard_map/ppermute | solution.py:210
  65.9 0.8 %collective-permute-done.25.refs_5_ = bf16[192,512]{1,0:T(8,128)(2,1)S(1)} collective-permute-done((bf16[192,512]{1,0:T(8,128)(2,1)S(1)}, bf16[192,512]{1,0:T(8,128)(2,1)S(1)}, u32[]{:S(2)}, u32[]{:S(2)}) %collective-permute-start.25) | collective-permute-done | bytes 196640 | tf_op jit(solution)/shard_map/ppermute | solution.py:210
  66.7 1.1 %shard_map.89 = (f32[192,640]{1,0:T(8,128)S(1)}, f32[192,128]{1,0:T(8,128)S(1)}) custom-call(bf16[192,512]{1,0:T(8,128)(2,1)S(1)} %collective-permute-done.15.refs_0_, bf16[192,512]{1,0:T(8,128)(2,1)S(1)} %collective-permute-done.19.refs_1_, bf16[192,512]{1,0:T(8,128)(2,1)S(1)} %collective-permute-done.21.refs_2_, ...), custom_call_target="tpu_custom_call" | custom-call | flops 754974720 | bytes 3932160 | tf_op jit(solution)/shard_map/pallas_call | solution.py:181
  67.9 1.2 %shard_map.90 = (f32[192,640]{1,0:T(8,128)S(1)}, f32[192,128]{1,0:T(8,128)S(1)}, bf16[192,1024]{1,0:T(8,128)(2,1)}) custom-call(bf16[192,512]{1,0:T(8,128)(2,1)S(1)} %shard_map.84.refs_0_, bf16[192,512]{1,0:T(8,128)(2,1)S(1)} %shard_map.85.refs_1_, f32[1,8192]{1,0:T(1,128)S(1)} %bitcast.7, bf16[8192,640]{1,0:T(8,128)(2,1)S(1)} %bitcast.2, ...), custom_call_target="tpu_custom_call" | custom-call | flops 251658240 | bytes 1310720 | tf_op jit(solution)/shard_map/pallas_call | solution.py:181
  69.1 0.3 shard_map.91
  69.4 0.7 collective-permute-done.26.refs_0_
  70.0 1.0 %shard_map.92 = bf16[192,640]{1,0:T(8,128)(2,1)} custom-call(bf16[192,512]{1,0:T(8,128)(2,1)S(1)} %collective-permute-done.26.refs_0_, f32[1,8192]{1,0:T(1,128)S(1)} %bitcast.9, bf16[8192,640]{1,0:T(8,128)(2,1)S(1)} %bitcast.2, f32[192,640]{1,0:T(8,128)S(1)} %get-tuple-element.106.refs_3_, f32[192,128]{1,0:T(8,128)S(1)} %get-tuple-element.107.refs_4_), custom_call_target="tpu_custom_call" | custom-call | flops 125829120 | bytes 655360 | tf_op jit(solution)/shard_map/pallas_call | solution.py:181
  (44 shorter events, 1.3 us)
Async XLA Ops:
  3.4 10.4 %collective-permute-start.1 = (bf16[192,512]{1,0:T(8,128)(2,1)S(1)}, bf16[192,512]{1,0:T(8,128)(2,1)S(1)}, u32[]{:S(2)}, u32[]{:S(2)}) collective-permute-start(bf16[192,512]{1,0:T(8,128)(2,1)S(1)} %get-tuple-element.59), channel_id=1, source_target_pairs={{0,1},{2,0},{4,2},{6,4},{7,6},{5,7},{3,5},{1,3},{8,9},{10,8},{12,1... | collective-permute-start | bytes 589832 | tf_op jit(solution)/shard_map/ppermute | solution.py:210
  6.5 9.4 %collective-permute-start = (bf16[192,512]{1,0:T(8,128)(2,1)S(1)}, bf16[192,512]{1,0:T(8,128)(2,1)S(1)}, u32[]{:S(2)}, u32[]{:S(2)}) collective-permute-start(bf16[192,512]{1,0:T(8,128)(2,1)S(1)} %get-tuple-element.57), channel_id=1, source_target_pairs={{0,2},{2,4},{4,6},{6,7},{7,5},{5,3},{3,1},{1,0},{8,10},{10,12},{12... | collective-permute-start | bytes 589832 | tf_op jit(solution)/shard_map/ppermute | solution.py:210
  9.2 12.7 %collective-permute-start.4 = (bf16[192,512]{1,0:T(8,128)(2,1)S(1)}, bf16[192,512]{1,0:T(8,128)(2,1)S(1)}, u32[]{:S(2)}, u32[]{:S(2)}) collective-permute-start(bf16[192,512]{1,0:T(8,128)(2,1)S(1)} %get-tuple-element.67), channel_id=1, source_target_pairs={{0,2},{2,4},{4,6},{6,7},{7,5},{5,3},{3,1},{1,0},{8,10},{10,12},{12... | collective-permute-start | bytes 589832 | tf_op jit(solution)/shard_map/ppermute | solution.py:210
  11.2 8.7 %collective-permute-start.5 = (bf16[192,512]{1,0:T(8,128)(2,1)S(1)}, bf16[192,512]{1,0:T(8,128)(2,1)S(1)}, u32[]{:S(2)}, u32[]{:S(2)}) collective-permute-start(bf16[192,512]{1,0:T(8,128)(2,1)S(1)} %get-tuple-element.69), channel_id=1, source_target_pairs={{0,1},{2,0},{4,2},{6,4},{7,6},{5,7},{3,5},{1,3},{8,9},{10,8},{12,1... | collective-permute-start | bytes 589832 | tf_op jit(solution)/shard_map/ppermute | solution.py:210
  13.9 8.2 %collective-permute-start.3 = (bf16[192,512]{1,0:T(8,128)(2,1)S(1)}, bf16[192,512]{1,0:T(8,128)(2,1)S(1)}, u32[]{:S(2)}, u32[]{:S(2)}) collective-permute-start(bf16[192,512]{1,0:T(8,128)(2,1)S(1)} %get-tuple-element.65), channel_id=1, source_target_pairs={{0,1},{2,0},{4,2},{6,4},{7,6},{5,7},{3,5},{1,3},{8,9},{10,8},{12,1... | collective-permute-start | bytes 589832 | tf_op jit(solution)/shard_map/ppermute | solution.py:210
  15.9 8.2 %collective-permute-start.2 = (bf16[192,512]{1,0:T(8,128)(2,1)S(1)}, bf16[192,512]{1,0:T(8,128)(2,1)S(1)}, u32[]{:S(2)}, u32[]{:S(2)}) collective-permute-start(bf16[192,512]{1,0:T(8,128)(2,1)S(1)} %get-tuple-element.63), channel_id=1, source_target_pairs={{0,2},{2,4},{4,6},{6,7},{7,5},{5,3},{3,1},{1,0},{8,10},{10,12},{12... | collective-permute-start | bytes 589832 | tf_op jit(solution)/shard_map/ppermute | solution.py:210
  19.9 8.4 %collective-permute-start.9 = (bf16[192,512]{1,0:T(8,128)(2,1)S(1)}, bf16[192,512]{1,0:T(8,128)(2,1)S(1)}, u32[]{:S(2)}, u32[]{:S(2)}) collective-permute-start(bf16[192,512]{1,0:T(8,128)(2,1)S(1)} %get-tuple-element.81), channel_id=1, source_target_pairs={{0,1},{2,0},{4,2},{6,4},{7,6},{5,7},{3,5},{1,3},{8,9},{10,8},{12,1... | collective-permute-start | bytes 589832 | tf_op jit(solution)/shard_map/ppermute | solution.py:210
  21.9 8.4 %collective-permute-start.8 = (bf16[192,512]{1,0:T(8,128)(2,1)S(1)}, bf16[192,512]{1,0:T(8,128)(2,1)S(1)}, u32[]{:S(2)}, u32[]{:S(2)}) collective-permute-start(bf16[192,512]{1,0:T(8,128)(2,1)S(1)} %get-tuple-element.79), channel_id=1, source_target_pairs={{0,2},{2,4},{4,6},{6,7},{7,5},{5,3},{3,1},{1,0},{8,10},{10,12},{12... | collective-permute-start | bytes 589832 | tf_op jit(solution)/shard_map/ppermute | solution.py:210
  22.2 8.7 %collective-permute-start.7 = (bf16[192,512]{1,0:T(8,128)(2,1)S(1)}, bf16[192,512]{1,0:T(8,128)(2,1)S(1)}, u32[]{:S(2)}, u32[]{:S(2)}) collective-permute-start(bf16[192,512]{1,0:T(8,128)(2,1)S(1)} %get-tuple-element.77), channel_id=1, source_target_pairs={{0,1},{2,0},{4,2},{6,4},{7,6},{5,7},{3,5},{1,3},{8,9},{10,8},{12,1... | collective-permute-start | bytes 589832 | tf_op jit(solution)/shard_map/ppermute | solution.py:210
  24.2 8.4 %collective-permute-start.6 = (bf16[192,512]{1,0:T(8,128)(2,1)S(1)}, bf16[192,512]{1,0:T(8,128)(2,1)S(1)}, u32[]{:S(2)}, u32[]{:S(2)}) collective-permute-start(bf16[192,512]{1,0:T(8,128)(2,1)S(1)} %get-tuple-element.75), channel_id=1, source_target_pairs={{0,2},{2,4},{4,6},{6,7},{7,5},{5,3},{3,1},{1,0},{8,10},{10,12},{12... | collective-permute-start | bytes 589832 | tf_op jit(solution)/shard_map/ppermute | solution.py:210
  24.4 13.7 %copy-start.1 = (bf16[192,1024]{1,0:T(8,128)(2,1)S(1)}, bf16[192,1024]{1,0:T(8,128)(2,1)}, u32[]{:S(2)}) copy-start(bf16[192,1024]{1,0:T(8,128)(2,1)} %residual_ref.3) | copy-start | bytes 1179652
  24.4 23.1 %slice-start = ((s8[10485760]{0:T(1024)(128)(4,1)}), s8[4194304]{0:T(1024)(128)(4,1)S(1)}, s32[]{:S(2)}) async-start(s8[10485760]{0:T(1024)(128)(4,1)} %bitcast.1), calls=%async_computation | async-start | bytes 8388608
  24.4 23.1 %slice-start.1 = ((s8[10485760]{0:T(1024)(128)(4,1)}), s8[4194304]{0:T(1024)(128)(4,1)S(1)}, s32[]{:S(2)}) async-start(s8[10485760]{0:T(1024)(128)(4,1)} %bitcast.1), calls=%async_computation.1 | async-start | bytes 8388608
  24.4 23.1 %copy-start = (f32[8192]{0:T(1024)S(1)}, f32[8192]{0:T(1024)}, u32[]{:S(2)}) copy-start(f32[8192]{0:T(1024)} %param.8) | copy-start | bytes 98308
  28.4 11.3 %collective-permute-start.11 = (bf16[192,512]{1,0:T(8,128)(2,1)S(1)}, bf16[192,512]{1,0:T(8,128)(2,1)S(1)}, u32[]{:S(2)}, u32[]{:S(2)}) collective-permute-start(bf16[192,512]{1,0:T(8,128)(2,1)S(1)} %get-tuple-element.88), channel_id=1, source_target_pairs={{0,1},{2,0},{4,2},{6,4},{7,6},{5,7},{3,5},{1,3},{8,9},{10,8},{12,1... | collective-permute-start | bytes 589832 | tf_op jit(solution)/shard_map/ppermute | solution.py:210
  30.4 6.8 %collective-permute-start.12 = (bf16[192,512]{1,0:T(8,128)(2,1)S(1)}, bf16[192,512]{1,0:T(8,128)(2,1)S(1)}, u32[]{:S(2)}, u32[]{:S(2)}) collective-permute-start(bf16[192,512]{1,0:T(8,128)(2,1)S(1)} %get-tuple-element.90), channel_id=1, source_target_pairs={{0,2},{2,4},{4,6},{6,7},{7,5},{5,3},{3,1},{1,0},{8,10},{10,12},{12... | collective-permute-start | bytes 589832 | tf_op jit(solution)/shard_map/ppermute | solution.py:210
  30.9 7.1 %collective-permute-start.13 = (bf16[192,512]{1,0:T(8,128)(2,1)S(1)}, bf16[192,512]{1,0:T(8,128)(2,1)S(1)}, u32[]{:S(2)}, u32[]{:S(2)}) collective-permute-start(bf16[192,512]{1,0:T(8,128)(2,1)S(1)} %get-tuple-element.91), channel_id=1, source_target_pairs={{0,1},{2,0},{4,2},{6,4},{7,6},{5,7},{3,5},{1,3},{8,9},{10,8},{12,1... | collective-permute-start | bytes 589832 | tf_op jit(solution)/shard_map/ppermute | solution.py:210
  32.6 7.0 %collective-permute-start.10 = (bf16[192,512]{1,0:T(8,128)(2,1)S(1)}, bf16[192,512]{1,0:T(8,128)(2,1)S(1)}, u32[]{:S(2)}, u32[]{:S(2)}) collective-permute-start(bf16[192,512]{1,0:T(8,128)(2,1)S(1)} %get-tuple-element.87), channel_id=1, source_target_pairs={{0,2},{2,4},{4,6},{6,7},{7,5},{5,3},{3,1},{1,0},{8,10},{10,12},{12... | collective-permute-start | bytes 589832 | tf_op jit(solution)/shard_map/ppermute | solution.py:210
  33.1 14.4 %slice-start.2 = ((s8[10485760]{0:T(1024)(128)(4,1)}), s8[2097152]{0:T(1024)(128)(4,1)S(1)}, s32[]{:S(2)}) async-start(s8[10485760]{0:T(1024)(128)(4,1)} %bitcast.1), calls=%async_computation.2 | async-start | bytes 4194304
  38.2 7.9 %collective-permute-start.17 = (bf16[192,512]{1,0:T(8,128)(2,1)S(1)}, bf16[192,512]{1,0:T(8,128)(2,1)S(1)}, u32[]{:S(2)}, u32[]{:S(2)}) collective-permute-start(bf16[192,512]{1,0:T(8,128)(2,1)S(1)} %shard_map.85.refs_1_), channel_id=1, source_target_pairs={{0,1},{2,0},{4,2},{6,4},{7,6},{5,7},{3,5},{1,3},{8,9},{10,8},{12,1... | collective-permute-start | bytes 589832 | tf_op jit(solution)/shard_map/ppermute | solution.py:210
  39.8 7.7 %collective-permute-start.18 = (bf16[192,512]{1,0:T(8,128)(2,1)S(1)}, bf16[192,512]{1,0:T(8,128)(2,1)S(1)}, u32[]{:S(2)}, u32[]{:S(2)}) collective-permute-start(bf16[192,512]{1,0:T(8,128)(2,1)S(1)} %shard_map.84.refs_0_), channel_id=1, source_target_pairs={{0,2},{2,4},{4,6},{6,7},{7,5},{5,3},{3,1},{1,0},{8,10},{10,12},{12... | collective-permute-start | bytes 589832 | tf_op jit(solution)/shard_map/ppermute | solution.py:210
  40.4 9.9 %collective-permute-start.14 = (bf16[192,512]{1,0:T(8,128)(2,1)S(1)}, bf16[192,512]{1,0:T(8,128)(2,1)S(1)}, u32[]{:S(2)}, u32[]{:S(2)}) collective-permute-start(bf16[192,512]{1,0:T(8,128)(2,1)S(1)} %shard_map.84.refs_0_), channel_id=1, source_target_pairs={{0,1},{2,0},{4,2},{6,4},{7,6},{5,7},{3,5},{1,3},{8,9},{10,8},{12,1... | collective-permute-start | bytes 589832 | tf_op jit(solution)/shard_map/ppermute | solution.py:210
  41.8 9.9 %collective-permute-start.16 = (bf16[192,512]{1,0:T(8,128)(2,1)S(1)}, bf16[192,512]{1,0:T(8,128)(2,1)S(1)}, u32[]{:S(2)}, u32[]{:S(2)}) collective-permute-start(bf16[192,512]{1,0:T(8,128)(2,1)S(1)} %shard_map.85.refs_1_), channel_id=1, source_target_pairs={{0,2},{2,4},{4,6},{6,7},{7,5},{5,3},{3,1},{1,0},{8,10},{10,12},{12... | collective-permute-start | bytes 589832 | tf_op jit(solution)/shard_map/ppermute | solution.py:210
  46.1 8.4 %collective-permute-start.20 = (bf16[192,512]{1,0:T(8,128)(2,1)S(1)}, bf16[192,512]{1,0:T(8,128)(2,1)S(1)}, u32[]{:S(2)}, u32[]{:S(2)}) collective-permute-start(bf16[192,512]{1,0:T(8,128)(2,1)S(1)} %collective-permute-done.17.refs_0_), channel_id=1, source_target_pairs={{0,1},{2,0},{4,2},{6,4},{7,6},{5,7},{3,5},{1,3},{8,9},{10,8},{12,1... | collective-permute-start | bytes 589832 | tf_op jit(solution)/shard_map/ppermute | solution.py:210
  48.1 7.9 %collective-permute-start.22 = (bf16[192,512]{1,0:T(8,128)(2,1)S(1)}, bf16[192,512]{1,0:T(8,128)(2,1)S(1)}, u32[]{:S(2)}, u32[]{:S(2)}) collective-permute-start(bf16[192,512]{1,0:T(8,128)(2,1)S(1)} %get-tuple-element.95), channel_id=1, source_target_pairs={{0,2},{2,4},{4,6},{6,7},{7,5},{5,3},{3,1},{1,0},{8,10},{10,12},{12... | collective-permute-start | bytes 589832 | tf_op jit(solution)/shard_map/ppermute | solution.py:210
  50.3 8.4 %collective-permute-start.15 = (bf16[192,512]{1,0:T(8,128)(2,1)S(1)}, bf16[192,512]{1,0:T(8,128)(2,1)S(1)}, u32[]{:S(2)}, u32[]{:S(2)}) collective-permute-start(bf16[192,512]{1,0:T(8,128)(2,1)S(1)} %collective-permute-done.14.refs_0_), channel_id=1, source_target_pairs={{0,1},{2,0},{4,2},{6,4},{7,6},{5,7},{3,5},{1,3},{8,9},{10,8},{12,1... | collective-permute-start | bytes 589832 | tf_op jit(solution)/shard_map/ppermute | solution.py:210
  52.2 7.9 %collective-permute-start.19 = (bf16[192,512]{1,0:T(8,128)(2,1)S(1)}, bf16[192,512]{1,0:T(8,128)(2,1)S(1)}, u32[]{:S(2)}, u32[]{:S(2)}) collective-permute-start(bf16[192,512]{1,0:T(8,128)(2,1)S(1)} %get-tuple-element.94), channel_id=1, source_target_pairs={{0,2},{2,4},{4,6},{6,7},{7,5},{5,3},{3,1},{1,0},{8,10},{10,12},{12... | collective-permute-start | bytes 589832 | tf_op jit(solution)/shard_map/ppermute | solution.py:210
  54.5 8.4 %collective-permute-start.21 = (bf16[192,512]{1,0:T(8,128)(2,1)S(1)}, bf16[192,512]{1,0:T(8,128)(2,1)S(1)}, u32[]{:S(2)}, u32[]{:S(2)}) collective-permute-start(bf16[192,512]{1,0:T(8,128)(2,1)S(1)} %collective-permute-done.20.refs_0_), channel_id=1, source_target_pairs={{0,1},{2,0},{4,2},{6,4},{7,6},{5,7},{3,5},{1,3},{8,9},{10,8},{12,1... | collective-permute-start | bytes 589832 | tf_op jit(solution)/shard_map/ppermute | solution.py:210
  56.4 7.9 %collective-permute-start.23 = (bf16[192,512]{1,0:T(8,128)(2,1)S(1)}, bf16[192,512]{1,0:T(8,128)(2,1)S(1)}, u32[]{:S(2)}, u32[]{:S(2)}) collective-permute-start(bf16[192,512]{1,0:T(8,128)(2,1)S(1)} %get-tuple-element.98), channel_id=1, source_target_pairs={{0,2},{2,4},{4,6},{6,7},{7,5},{5,3},{3,1},{1,0},{8,10},{10,12},{12... | collective-permute-start | bytes 589832 | tf_op jit(solution)/shard_map/ppermute | solution.py:210
  58.7 7.2 %collective-permute-start.24 = (bf16[192,512]{1,0:T(8,128)(2,1)S(1)}, bf16[192,512]{1,0:T(8,128)(2,1)S(1)}, u32[]{:S(2)}, u32[]{:S(2)}) collective-permute-start(bf16[192,512]{1,0:T(8,128)(2,1)S(1)} %collective-permute-done.15.refs_0_), channel_id=1, source_target_pairs={{0,1},{2,0},{4,2},{6,4},{7,6},{5,7},{3,5},{1,3},{8,9},{10,8},{12,1... | collective-permute-start | bytes 589832 | tf_op jit(solution)/shard_map/ppermute | solution.py:210
  60.2 6.6 %collective-permute-start.25 = (bf16[192,512]{1,0:T(8,128)(2,1)S(1)}, bf16[192,512]{1,0:T(8,128)(2,1)S(1)}, u32[]{:S(2)}, u32[]{:S(2)}) collective-permute-start(bf16[192,512]{1,0:T(8,128)(2,1)S(1)} %collective-permute-done.19.refs_1_), channel_id=1, source_target_pairs={{0,2},{2,4},{4,6},{6,7},{7,5},{5,3},{3,1},{1,0},{8,10},{10,12},{12... | collective-permute-start | bytes 589832 | tf_op jit(solution)/shard_map/ppermute | solution.py:210
  62.9 6.1 %collective-permute-start.27 = (bf16[192,512]{1,0:T(8,128)(2,1)S(1)}, bf16[192,512]{1,0:T(8,128)(2,1)S(1)}, u32[]{:S(2)}, u32[]{:S(2)}) collective-permute-start(bf16[192,512]{1,0:T(8,128)(2,1)S(1)} %collective-permute-done.21.refs_2_), channel_id=1, source_target_pairs={{0,1},{2,0},{4,2},{6,4},{7,6},{5,7},{3,5},{1,3},{8,9},{10,8},{12,1... | collective-permute-start | bytes 589832 | tf_op jit(solution)/shard_map/ppermute | solution.py:210
  64.4 5.7 %collective-permute-start.26 = (bf16[192,512]{1,0:T(8,128)(2,1)S(1)}, bf16[192,512]{1,0:T(8,128)(2,1)S(1)}, u32[]{:S(2)}, u32[]{:S(2)}) collective-permute-start(bf16[192,512]{1,0:T(8,128)(2,1)S(1)} %collective-permute-done.23.refs_3_), channel_id=1, source_target_pairs={{0,2},{2,4},{4,6},{6,7},{7,5},{5,3},{3,1},{1,0},{8,10},{10,12},{12... | collective-permute-start | bytes 589832 | tf_op jit(solution)/shard_map/ppermute | solution.py:210

commit v4 on v2

--- a/solution.py
+++ b/solution.py
@@ -151,6 +151,7 @@
         inverse = 1.0 / scale
     else:
         rest[1][...] = squares
+    copies = []
     for c in range(0, columns, 256):
         wide = min(256, columns - c)
         acc = None if first else total_in[:, c : c + wide]
@@ -158,17 +159,25 @@
             more = jnp.dot(x, w_ref[pl.ds(row, sub), c : c + wide], preferred_element_type=f32)
             acc = more if acc is None else acc + more
         if last:
-            rest[0][:, c : c + wide] = (acc * inverse).astype(bf16)
+            out, ready, sems = rest
+            ready[:, c : c + wide] = (acc * inverse).astype(bf16)
+            tile = ready.at[:, pl.ds(c, wide)]
+            copies.append(pltpu.make_async_copy(tile, out.at[:, pl.ds(c, wide)], sems.at[len(copies)]))
+            copies[-1].start()
         else:
             rest[0][:, c : c + wide] = acc
+    for copy in copies:
+        copy.wait()
 
 
 def qkv_step(n, parts, xs, gain, weight, state, last=False, hand_on=False, joins=False):
     rows, sub = xs[0].shape
     columns = weight.shape[1]
     vmem = pl.BlockSpec(memory_space=pltpu.VMEM)
+    scratch = []
     if last:
         out_shape = [jax.ShapeDtypeStruct((rows, columns), bf16)]
+        scratch = [pltpu.VMEM((rows, columns), bf16), pltpu.SemaphoreType.DMA((pl.cdiv(columns, 256),))]
     else:
         out_shape = [pltpu.VMEM((rows, columns), f32), pltpu.VMEM((rows, 128), f32)]
     aliases = {}
@@ -182,7 +191,8 @@
         functools.partial(qkv_kernel, n, parts, not state, last, joins, float(weight.shape[0])),
         out_shape=out_shape,
         in_specs=[vmem] * len(operands),
-        out_specs=[vmem] * len(out_shape),
+        out_specs=[pl.BlockSpec(memory_space=pltpu.HBM)] if last else [vmem] * len(out_shape),
+        scratch_shapes=scratch,
         input_output_aliases=aliases,
         compiler_params=pltpu.CompilerParams(vmem_limit_bytes=16 * MIB),
         cost_estimate=pl.CostEstimate(

time: 71.2 us -> 71.1 us (level)
  no operation moved by 1% of the time
where the time goes in v4:
time: 71.1 us; the launch traced here: 71 us
  starting transfers between devices  30.3 us (43%)
  Pallas kernels  22.8 us (32%)
  waiting for transfers between devices  17.1 us (24%)
  between operations  0.82 us (1%)
    ppermute x28, starting transfers between devices, send(): return lax.ppermute(x, 'tensor', pairs)  30.3 us
    ppermute x28, waiting for transfers between devices, send(): return lax.ppermute(x, 'tensor', pairs)  17.1 us
    pallas_call x5, Pallas kernels, down(): pl.pallas_call(functools.partial(down_kernel, n, parts), out_shape=out_sh...  17 us
    pallas_call x7, Pallas kernels, qkv_step(): pl.pallas_call(functools.partial(qkv_kernel, n, parts, not state, last, j...  5.13 us
  transfers between devices with their start and end apart: 28, of which 11 were waited for; matrix products, arithmetic and copies ran while one was open for 0% of the time, Pallas kernels for 27%

profile of v4, /device:TPU:0, one launch (start us, length us, event | category | flops | bytes accessed | tf_op | source)
XLA Modules:
  0.0 71.0 jit_solution(2464060254677596383)
XLA Ops:
  0.6 2.8 %shard_map.68 = (bf16[192,512]{1,0:T(8,128)(2,1)S(1)}, bf16[192,512]{1,0:T(8,128)(2,1)S(1)}, bf16[192,1792]{1,0:T(8,128)(2,1)S(1)}) custom-call(bf16[192,1792]{1,0:T(8,128)(2,1)} %x_ref.1, bf16[1792,8192]{1,0:T(8,128)(2,1)} %w_ref.9), custom_call_target="tpu_custom_call" | custom-call | flops 704643072 | bytes 3670016 | tf_op jit(solution)/shard_map/pallas_call | solution.py:78
  3.4 3.0 %collective-permute-start.1 = (bf16[192,512]{1,0:T(8,128)(2,1)S(1)}, bf16[192,512]{1,0:T(8,128)(2,1)S(1)}, u32[]{:S(2)}, u32[]{:S(2)}) collective-permute-start(bf16[192,512]{1,0:T(8,128)(2,1)S(1)} %get-tuple-element.59), channel_id=1, source_target_pairs={{0,1},{2,0},{4,2},{6,4},{7,6},{5,7},{3,5},{1,3},{8,9},{10,8},{12,1... | collective-permute-start | bytes 589832 | tf_op jit(solution)/shard_map/ppermute | solution.py:220
  6.6 3.7 %shard_map.69 = (bf16[192,512]{1,0:T(8,128)(2,1)S(1)}, bf16[192,512]{1,0:T(8,128)(2,1)S(1)}, bf16[192,512]{1,0:T(8,128)(2,1)S(1)}, bf16[192,512]{1,0:T(8,128)(2,1)S(1)}) custom-call(bf16[192,1792]{1,0:T(8,128)(2,1)S(1)} %get-tuple-element.55.x_ref.hidden_ref, bf16[1792,8192]{1,0:T(8,128)(2,1)} %w_ref.9), custom_call_target="tpu_custom_call" | custom-call | flops 1409286144 | bytes 7340032 | tf_op jit(solution)/shard_map/pallas_call | solution.py:78
  10.3 2.0 %collective-permute-start.5 = (bf16[192,512]{1,0:T(8,128)(2,1)S(1)}, bf16[192,512]{1,0:T(8,128)(2,1)S(1)}, u32[]{:S(2)}, u32[]{:S(2)}) collective-permute-start(bf16[192,512]{1,0:T(8,128)(2,1)S(1)} %get-tuple-element.69), channel_id=1, source_target_pairs={{0,1},{2,0},{4,2},{6,4},{7,6},{5,7},{3,5},{1,3},{8,9},{10,8},{12,1... | collective-permute-start | bytes 589832 | tf_op jit(solution)/shard_map/ppermute | solution.py:220
  12.5 2.0 %collective-permute-start.3 = (bf16[192,512]{1,0:T(8,128)(2,1)S(1)}, bf16[192,512]{1,0:T(8,128)(2,1)S(1)}, u32[]{:S(2)}, u32[]{:S(2)}) collective-permute-start(bf16[192,512]{1,0:T(8,128)(2,1)S(1)} %get-tuple-element.65), channel_id=1, source_target_pairs={{0,1},{2,0},{4,2},{6,4},{7,6},{5,7},{3,5},{1,3},{8,9},{10,8},{12,1... | collective-permute-start | bytes 589832 | tf_op jit(solution)/shard_map/ppermute | solution.py:220
  14.7 3.7 %shard_map.72 = (bf16[192,512]{1,0:T(8,128)(2,1)S(1)}, bf16[192,512]{1,0:T(8,128)(2,1)S(1)}, bf16[192,512]{1,0:T(8,128)(2,1)S(1)}, bf16[192,512]{1,0:T(8,128)(2,1)S(1)}) custom-call(bf16[192,1792]{1,0:T(8,128)(2,1)S(1)} %get-tuple-element.61.x_ref.hidden_ref, bf16[1792,8192]{1,0:T(8,128)(2,1)} %w_ref.9), custom_call_target="tpu_custom_call" | custom-call | flops 1409286144 | bytes 7340032 | tf_op jit(solution)/shard_map/pallas_call | solution.py:78
  18.5 1.9 %collective-permute-start.9 = (bf16[192,512]{1,0:T(8,128)(2,1)S(1)}, bf16[192,512]{1,0:T(8,128)(2,1)S(1)}, u32[]{:S(2)}, u32[]{:S(2)}) collective-permute-start(bf16[192,512]{1,0:T(8,128)(2,1)S(1)} %get-tuple-element.81), channel_id=1, source_target_pairs={{0,1},{2,0},{4,2},{6,4},{7,6},{5,7},{3,5},{1,3},{8,9},{10,8},{12,1... | collective-permute-start | bytes 589832 | tf_op jit(solution)/shard_map/ppermute | solution.py:220
  20.5 0.2 collective-permute-start.8
  20.7 1.6 %collective-permute-done.3.x_ref = bf16[192,512]{1,0:T(8,128)(2,1)S(1)} collective-permute-done((bf16[192,512]{1,0:T(8,128)(2,1)S(1)}, bf16[192,512]{1,0:T(8,128)(2,1)S(1)}, u32[]{:S(2)}, u32[]{:S(2)}) %collective-permute-start.3) | collective-permute-done | bytes 196640 | tf_op jit(solution)/shard_map/ppermute | solution.py:220
  22.4 1.7 %collective-permute-start.7 = (bf16[192,512]{1,0:T(8,128)(2,1)S(1)}, bf16[192,512]{1,0:T(8,128)(2,1)S(1)}, u32[]{:S(2)}, u32[]{:S(2)}) collective-permute-start(bf16[192,512]{1,0:T(8,128)(2,1)S(1)} %get-tuple-element.77), channel_id=1, source_target_pairs={{0,1},{2,0},{4,2},{6,4},{7,6},{5,7},{3,5},{1,3},{8,9},{10,8},{12,1... | collective-permute-start | bytes 589832 | tf_op jit(solution)/shard_map/ppermute | solution.py:220
  24.1 0.5 collective-permute-start.6
  24.6 3.9 %shard_map.77 = (bf16[192,512]{1,0:T(8,128)(2,1)S(1)}, bf16[192,512]{1,0:T(8,128)(2,1)S(1)}, bf16[192,512]{1,0:T(8,128)(2,1)S(1)}, bf16[192,512]{1,0:T(8,128)(2,1)S(1)}) custom-call(bf16[192,1792]{1,0:T(8,128)(2,1)S(1)} %get-tuple-element.73.x_ref.hidden_ref, bf16[1792,8192]{1,0:T(8,128)(2,1)} %w_ref.9), custom_call_target="tpu_custom_call" | custom-call | flops 1409286144 | bytes 7340032 | tf_op jit(solution)/shard_map/pallas_call | solution.py:78
  28.6 1.7 %collective-permute-start.11 = (bf16[192,512]{1,0:T(8,128)(2,1)S(1)}, bf16[192,512]{1,0:T(8,128)(2,1)S(1)}, u32[]{:S(2)}, u32[]{:S(2)}) collective-permute-start(bf16[192,512]{1,0:T(8,128)(2,1)S(1)} %get-tuple-element.88), channel_id=1, source_target_pairs={{0,1},{2,0},{4,2},{6,4},{7,6},{5,7},{3,5},{1,3},{8,9},{10,8},{12,1... | collective-permute-start | bytes 589832 | tf_op jit(solution)/shard_map/ppermute | solution.py:220
  30.3 0.5 collective-permute-start.12
  30.8 1.8 %collective-permute-start.13 = (bf16[192,512]{1,0:T(8,128)(2,1)S(1)}, bf16[192,512]{1,0:T(8,128)(2,1)S(1)}, u32[]{:S(2)}, u32[]{:S(2)}) collective-permute-start(bf16[192,512]{1,0:T(8,128)(2,1)S(1)} %get-tuple-element.91), channel_id=1, source_target_pairs={{0,1},{2,0},{4,2},{6,4},{7,6},{5,7},{3,5},{1,3},{8,9},{10,8},{12,1... | collective-permute-start | bytes 589832 | tf_op jit(solution)/shard_map/ppermute | solution.py:220
  32.6 0.3 collective-permute-start.10
  33.0 2.7 %shard_map.82 = (bf16[192,512]{1,0:T(8,128)(2,1)S(1)}, bf16[192,512]{1,0:T(8,128)(2,1)S(1)}) custom-call(bf16[192,1792]{1,0:T(8,128)(2,1)S(1)} %get-tuple-element.85.x_ref, bf16[1792,8192]{1,0:T(8,128)(2,1)} %w_ref.9), custom_call_target="tpu_custom_call" | custom-call | flops 704643072 | bytes 3670016 | tf_op jit(solution)/shard_map/pallas_call | solution.py:78
  35.7 1.3 %collective-permute-done.12.x_ref = bf16[192,512]{1,0:T(8,128)(2,1)S(1)} collective-permute-done((bf16[192,512]{1,0:T(8,128)(2,1)S(1)}, bf16[192,512]{1,0:T(8,128)(2,1)S(1)}, u32[]{:S(2)}, u32[]{:S(2)}) %collective-permute-start.12) | collective-permute-done | bytes 196640 | tf_op jit(solution)/shard_map/ppermute | solution.py:220
  37.1 0.8 %collective-permute-done.13.y_ref = bf16[192,512]{1,0:T(8,128)(2,1)S(1)} collective-permute-done((bf16[192,512]{1,0:T(8,128)(2,1)S(1)}, bf16[192,512]{1,0:T(8,128)(2,1)S(1)}, u32[]{:S(2)}, u32[]{:S(2)}) %collective-permute-start.13) | collective-permute-done | bytes 196640 | tf_op jit(solution)/shard_map/ppermute | solution.py:220
  37.9 1.7 %collective-permute-start.17 = (bf16[192,512]{1,0:T(8,128)(2,1)S(1)}, bf16[192,512]{1,0:T(8,128)(2,1)S(1)}, u32[]{:S(2)}, u32[]{:S(2)}) collective-permute-start(bf16[192,512]{1,0:T(8,128)(2,1)S(1)} %shard_map.84.refs_1_), channel_id=1, source_target_pairs={{0,1},{2,0},{4,2},{6,4},{7,6},{5,7},{3,5},{1,3},{8,9},{10,8},{12,1... | collective-permute-start | bytes 589832 | tf_op jit(solution)/shard_map/ppermute | solution.py:220
  39.7 0.5 collective-permute-start.18
  40.2 1.6 %collective-permute-start.14 = (bf16[192,512]{1,0:T(8,128)(2,1)S(1)}, bf16[192,512]{1,0:T(8,128)(2,1)S(1)}, u32[]{:S(2)}, u32[]{:S(2)}) collective-permute-start(bf16[192,512]{1,0:T(8,128)(2,1)S(1)} %shard_map.83.refs_0_), channel_id=1, source_target_pairs={{0,1},{2,0},{4,2},{6,4},{7,6},{5,7},{3,5},{1,3},{8,9},{10,8},{12,1... | collective-permute-start | bytes 589832 | tf_op jit(solution)/shard_map/ppermute | solution.py:220
  41.8 0.4 collective-permute-start.16
  42.2 3.6 %collective-permute-done.17.refs_0_ = bf16[192,512]{1,0:T(8,128)(2,1)S(1)} collective-permute-done((bf16[192,512]{1,0:T(8,128)(2,1)S(1)}, bf16[192,512]{1,0:T(8,128)(2,1)S(1)}, u32[]{:S(2)}, u32[]{:S(2)}) %collective-permute-start.17) | collective-permute-done | bytes 196640 | tf_op jit(solution)/shard_map/ppermute | solution.py:220
  45.8 1.6 %collective-permute-start.20 = (bf16[192,512]{1,0:T(8,128)(2,1)S(1)}, bf16[192,512]{1,0:T(8,128)(2,1)S(1)}, u32[]{:S(2)}, u32[]{:S(2)}) collective-permute-start(bf16[192,512]{1,0:T(8,128)(2,1)S(1)} %collective-permute-done.17.refs_0_), channel_id=1, source_target_pairs={{0,1},{2,0},{4,2},{6,4},{7,6},{5,7},{3,5},{1,3},{8,9},{10,8},{12,1... | collective-permute-start | bytes 589832 | tf_op jit(solution)/shard_map/ppermute | solution.py:220
  47.5 0.5 shard_map.85
  48.0 0.5 collective-permute-start.22
  48.5 1.6 %collective-permute-done.14.refs_0_ = bf16[192,512]{1,0:T(8,128)(2,1)S(1)} collective-permute-done((bf16[192,512]{1,0:T(8,128)(2,1)S(1)}, bf16[192,512]{1,0:T(8,128)(2,1)S(1)}, u32[]{:S(2)}, u32[]{:S(2)}) %collective-permute-start.14) | collective-permute-done | bytes 196640 | tf_op jit(solution)/shard_map/ppermute | solution.py:220
  50.0 1.6 %collective-permute-start.15 = (bf16[192,512]{1,0:T(8,128)(2,1)S(1)}, bf16[192,512]{1,0:T(8,128)(2,1)S(1)}, u32[]{:S(2)}, u32[]{:S(2)}) collective-permute-start(bf16[192,512]{1,0:T(8,128)(2,1)S(1)} %collective-permute-done.14.refs_0_), channel_id=1, source_target_pairs={{0,1},{2,0},{4,2},{6,4},{7,6},{5,7},{3,5},{1,3},{8,9},{10,8},{12,1... | collective-permute-start | bytes 589832 | tf_op jit(solution)/shard_map/ppermute | solution.py:220
  51.7 0.5 shard_map.86
  52.2 0.5 collective-permute-start.19
  52.6 1.6 %collective-permute-done.20.refs_0_ = bf16[192,512]{1,0:T(8,128)(2,1)S(1)} collective-permute-done((bf16[192,512]{1,0:T(8,128)(2,1)S(1)}, bf16[192,512]{1,0:T(8,128)(2,1)S(1)}, u32[]{:S(2)}, u32[]{:S(2)}) %collective-permute-start.20) | collective-permute-done | bytes 196640 | tf_op jit(solution)/shard_map/ppermute | solution.py:220
  54.3 1.6 %collective-permute-start.21 = (bf16[192,512]{1,0:T(8,128)(2,1)S(1)}, bf16[192,512]{1,0:T(8,128)(2,1)S(1)}, u32[]{:S(2)}, u32[]{:S(2)}) collective-permute-start(bf16[192,512]{1,0:T(8,128)(2,1)S(1)} %collective-permute-done.20.refs_0_), channel_id=1, source_target_pairs={{0,1},{2,0},{4,2},{6,4},{7,6},{5,7},{3,5},{1,3},{8,9},{10,8},{12,1... | collective-permute-start | bytes 589832 | tf_op jit(solution)/shard_map/ppermute | solution.py:220
  55.9 0.5 shard_map.87
  56.4 0.5 collective-permute-start.23
  56.9 1.6 %collective-permute-done.15.refs_0_ = bf16[192,512]{1,0:T(8,128)(2,1)S(1)} collective-permute-done((bf16[192,512]{1,0:T(8,128)(2,1)S(1)}, bf16[192,512]{1,0:T(8,128)(2,1)S(1)}, u32[]{:S(2)}, u32[]{:S(2)}) %collective-permute-start.15) | collective-permute-done | bytes 196640 | tf_op jit(solution)/shard_map/ppermute | solution.py:220
  58.5 1.6 %collective-permute-start.24 = (bf16[192,512]{1,0:T(8,128)(2,1)S(1)}, bf16[192,512]{1,0:T(8,128)(2,1)S(1)}, u32[]{:S(2)}, u32[]{:S(2)}) collective-permute-start(bf16[192,512]{1,0:T(8,128)(2,1)S(1)} %collective-permute-done.15.refs_0_), channel_id=1, source_target_pairs={{0,1},{2,0},{4,2},{6,4},{7,6},{5,7},{3,5},{1,3},{8,9},{10,8},{12,1... | collective-permute-start | bytes 589832 | tf_op jit(solution)/shard_map/ppermute | solution.py:220
  60.1 0.4 collective-permute-start.25
  60.5 2.2 %collective-permute-done.21.refs_2_ = bf16[192,512]{1,0:T(8,128)(2,1)S(1)} collective-permute-done((bf16[192,512]{1,0:T(8,128)(2,1)S(1)}, bf16[192,512]{1,0:T(8,128)(2,1)S(1)}, u32[]{:S(2)}, u32[]{:S(2)}) %collective-permute-start.21) | collective-permute-done | bytes 196640 | tf_op jit(solution)/shard_map/ppermute | solution.py:220
  62.7 1.6 %collective-permute-start.27 = (bf16[192,512]{1,0:T(8,128)(2,1)S(1)}, bf16[192,512]{1,0:T(8,128)(2,1)S(1)}, u32[]{:S(2)}, u32[]{:S(2)}) collective-permute-start(bf16[192,512]{1,0:T(8,128)(2,1)S(1)} %collective-permute-done.21.refs_2_), channel_id=1, source_target_pairs={{0,1},{2,0},{4,2},{6,4},{7,6},{5,7},{3,5},{1,3},{8,9},{10,8},{12,1... | collective-permute-start | bytes 589832 | tf_op jit(solution)/shard_map/ppermute | solution.py:220
  64.3 0.4 collective-permute-start.26
  64.7 0.5 collective-permute-done.24.refs_4_
  65.2 1.5 %collective-permute-done.25.refs_5_ = bf16[192,512]{1,0:T(8,128)(2,1)S(1)} collective-permute-done((bf16[192,512]{1,0:T(8,128)(2,1)S(1)}, bf16[192,512]{1,0:T(8,128)(2,1)S(1)}, u32[]{:S(2)}, u32[]{:S(2)}) %collective-permute-start.25) | collective-permute-done | bytes 196640 | tf_op jit(solution)/shard_map/ppermute | solution.py:220
  66.7 1.1 %shard_map.88 = (f32[192,640]{1,0:T(8,128)S(1)}, f32[192,128]{1,0:T(8,128)S(1)}) custom-call(bf16[192,512]{1,0:T(8,128)(2,1)S(1)} %collective-permute-done.15.refs_0_, bf16[192,512]{1,0:T(8,128)(2,1)S(1)} %collective-permute-done.19.refs_1_, bf16[192,512]{1,0:T(8,128)(2,1)S(1)} %collective-permute-done.21.refs_2_, ...), custom_call_target="tpu_custom_call" | custom-call | flops 754974720 | bytes 3932160 | tf_op jit(solution)/shard_map/pallas_call | solution.py:190
  67.8 1.2 %shard_map.89 = (f32[192,640]{1,0:T(8,128)S(1)}, f32[192,128]{1,0:T(8,128)S(1)}, bf16[192,1024]{1,0:T(8,128)(2,1)}) custom-call(bf16[192,512]{1,0:T(8,128)(2,1)S(1)} %shard_map.83.refs_0_, bf16[192,512]{1,0:T(8,128)(2,1)S(1)} %shard_map.84.refs_1_, f32[1,8192]{1,0:T(1,128)S(1)} %bitcast.7, bf16[8192,640]{1,0:T(8,128)(2,1)S(1)} %bitcast.2, ...), custom_call_target="tpu_custom_call" | custom-call | flops 251658240 | bytes 1310720 | tf_op jit(solution)/shard_map/pallas_call | solution.py:190
  69.1 0.3 shard_map.90
  69.4 0.6 collective-permute-done.26.refs_0_
  70.0 1.0 %shard_map.91 = bf16[192,640]{1,0:T(8,128)(2,1)} custom-call(bf16[192,512]{1,0:T(8,128)(2,1)S(1)} %collective-permute-done.26.refs_0_, f32[1,8192]{1,0:T(1,128)S(1)} %bitcast.9, bf16[8192,640]{1,0:T(8,128)(2,1)S(1)} %bitcast.2, f32[192,640]{1,0:T(8,128)S(1)} %get-tuple-element.106.refs_3_, f32[192,128]{1,0:T(8,128)S(1)} %get-tuple-element.107.refs_4_), custom_call_target="tpu_custom_call" | custom-call | flops 125829120 | bytes 655360 | tf_op jit(solution)/shard_map/pallas_call | solution.py:190
  (43 shorter events, 1.2 us)
Async XLA Ops:
  3.4 9.0 %collective-permute-start.1 = (bf16[192,512]{1,0:T(8,128)(2,1)S(1)}, bf16[192,512]{1,0:T(8,128)(2,1)S(1)}, u32[]{:S(2)}, u32[]{:S(2)}) collective-permute-start(bf16[192,512]{1,0:T(8,128)(2,1)S(1)} %get-tuple-element.59), channel_id=1, source_target_pairs={{0,1},{2,0},{4,2},{6,4},{7,6},{5,7},{3,5},{1,3},{8,9},{10,8},{12,1... | collective-permute-start | bytes 589832 | tf_op jit(solution)/shard_map/ppermute | solution.py:220
  6.5 8.0 %collective-permute-start = (bf16[192,512]{1,0:T(8,128)(2,1)S(1)}, bf16[192,512]{1,0:T(8,128)(2,1)S(1)}, u32[]{:S(2)}, u32[]{:S(2)}) collective-permute-start(bf16[192,512]{1,0:T(8,128)(2,1)S(1)} %get-tuple-element.57), channel_id=1, source_target_pairs={{0,2},{2,4},{4,6},{6,7},{7,5},{5,3},{3,1},{1,0},{8,10},{10,12},{12... | collective-permute-start | bytes 589832 | tf_op jit(solution)/shard_map/ppermute | solution.py:220
  10.3 8.1 %collective-permute-start.5 = (bf16[192,512]{1,0:T(8,128)(2,1)S(1)}, bf16[192,512]{1,0:T(8,128)(2,1)S(1)}, u32[]{:S(2)}, u32[]{:S(2)}) collective-permute-start(bf16[192,512]{1,0:T(8,128)(2,1)S(1)} %get-tuple-element.69), channel_id=1, source_target_pairs={{0,1},{2,0},{4,2},{6,4},{7,6},{5,7},{3,5},{1,3},{8,9},{10,8},{12,1... | collective-permute-start | bytes 589832 | tf_op jit(solution)/shard_map/ppermute | solution.py:220
  12.3 8.1 %collective-permute-start.4 = (bf16[192,512]{1,0:T(8,128)(2,1)S(1)}, bf16[192,512]{1,0:T(8,128)(2,1)S(1)}, u32[]{:S(2)}, u32[]{:S(2)}) collective-permute-start(bf16[192,512]{1,0:T(8,128)(2,1)S(1)} %get-tuple-element.67), channel_id=1, source_target_pairs={{0,2},{2,4},{4,6},{6,7},{7,5},{5,3},{3,1},{1,0},{8,10},{10,12},{12... | collective-permute-start | bytes 589832 | tf_op jit(solution)/shard_map/ppermute | solution.py:220
  12.5 9.8 %collective-permute-start.3 = (bf16[192,512]{1,0:T(8,128)(2,1)S(1)}, bf16[192,512]{1,0:T(8,128)(2,1)S(1)}, u32[]{:S(2)}, u32[]{:S(2)}) collective-permute-start(bf16[192,512]{1,0:T(8,128)(2,1)S(1)} %get-tuple-element.65), channel_id=1, source_target_pairs={{0,1},{2,0},{4,2},{6,4},{7,6},{5,7},{3,5},{1,3},{8,9},{10,8},{12,1... | collective-permute-start | bytes 589832 | tf_op jit(solution)/shard_map/ppermute | solution.py:220
  14.5 9.6 %collective-permute-start.2 = (bf16[192,512]{1,0:T(8,128)(2,1)S(1)}, bf16[192,512]{1,0:T(8,128)(2,1)S(1)}, u32[]{:S(2)}, u32[]{:S(2)}) collective-permute-start(bf16[192,512]{1,0:T(8,128)(2,1)S(1)} %get-tuple-element.63), channel_id=1, source_target_pairs={{0,2},{2,4},{4,6},{6,7},{7,5},{5,3},{3,1},{1,0},{8,10},{10,12},{12... | collective-permute-start | bytes 589832 | tf_op jit(solution)/shard_map/ppermute | solution.py:220
  18.5 10.0 %collective-permute-start.9 = (bf16[192,512]{1,0:T(8,128)(2,1)S(1)}, bf16[192,512]{1,0:T(8,128)(2,1)S(1)}, u32[]{:S(2)}, u32[]{:S(2)}) collective-permute-start(bf16[192,512]{1,0:T(8,128)(2,1)S(1)} %get-tuple-element.81), channel_id=1, source_target_pairs={{0,1},{2,0},{4,2},{6,4},{7,6},{5,7},{3,5},{1,3},{8,9},{10,8},{12,1... | collective-permute-start | bytes 589832 | tf_op jit(solution)/shard_map/ppermute | solution.py:220
  20.5 9.7 %collective-permute-start.8 = (bf16[192,512]{1,0:T(8,128)(2,1)S(1)}, bf16[192,512]{1,0:T(8,128)(2,1)S(1)}, u32[]{:S(2)}, u32[]{:S(2)}) collective-permute-start(bf16[192,512]{1,0:T(8,128)(2,1)S(1)} %get-tuple-element.79), channel_id=1, source_target_pairs={{0,2},{2,4},{4,6},{6,7},{7,5},{5,3},{3,1},{1,0},{8,10},{10,12},{12... | collective-permute-start | bytes 589832 | tf_op jit(solution)/shard_map/ppermute | solution.py:220
  22.4 8.4 %collective-permute-start.7 = (bf16[192,512]{1,0:T(8,128)(2,1)S(1)}, bf16[192,512]{1,0:T(8,128)(2,1)S(1)}, u32[]{:S(2)}, u32[]{:S(2)}) collective-permute-start(bf16[192,512]{1,0:T(8,128)(2,1)S(1)} %get-tuple-element.77), channel_id=1, source_target_pairs={{0,1},{2,0},{4,2},{6,4},{7,6},{5,7},{3,5},{1,3},{8,9},{10,8},{12,1... | collective-permute-start | bytes 589832 | tf_op jit(solution)/shard_map/ppermute | solution.py:220
  24.1 8.5 %collective-permute-start.6 = (bf16[192,512]{1,0:T(8,128)(2,1)S(1)}, bf16[192,512]{1,0:T(8,128)(2,1)S(1)}, u32[]{:S(2)}, u32[]{:S(2)}) collective-permute-start(bf16[192,512]{1,0:T(8,128)(2,1)S(1)} %get-tuple-element.75), channel_id=1, source_target_pairs={{0,2},{2,4},{4,6},{6,7},{7,5},{5,3},{3,1},{1,0},{8,10},{10,12},{12... | collective-permute-start | bytes 589832 | tf_op jit(solution)/shard_map/ppermute | solution.py:220
  24.5 13.3 %copy-start.1 = (bf16[192,1024]{1,0:T(8,128)(2,1)S(1)}, bf16[192,1024]{1,0:T(8,128)(2,1)}, u32[]{:S(2)}) copy-start(bf16[192,1024]{1,0:T(8,128)(2,1)} %residual_ref.3) | copy-start | bytes 1179652
  24.6 22.9 %slice-start = ((s8[10485760]{0:T(1024)(128)(4,1)}), s8[4194304]{0:T(1024)(128)(4,1)S(1)}, s32[]{:S(2)}) async-start(s8[10485760]{0:T(1024)(128)(4,1)} %bitcast.1), calls=%async_computation | async-start | bytes 8388608
  24.6 22.9 %slice-start.1 = ((s8[10485760]{0:T(1024)(128)(4,1)}), s8[4194304]{0:T(1024)(128)(4,1)S(1)}, s32[]{:S(2)}) async-start(s8[10485760]{0:T(1024)(128)(4,1)} %bitcast.1), calls=%async_computation.1 | async-start | bytes 8388608
  24.6 22.9 %copy-start = (f32[8192]{0:T(1024)S(1)}, f32[8192]{0:T(1024)}, u32[]{:S(2)}) copy-start(f32[8192]{0:T(1024)} %param.8) | copy-start | bytes 98308
  28.6 11.0 %collective-permute-start.11 = (bf16[192,512]{1,0:T(8,128)(2,1)S(1)}, bf16[192,512]{1,0:T(8,128)(2,1)S(1)}, u32[]{:S(2)}, u32[]{:S(2)}) collective-permute-start(bf16[192,512]{1,0:T(8,128)(2,1)S(1)} %get-tuple-element.88), channel_id=1, source_target_pairs={{0,1},{2,0},{4,2},{6,4},{7,6},{5,7},{3,5},{1,3},{8,9},{10,8},{12,1... | collective-permute-start | bytes 589832 | tf_op jit(solution)/shard_map/ppermute | solution.py:220
  30.3 6.8 %collective-permute-start.12 = (bf16[192,512]{1,0:T(8,128)(2,1)S(1)}, bf16[192,512]{1,0:T(8,128)(2,1)S(1)}, u32[]{:S(2)}, u32[]{:S(2)}) collective-permute-start(bf16[192,512]{1,0:T(8,128)(2,1)S(1)} %get-tuple-element.90), channel_id=1, source_target_pairs={{0,2},{2,4},{4,6},{6,7},{7,5},{5,3},{3,1},{1,0},{8,10},{10,12},{12... | collective-permute-start | bytes 589832 | tf_op jit(solution)/shard_map/ppermute | solution.py:220
  30.8 7.0 %collective-permute-start.13 = (bf16[192,512]{1,0:T(8,128)(2,1)S(1)}, bf16[192,512]{1,0:T(8,128)(2,1)S(1)}, u32[]{:S(2)}, u32[]{:S(2)}) collective-permute-start(bf16[192,512]{1,0:T(8,128)(2,1)S(1)} %get-tuple-element.91), channel_id=1, source_target_pairs={{0,1},{2,0},{4,2},{6,4},{7,6},{5,7},{3,5},{1,3},{8,9},{10,8},{12,1... | collective-permute-start | bytes 589832 | tf_op jit(solution)/shard_map/ppermute | solution.py:220
  32.6 7.0 %collective-permute-start.10 = (bf16[192,512]{1,0:T(8,128)(2,1)S(1)}, bf16[192,512]{1,0:T(8,128)(2,1)S(1)}, u32[]{:S(2)}, u32[]{:S(2)}) collective-permute-start(bf16[192,512]{1,0:T(8,128)(2,1)S(1)} %get-tuple-element.87), channel_id=1, source_target_pairs={{0,2},{2,4},{4,6},{6,7},{7,5},{5,3},{3,1},{1,0},{8,10},{10,12},{12... | collective-permute-start | bytes 589832 | tf_op jit(solution)/shard_map/ppermute | solution.py:220
  33.0 14.5 %slice-start.2 = ((s8[10485760]{0:T(1024)(128)(4,1)}), s8[2097152]{0:T(1024)(128)(4,1)S(1)}, s32[]{:S(2)}) async-start(s8[10485760]{0:T(1024)(128)(4,1)} %bitcast.1), calls=%async_computation.2 | async-start | bytes 4194304
  37.9 7.9 %collective-permute-start.17 = (bf16[192,512]{1,0:T(8,128)(2,1)S(1)}, bf16[192,512]{1,0:T(8,128)(2,1)S(1)}, u32[]{:S(2)}, u32[]{:S(2)}) collective-permute-start(bf16[192,512]{1,0:T(8,128)(2,1)S(1)} %shard_map.84.refs_1_), channel_id=1, source_target_pairs={{0,1},{2,0},{4,2},{6,4},{7,6},{5,7},{3,5},{1,3},{8,9},{10,8},{12,1... | collective-permute-start | bytes 589832 | tf_op jit(solution)/shard_map/ppermute | solution.py:220
  39.7 7.7 %collective-permute-start.18 = (bf16[192,512]{1,0:T(8,128)(2,1)S(1)}, bf16[192,512]{1,0:T(8,128)(2,1)S(1)}, u32[]{:S(2)}, u32[]{:S(2)}) collective-permute-start(bf16[192,512]{1,0:T(8,128)(2,1)S(1)} %shard_map.83.refs_0_), channel_id=1, source_target_pairs={{0,2},{2,4},{4,6},{6,7},{7,5},{5,3},{3,1},{1,0},{8,10},{10,12},{12... | collective-permute-start | bytes 589832 | tf_op jit(solution)/shard_map/ppermute | solution.py:220
  40.2 9.9 %collective-permute-start.14 = (bf16[192,512]{1,0:T(8,128)(2,1)S(1)}, bf16[192,512]{1,0:T(8,128)(2,1)S(1)}, u32[]{:S(2)}, u32[]{:S(2)}) collective-permute-start(bf16[192,512]{1,0:T(8,128)(2,1)S(1)} %shard_map.83.refs_0_), channel_id=1, source_target_pairs={{0,1},{2,0},{4,2},{6,4},{7,6},{5,7},{3,5},{1,3},{8,9},{10,8},{12,1... | collective-permute-start | bytes 589832 | tf_op jit(solution)/shard_map/ppermute | solution.py:220
  41.8 9.9 %collective-permute-start.16 = (bf16[192,512]{1,0:T(8,128)(2,1)S(1)}, bf16[192,512]{1,0:T(8,128)(2,1)S(1)}, u32[]{:S(2)}, u32[]{:S(2)}) collective-permute-start(bf16[192,512]{1,0:T(8,128)(2,1)S(1)} %shard_map.84.refs_1_), channel_id=1, source_target_pairs={{0,2},{2,4},{4,6},{6,7},{7,5},{5,3},{3,1},{1,0},{8,10},{10,12},{12... | collective-permute-start | bytes 589832 | tf_op jit(solution)/shard_map/ppermute | solution.py:220
  45.8 8.4 %collective-permute-start.20 = (bf16[192,512]{1,0:T(8,128)(2,1)S(1)}, bf16[192,512]{1,0:T(8,128)(2,1)S(1)}, u32[]{:S(2)}, u32[]{:S(2)}) collective-permute-start(bf16[192,512]{1,0:T(8,128)(2,1)S(1)} %collective-permute-done.17.refs_0_), channel_id=1, source_target_pairs={{0,1},{2,0},{4,2},{6,4},{7,6},{5,7},{3,5},{1,3},{8,9},{10,8},{12,1... | collective-permute-start | bytes 589832 | tf_op jit(solution)/shard_map/ppermute | solution.py:220
  48.0 7.9 %collective-permute-start.22 = (bf16[192,512]{1,0:T(8,128)(2,1)S(1)}, bf16[192,512]{1,0:T(8,128)(2,1)S(1)}, u32[]{:S(2)}, u32[]{:S(2)}) collective-permute-start(bf16[192,512]{1,0:T(8,128)(2,1)S(1)} %get-tuple-element.95), channel_id=1, source_target_pairs={{0,2},{2,4},{4,6},{6,7},{7,5},{5,3},{3,1},{1,0},{8,10},{10,12},{12... | collective-permute-start | bytes 589832 | tf_op jit(solution)/shard_map/ppermute | solution.py:220
  50.0 8.4 %collective-permute-start.15 = (bf16[192,512]{1,0:T(8,128)(2,1)S(1)}, bf16[192,512]{1,0:T(8,128)(2,1)S(1)}, u32[]{:S(2)}, u32[]{:S(2)}) collective-permute-start(bf16[192,512]{1,0:T(8,128)(2,1)S(1)} %collective-permute-done.14.refs_0_), channel_id=1, source_target_pairs={{0,1},{2,0},{4,2},{6,4},{7,6},{5,7},{3,5},{1,3},{8,9},{10,8},{12,1... | collective-permute-start | bytes 589832 | tf_op jit(solution)/shard_map/ppermute | solution.py:220
  52.2 7.9 %collective-permute-start.19 = (bf16[192,512]{1,0:T(8,128)(2,1)S(1)}, bf16[192,512]{1,0:T(8,128)(2,1)S(1)}, u32[]{:S(2)}, u32[]{:S(2)}) collective-permute-start(bf16[192,512]{1,0:T(8,128)(2,1)S(1)} %get-tuple-element.94), channel_id=1, source_target_pairs={{0,2},{2,4},{4,6},{6,7},{7,5},{5,3},{3,1},{1,0},{8,10},{10,12},{12... | collective-permute-start | bytes 589832 | tf_op jit(solution)/shard_map/ppermute | solution.py:220
  54.3 8.4 %collective-permute-start.21 = (bf16[192,512]{1,0:T(8,128)(2,1)S(1)}, bf16[192,512]{1,0:T(8,128)(2,1)S(1)}, u32[]{:S(2)}, u32[]{:S(2)}) collective-permute-start(bf16[192,512]{1,0:T(8,128)(2,1)S(1)} %collective-permute-done.20.refs_0_), channel_id=1, source_target_pairs={{0,1},{2,0},{4,2},{6,4},{7,6},{5,7},{3,5},{1,3},{8,9},{10,8},{12,1... | collective-permute-start | bytes 589832 | tf_op jit(solution)/shard_map/ppermute | solution.py:220
  56.4 7.9 %collective-permute-start.23 = (bf16[192,512]{1,0:T(8,128)(2,1)S(1)}, bf16[192,512]{1,0:T(8,128)(2,1)S(1)}, u32[]{:S(2)}, u32[]{:S(2)}) collective-permute-start(bf16[192,512]{1,0:T(8,128)(2,1)S(1)} %get-tuple-element.98), channel_id=1, source_target_pairs={{0,2},{2,4},{4,6},{6,7},{7,5},{5,3},{3,1},{1,0},{8,10},{10,12},{12... | collective-permute-start | bytes 589832 | tf_op jit(solution)/shard_map/ppermute | solution.py:220
  58.5 6.8 %collective-permute-start.24 = (bf16[192,512]{1,0:T(8,128)(2,1)S(1)}, bf16[192,512]{1,0:T(8,128)(2,1)S(1)}, u32[]{:S(2)}, u32[]{:S(2)}) collective-permute-start(bf16[192,512]{1,0:T(8,128)(2,1)S(1)} %collective-permute-done.15.refs_0_), channel_id=1, source_target_pairs={{0,1},{2,0},{4,2},{6,4},{7,6},{5,7},{3,5},{1,3},{8,9},{10,8},{12,1... | collective-permute-start | bytes 589832 | tf_op jit(solution)/shard_map/ppermute | solution.py:220
  60.1 6.6 %collective-permute-start.25 = (bf16[192,512]{1,0:T(8,128)(2,1)S(1)}, bf16[192,512]{1,0:T(8,128)(2,1)S(1)}, u32[]{:S(2)}, u32[]{:S(2)}) collective-permute-start(bf16[192,512]{1,0:T(8,128)(2,1)S(1)} %collective-permute-done.19.refs_1_), channel_id=1, source_target_pairs={{0,2},{2,4},{4,6},{6,7},{7,5},{5,3},{3,1},{1,0},{8,10},{10,12},{12... | collective-permute-start | bytes 589832 | tf_op jit(solution)/shard_map/ppermute | solution.py:220
  62.7 6.4 %collective-permute-start.27 = (bf16[192,512]{1,0:T(8,128)(2,1)S(1)}, bf16[192,512]{1,0:T(8,128)(2,1)S(1)}, u32[]{:S(2)}, u32[]{:S(2)}) collective-permute-start(bf16[192,512]{1,0:T(8,128)(2,1)S(1)} %collective-permute-done.21.refs_2_), channel_id=1, source_target_pairs={{0,1},{2,0},{4,2},{6,4},{7,6},{5,7},{3,5},{1,3},{8,9},{10,8},{12,1... | collective-permute-start | bytes 589832 | tf_op jit(solution)/shard_map/ppermute | solution.py:220
  64.3 5.7 %collective-permute-start.26 = (bf16[192,512]{1,0:T(8,128)(2,1)S(1)}, bf16[192,512]{1,0:T(8,128)(2,1)S(1)}, u32[]{:S(2)}, u32[]{:S(2)}) collective-permute-start(bf16[192,512]{1,0:T(8,128)(2,1)S(1)} %collective-permute-done.23.refs_3_), channel_id=1, source_target_pairs={{0,2},{2,4},{4,6},{6,7},{7,5},{5,3},{3,1},{1,0},{8,10},{10,12},{12... | collective-permute-start | bytes 589832 | tf_op jit(solution)/shard_map/ppermute | solution.py:220

commit v5 on v2

--- a/solution.py
+++ b/solution.py
@@ -233,7 +233,7 @@
             k = step // 2 + 1
             parts += [(k, 1 - step % 2), (-k, step % 2)]
             xs += [y, x]
-            if step in (n - 4, n - 5):
+            if step in (n - 4, n - 5, n - 7):
                 arrived.append((send(x, right), send(y, left)))
             elif step == n - 3:
                 state = qkv_step(n, parts, xs, gain, qkv_weight, state)

time: 71.2 us -> 71.4 us (level)
    pallas_call x7 -> x6, Pallas kernels: 5.16 us -> 4.97 us  [qkv_step(): pl.pallas_call(functools.partial(qkv_kernel, n, parts, not state, last, j...]
  transfers between devices with their start and end apart: 28 -> 28, of which waited for: 11 -> 12; matrix products, arithmetic and copies ran while one was open for 0% -> 0% of each run, Pallas kernels for 27% -> 26%
where the time goes in v5:
time: 71.4 us; the launch traced here: 71.3 us
  starting transfers between devices  30.3 us (42%)
  Pallas kernels  22.6 us (32%)
  waiting for transfers between devices  17.6 us (25%)
  between operations  0.81 us (1%)
    ppermute x28, starting transfers between devices, send(): return lax.ppermute(x, 'tensor', pairs)  30.3 us
    ppermute x28, waiting for transfers between devices, send(): return lax.ppermute(x, 'tensor', pairs)  17.6 us
    pallas_call x5, Pallas kernels, down(): pl.pallas_call(functools.partial(down_kernel, n, parts), out_shape=out_sh...  17 us
    pallas_call x6, Pallas kernels, qkv_step(): pl.pallas_call(functools.partial(qkv_kernel, n, parts, not state, last, j...  4.97 us
  transfers between devices with their start and end apart: 28, of which 12 were waited for; matrix products, arithmetic and copies ran while one was open for 0% of the time, Pallas kernels for 26%

profile of v5, /device:TPU:0, one launch (start us, length us, event | category | flops | bytes accessed | tf_op | source)
XLA Modules:
  0.0 71.3 jit_solution(553996011235022331)
XLA Ops:
  0.6 2.8 %shard_map.68 = (bf16[192,512]{1,0:T(8,128)(2,1)S(1)}, bf16[192,512]{1,0:T(8,128)(2,1)S(1)}, bf16[192,1792]{1,0:T(8,128)(2,1)S(1)}) custom-call(bf16[192,1792]{1,0:T(8,128)(2,1)} %x_ref.1, bf16[1792,8192]{1,0:T(8,128)(2,1)} %w_ref.9), custom_call_target="tpu_custom_call" | custom-call | flops 704643072 | bytes 3670016 | tf_op jit(solution)/shard_map/pallas_call | solution.py:78
  3.4 3.0 %collective-permute-start.1 = (bf16[192,512]{1,0:T(8,128)(2,1)S(1)}, bf16[192,512]{1,0:T(8,128)(2,1)S(1)}, u32[]{:S(2)}, u32[]{:S(2)}) collective-permute-start(bf16[192,512]{1,0:T(8,128)(2,1)S(1)} %get-tuple-element.56), channel_id=1, source_target_pairs={{0,1},{2,0},{4,2},{6,4},{7,6},{5,7},{3,5},{1,3},{8,9},{10,8},{12,1... | collective-permute-start | bytes 589832 | tf_op jit(solution)/shard_map/ppermute | solution.py:210
  6.6 3.7 %shard_map.69 = (bf16[192,512]{1,0:T(8,128)(2,1)S(1)}, bf16[192,512]{1,0:T(8,128)(2,1)S(1)}, bf16[192,512]{1,0:T(8,128)(2,1)S(1)}, bf16[192,512]{1,0:T(8,128)(2,1)S(1)}) custom-call(bf16[192,1792]{1,0:T(8,128)(2,1)S(1)} %get-tuple-element.52.x_ref.hidden_ref, bf16[1792,8192]{1,0:T(8,128)(2,1)} %w_ref.9), custom_call_target="tpu_custom_call" | custom-call | flops 1409286144 | bytes 7340032 | tf_op jit(solution)/shard_map/pallas_call | solution.py:78
  10.3 2.0 %collective-permute-start.5 = (bf16[192,512]{1,0:T(8,128)(2,1)S(1)}, bf16[192,512]{1,0:T(8,128)(2,1)S(1)}, u32[]{:S(2)}, u32[]{:S(2)}) collective-permute-start(bf16[192,512]{1,0:T(8,128)(2,1)S(1)} %get-tuple-element.66), channel_id=1, source_target_pairs={{0,1},{2,0},{4,2},{6,4},{7,6},{5,7},{3,5},{1,3},{8,9},{10,8},{12,1... | collective-permute-start | bytes 589832 | tf_op jit(solution)/shard_map/ppermute | solution.py:210
  12.5 2.0 %collective-permute-start.3 = (bf16[192,512]{1,0:T(8,128)(2,1)S(1)}, bf16[192,512]{1,0:T(8,128)(2,1)S(1)}, u32[]{:S(2)}, u32[]{:S(2)}) collective-permute-start(bf16[192,512]{1,0:T(8,128)(2,1)S(1)} %get-tuple-element.62), channel_id=1, source_target_pairs={{0,1},{2,0},{4,2},{6,4},{7,6},{5,7},{3,5},{1,3},{8,9},{10,8},{12,1... | collective-permute-start | bytes 589832 | tf_op jit(solution)/shard_map/ppermute | solution.py:210
  14.7 3.7 %shard_map.72 = (bf16[192,512]{1,0:T(8,128)(2,1)S(1)}, bf16[192,512]{1,0:T(8,128)(2,1)S(1)}, bf16[192,512]{1,0:T(8,128)(2,1)S(1)}, bf16[192,512]{1,0:T(8,128)(2,1)S(1)}) custom-call(bf16[192,1792]{1,0:T(8,128)(2,1)S(1)} %get-tuple-element.58.x_ref.hidden_ref, bf16[1792,8192]{1,0:T(8,128)(2,1)} %w_ref.9), custom_call_target="tpu_custom_call" | custom-call | flops 1409286144 | bytes 7340032 | tf_op jit(solution)/shard_map/pallas_call | solution.py:78
  18.5 1.9 %collective-permute-start.9 = (bf16[192,512]{1,0:T(8,128)(2,1)S(1)}, bf16[192,512]{1,0:T(8,128)(2,1)S(1)}, u32[]{:S(2)}, u32[]{:S(2)}) collective-permute-start(bf16[192,512]{1,0:T(8,128)(2,1)S(1)} %get-tuple-element.78), channel_id=1, source_target_pairs={{0,1},{2,0},{4,2},{6,4},{7,6},{5,7},{3,5},{1,3},{8,9},{10,8},{12,1... | collective-permute-start | bytes 589832 | tf_op jit(solution)/shard_map/ppermute | solution.py:210
  20.5 0.2 collective-permute-start.8
  20.7 1.6 %collective-permute-done.3.x_ref = bf16[192,512]{1,0:T(8,128)(2,1)S(1)} collective-permute-done((bf16[192,512]{1,0:T(8,128)(2,1)S(1)}, bf16[192,512]{1,0:T(8,128)(2,1)S(1)}, u32[]{:S(2)}, u32[]{:S(2)}) %collective-permute-start.3) | collective-permute-done | bytes 196640 | tf_op jit(solution)/shard_map/ppermute | solution.py:210
  22.4 1.7 %collective-permute-start.7 = (bf16[192,512]{1,0:T(8,128)(2,1)S(1)}, bf16[192,512]{1,0:T(8,128)(2,1)S(1)}, u32[]{:S(2)}, u32[]{:S(2)}) collective-permute-start(bf16[192,512]{1,0:T(8,128)(2,1)S(1)} %get-tuple-element.74), channel_id=1, source_target_pairs={{0,1},{2,0},{4,2},{6,4},{7,6},{5,7},{3,5},{1,3},{8,9},{10,8},{12,1... | collective-permute-start | bytes 589832 | tf_op jit(solution)/shard_map/ppermute | solution.py:210
  24.1 0.5 collective-permute-start.6
  24.6 3.9 %shard_map.77 = (bf16[192,512]{1,0:T(8,128)(2,1)S(1)}, bf16[192,512]{1,0:T(8,128)(2,1)S(1)}, bf16[192,512]{1,0:T(8,128)(2,1)S(1)}, bf16[192,512]{1,0:T(8,128)(2,1)S(1)}) custom-call(bf16[192,1792]{1,0:T(8,128)(2,1)S(1)} %get-tuple-element.70.x_ref.hidden_ref, bf16[1792,8192]{1,0:T(8,128)(2,1)} %w_ref.9), custom_call_target="tpu_custom_call" | custom-call | flops 1409286144 | bytes 7340032 | tf_op jit(solution)/shard_map/pallas_call | solution.py:78
  28.6 1.7 %collective-permute-start.11 = (bf16[192,512]{1,0:T(8,128)(2,1)S(1)}, bf16[192,512]{1,0:T(8,128)(2,1)S(1)}, u32[]{:S(2)}, u32[]{:S(2)}) collective-permute-start(bf16[192,512]{1,0:T(8,128)(2,1)S(1)} %get-tuple-element.85), channel_id=1, source_target_pairs={{0,1},{2,0},{4,2},{6,4},{7,6},{5,7},{3,5},{1,3},{8,9},{10,8},{12,1... | collective-permute-start | bytes 589832 | tf_op jit(solution)/shard_map/ppermute | solution.py:210
  30.3 0.5 collective-permute-start.12
  30.8 1.8 %collective-permute-start.13 = (bf16[192,512]{1,0:T(8,128)(2,1)S(1)}, bf16[192,512]{1,0:T(8,128)(2,1)S(1)}, u32[]{:S(2)}, u32[]{:S(2)}) collective-permute-start(bf16[192,512]{1,0:T(8,128)(2,1)S(1)} %get-tuple-element.88), channel_id=1, source_target_pairs={{0,1},{2,0},{4,2},{6,4},{7,6},{5,7},{3,5},{1,3},{8,9},{10,8},{12,1... | collective-permute-start | bytes 589832 | tf_op jit(solution)/shard_map/ppermute | solution.py:210
  32.6 0.3 collective-permute-start.10
  33.0 2.7 %shard_map.82 = (bf16[192,512]{1,0:T(8,128)(2,1)S(1)}, bf16[192,512]{1,0:T(8,128)(2,1)S(1)}) custom-call(bf16[192,1792]{1,0:T(8,128)(2,1)S(1)} %get-tuple-element.82.x_ref, bf16[1792,8192]{1,0:T(8,128)(2,1)} %w_ref.9), custom_call_target="tpu_custom_call" | custom-call | flops 704643072 | bytes 3670016 | tf_op jit(solution)/shard_map/pallas_call | solution.py:78
  35.7 1.3 %collective-permute-done.12.x_ref = bf16[192,512]{1,0:T(8,128)(2,1)S(1)} collective-permute-done((bf16[192,512]{1,0:T(8,128)(2,1)S(1)}, bf16[192,512]{1,0:T(8,128)(2,1)S(1)}, u32[]{:S(2)}, u32[]{:S(2)}) %collective-permute-start.12) | collective-permute-done | bytes 196640 | tf_op jit(solution)/shard_map/ppermute | solution.py:210
  37.1 0.8 %collective-permute-done.13.y_ref = bf16[192,512]{1,0:T(8,128)(2,1)S(1)} collective-permute-done((bf16[192,512]{1,0:T(8,128)(2,1)S(1)}, bf16[192,512]{1,0:T(8,128)(2,1)S(1)}, u32[]{:S(2)}, u32[]{:S(2)}) %collective-permute-start.13) | collective-permute-done | bytes 196640 | tf_op jit(solution)/shard_map/ppermute | solution.py:210
  37.9 1.7 %collective-permute-start.18 = (bf16[192,512]{1,0:T(8,128)(2,1)S(1)}, bf16[192,512]{1,0:T(8,128)(2,1)S(1)}, u32[]{:S(2)}, u32[]{:S(2)}) collective-permute-start(bf16[192,512]{1,0:T(8,128)(2,1)S(1)} %shard_map.84.refs_1_), channel_id=1, source_target_pairs={{0,1},{2,0},{4,2},{6,4},{7,6},{5,7},{3,5},{1,3},{8,9},{10,8},{12,1... | collective-permute-start | bytes 589832 | tf_op jit(solution)/shard_map/ppermute | solution.py:210
  39.7 0.5 collective-permute-start.21
  40.2 1.6 %collective-permute-start.14 = (bf16[192,512]{1,0:T(8,128)(2,1)S(1)}, bf16[192,512]{1,0:T(8,128)(2,1)S(1)}, u32[]{:S(2)}, u32[]{:S(2)}) collective-permute-start(bf16[192,512]{1,0:T(8,128)(2,1)S(1)} %shard_map.83.refs_0_), channel_id=1, source_target_pairs={{0,1},{2,0},{4,2},{6,4},{7,6},{5,7},{3,5},{1,3},{8,9},{10,8},{12,1... | collective-permute-start | bytes 589832 | tf_op jit(solution)/shard_map/ppermute | solution.py:210
  41.8 0.4 collective-permute-start.16
  42.2 3.6 %collective-permute-done.18.refs_0_ = bf16[192,512]{1,0:T(8,128)(2,1)S(1)} collective-permute-done((bf16[192,512]{1,0:T(8,128)(2,1)S(1)}, bf16[192,512]{1,0:T(8,128)(2,1)S(1)}, u32[]{:S(2)}, u32[]{:S(2)}) %collective-permute-start.18) | collective-permute-done | bytes 196640 | tf_op jit(solution)/shard_map/ppermute | solution.py:210
  45.8 1.6 %collective-permute-start.19 = (bf16[192,512]{1,0:T(8,128)(2,1)S(1)}, bf16[192,512]{1,0:T(8,128)(2,1)S(1)}, u32[]{:S(2)}, u32[]{:S(2)}) collective-permute-start(bf16[192,512]{1,0:T(8,128)(2,1)S(1)} %collective-permute-done.18.refs_0_), channel_id=1, source_target_pairs={{0,1},{2,0},{4,2},{6,4},{7,6},{5,7},{3,5},{1,3},{8,9},{10,8},{12,1... | collective-permute-start | bytes 589832 | tf_op jit(solution)/shard_map/ppermute | solution.py:210
  47.5 0.5 shard_map.85
  48.0 0.5 collective-permute-start.22
  48.5 1.6 %collective-permute-done.14.refs_0_ = bf16[192,512]{1,0:T(8,128)(2,1)S(1)} collective-permute-done((bf16[192,512]{1,0:T(8,128)(2,1)S(1)}, bf16[192,512]{1,0:T(8,128)(2,1)S(1)}, u32[]{:S(2)}, u32[]{:S(2)}) %collective-permute-start.14) | collective-permute-done | bytes 196640 | tf_op jit(solution)/shard_map/ppermute | solution.py:210
  50.0 1.6 %collective-permute-start.15 = (bf16[192,512]{1,0:T(8,128)(2,1)S(1)}, bf16[192,512]{1,0:T(8,128)(2,1)S(1)}, u32[]{:S(2)}, u32[]{:S(2)}) collective-permute-start(bf16[192,512]{1,0:T(8,128)(2,1)S(1)} %collective-permute-done.14.refs_0_), channel_id=1, source_target_pairs={{0,1},{2,0},{4,2},{6,4},{7,6},{5,7},{3,5},{1,3},{8,9},{10,8},{12,1... | collective-permute-start | bytes 589832 | tf_op jit(solution)/shard_map/ppermute | solution.py:210
  51.7 0.4 collective-permute-start.17
  52.1 2.2 %collective-permute-done.19.refs_2_ = bf16[192,512]{1,0:T(8,128)(2,1)S(1)} collective-permute-done((bf16[192,512]{1,0:T(8,128)(2,1)S(1)}, bf16[192,512]{1,0:T(8,128)(2,1)S(1)}, u32[]{:S(2)}, u32[]{:S(2)}) %collective-permute-start.19) | collective-permute-done | bytes 196640 | tf_op jit(solution)/shard_map/ppermute | solution.py:210
  54.3 1.6 %collective-permute-start.20 = (bf16[192,512]{1,0:T(8,128)(2,1)S(1)}, bf16[192,512]{1,0:T(8,128)(2,1)S(1)}, u32[]{:S(2)}, u32[]{:S(2)}) collective-permute-start(bf16[192,512]{1,0:T(8,128)(2,1)S(1)} %collective-permute-done.19.refs_2_), channel_id=1, source_target_pairs={{0,1},{2,0},{4,2},{6,4},{7,6},{5,7},{3,5},{1,3},{8,9},{10,8},{12,1... | collective-permute-start | bytes 589832 | tf_op jit(solution)/shard_map/ppermute | solution.py:210
  55.9 0.8 %shard_map.86 = (f32[192,640]{1,0:T(8,128)S(1)}, f32[192,128]{1,0:T(8,128)S(1)}, bf16[192,512]{1,0:T(8,128)(2,1)S(1)}) custom-call(bf16[192,512]{1,0:T(8,128)(2,1)S(1)} %collective-permute-done.14.refs_0_, bf16[192,512]{1,0:T(8,128)(2,1)S(1)} %collective-permute-done.16.refs_1_, ...), custom_call_target="tpu_custom_call", output_to_operand_aliasing={{2}: (3, {})} | custom-call | flops 503316480 | bytes 2621440 | tf_op jit(solution)/shard_map/pallas_call | solution.py:181
  56.7 0.5 collective-permute-start.23
  57.2 1.3 %collective-permute-done.15.refs_0_ = bf16[192,512]{1,0:T(8,128)(2,1)S(1)} collective-permute-done((bf16[192,512]{1,0:T(8,128)(2,1)S(1)}, bf16[192,512]{1,0:T(8,128)(2,1)S(1)}, u32[]{:S(2)}, u32[]{:S(2)}) %collective-permute-start.15) | collective-permute-done | bytes 196640 | tf_op jit(solution)/shard_map/ppermute | solution.py:210
  58.5 1.6 %collective-permute-start.24 = (bf16[192,512]{1,0:T(8,128)(2,1)S(1)}, bf16[192,512]{1,0:T(8,128)(2,1)S(1)}, u32[]{:S(2)}, u32[]{:S(2)}) collective-permute-start(bf16[192,512]{1,0:T(8,128)(2,1)S(1)} %collective-permute-done.15.refs_0_), channel_id=1, source_target_pairs={{0,1},{2,0},{4,2},{6,4},{7,6},{5,7},{3,5},{1,3},{8,9},{10,8},{12,1... | collective-permute-start | bytes 589832 | tf_op jit(solution)/shard_map/ppermute | solution.py:210
  60.1 0.4 collective-permute-start.25
  60.5 2.2 %collective-permute-done.20.refs_2_ = bf16[192,512]{1,0:T(8,128)(2,1)S(1)} collective-permute-done((bf16[192,512]{1,0:T(8,128)(2,1)S(1)}, bf16[192,512]{1,0:T(8,128)(2,1)S(1)}, u32[]{:S(2)}, u32[]{:S(2)}) %collective-permute-start.20) | collective-permute-done | bytes 196640 | tf_op jit(solution)/shard_map/ppermute | solution.py:210
  62.7 1.6 %collective-permute-start.27 = (bf16[192,512]{1,0:T(8,128)(2,1)S(1)}, bf16[192,512]{1,0:T(8,128)(2,1)S(1)}, u32[]{:S(2)}, u32[]{:S(2)}) collective-permute-start(bf16[192,512]{1,0:T(8,128)(2,1)S(1)} %collective-permute-done.20.refs_2_), channel_id=1, source_target_pairs={{0,1},{2,0},{4,2},{6,4},{7,6},{5,7},{3,5},{1,3},{8,9},{10,8},{12,1... | collective-permute-start | bytes 589832 | tf_op jit(solution)/shard_map/ppermute | solution.py:210
  64.3 0.3 collective-permute-done.23.refs_3_
  64.6 0.4 collective-permute-start.26
  65.0 0.2 collective-permute-done.24.refs_4_
  65.2 1.5 %collective-permute-done.25.refs_5_ = bf16[192,512]{1,0:T(8,128)(2,1)S(1)} collective-permute-done((bf16[192,512]{1,0:T(8,128)(2,1)S(1)}, bf16[192,512]{1,0:T(8,128)(2,1)S(1)}, u32[]{:S(2)}, u32[]{:S(2)}) %collective-permute-start.25) | collective-permute-done | bytes 196640 | tf_op jit(solution)/shard_map/ppermute | solution.py:210
  66.7 1.1 %shard_map.87 = (f32[192,640]{1,0:T(8,128)S(1)}, f32[192,128]{1,0:T(8,128)S(1)}) custom-call(bf16[192,512]{1,0:T(8,128)(2,1)S(1)} %collective-permute-done.15.refs_0_, bf16[192,512]{1,0:T(8,128)(2,1)S(1)} %collective-permute-done.17.refs_1_, bf16[192,512]{1,0:T(8,128)(2,1)S(1)} %collective-permute-done.20.refs_2_, ...), custom_call_target="tpu_custom_call" | custom-call | flops 754974720 | bytes 3932160 | tf_op jit(solution)/shard_map/pallas_call | solution.py:181
  67.8 1.2 %shard_map.88 = (f32[192,640]{1,0:T(8,128)S(1)}, f32[192,128]{1,0:T(8,128)S(1)}, bf16[192,1024]{1,0:T(8,128)(2,1)}) custom-call(bf16[192,512]{1,0:T(8,128)(2,1)S(1)} %shard_map.83.refs_0_, bf16[192,512]{1,0:T(8,128)(2,1)S(1)} %shard_map.84.refs_1_, f32[1,8192]{1,0:T(1,128)S(1)} %bitcast.6, bf16[8192,640]{1,0:T(8,128)(2,1)S(1)} %bitcast.2, ...), custom_call_target="tpu_custom_call" | custom-call | flops 251658240 | bytes 1310720 | tf_op jit(solution)/shard_map/pallas_call | solution.py:181
  69.1 0.3 shard_map.89
  69.4 0.9 %collective-permute-done.26.refs_0_ = bf16[192,512]{1,0:T(8,128)(2,1)S(1)} collective-permute-done((bf16[192,512]{1,0:T(8,128)(2,1)S(1)}, bf16[192,512]{1,0:T(8,128)(2,1)S(1)}, u32[]{:S(2)}, u32[]{:S(2)}) %collective-permute-start.26) | collective-permute-done | bytes 196640 | tf_op jit(solution)/shard_map/ppermute | solution.py:210
  70.3 1.0 %shard_map.90 = bf16[192,640]{1,0:T(8,128)(2,1)} custom-call(bf16[192,512]{1,0:T(8,128)(2,1)S(1)} %collective-permute-done.26.refs_0_, f32[1,8192]{1,0:T(1,128)S(1)} %bitcast.8, bf16[8192,640]{1,0:T(8,128)(2,1)S(1)} %bitcast.2, f32[192,640]{1,0:T(8,128)S(1)} %get-tuple-element.100.refs_3_, f32[192,128]{1,0:T(8,128)S(1)} %get-tuple-element.101.refs_4_), custom_call_target="tpu_custom_call" | custom-call | flops 125829120 | bytes 655360 | tf_op jit(solution)/shard_map/pallas_call | solution.py:181
  (42 shorter events, 1.2 us)
Async XLA Ops:
  3.4 9.0 %collective-permute-start.1 = (bf16[192,512]{1,0:T(8,128)(2,1)S(1)}, bf16[192,512]{1,0:T(8,128)(2,1)S(1)}, u32[]{:S(2)}, u32[]{:S(2)}) collective-permute-start(bf16[192,512]{1,0:T(8,128)(2,1)S(1)} %get-tuple-element.56), channel_id=1, source_target_pairs={{0,1},{2,0},{4,2},{6,4},{7,6},{5,7},{3,5},{1,3},{8,9},{10,8},{12,1... | collective-permute-start | bytes 589832 | tf_op jit(solution)/shard_map/ppermute | solution.py:210
  6.5 8.0 %collective-permute-start = (bf16[192,512]{1,0:T(8,128)(2,1)S(1)}, bf16[192,512]{1,0:T(8,128)(2,1)S(1)}, u32[]{:S(2)}, u32[]{:S(2)}) collective-permute-start(bf16[192,512]{1,0:T(8,128)(2,1)S(1)} %get-tuple-element.54), channel_id=1, source_target_pairs={{0,2},{2,4},{4,6},{6,7},{7,5},{5,3},{3,1},{1,0},{8,10},{10,12},{12... | collective-permute-start | bytes 589832 | tf_op jit(solution)/shard_map/ppermute | solution.py:210
  10.3 8.1 %collective-permute-start.5 = (bf16[192,512]{1,0:T(8,128)(2,1)S(1)}, bf16[192,512]{1,0:T(8,128)(2,1)S(1)}, u32[]{:S(2)}, u32[]{:S(2)}) collective-permute-start(bf16[192,512]{1,0:T(8,128)(2,1)S(1)} %get-tuple-element.66), channel_id=1, source_target_pairs={{0,1},{2,0},{4,2},{6,4},{7,6},{5,7},{3,5},{1,3},{8,9},{10,8},{12,1... | collective-permute-start | bytes 589832 | tf_op jit(solution)/shard_map/ppermute | solution.py:210
  12.3 8.1 %collective-permute-start.4 = (bf16[192,512]{1,0:T(8,128)(2,1)S(1)}, bf16[192,512]{1,0:T(8,128)(2,1)S(1)}, u32[]{:S(2)}, u32[]{:S(2)}) collective-permute-start(bf16[192,512]{1,0:T(8,128)(2,1)S(1)} %get-tuple-element.64), channel_id=1, source_target_pairs={{0,2},{2,4},{4,6},{6,7},{7,5},{5,3},{3,1},{1,0},{8,10},{10,12},{12... | collective-permute-start | bytes 589832 | tf_op jit(solution)/shard_map/ppermute | solution.py:210
  12.5 9.8 %collective-permute-start.3 = (bf16[192,512]{1,0:T(8,128)(2,1)S(1)}, bf16[192,512]{1,0:T(8,128)(2,1)S(1)}, u32[]{:S(2)}, u32[]{:S(2)}) collective-permute-start(bf16[192,512]{1,0:T(8,128)(2,1)S(1)} %get-tuple-element.62), channel_id=1, source_target_pairs={{0,1},{2,0},{4,2},{6,4},{7,6},{5,7},{3,5},{1,3},{8,9},{10,8},{12,1... | collective-permute-start | bytes 589832 | tf_op jit(solution)/shard_map/ppermute | solution.py:210
  14.5 9.6 %collective-permute-start.2 = (bf16[192,512]{1,0:T(8,128)(2,1)S(1)}, bf16[192,512]{1,0:T(8,128)(2,1)S(1)}, u32[]{:S(2)}, u32[]{:S(2)}) collective-permute-start(bf16[192,512]{1,0:T(8,128)(2,1)S(1)} %get-tuple-element.60), channel_id=1, source_target_pairs={{0,2},{2,4},{4,6},{6,7},{7,5},{5,3},{3,1},{1,0},{8,10},{10,12},{12... | collective-permute-start | bytes 589832 | tf_op jit(solution)/shard_map/ppermute | solution.py:210
  18.5 10.0 %collective-permute-start.9 = (bf16[192,512]{1,0:T(8,128)(2,1)S(1)}, bf16[192,512]{1,0:T(8,128)(2,1)S(1)}, u32[]{:S(2)}, u32[]{:S(2)}) collective-permute-start(bf16[192,512]{1,0:T(8,128)(2,1)S(1)} %get-tuple-element.78), channel_id=1, source_target_pairs={{0,1},{2,0},{4,2},{6,4},{7,6},{5,7},{3,5},{1,3},{8,9},{10,8},{12,1... | collective-permute-start | bytes 589832 | tf_op jit(solution)/shard_map/ppermute | solution.py:210
  20.5 9.7 %collective-permute-start.8 = (bf16[192,512]{1,0:T(8,128)(2,1)S(1)}, bf16[192,512]{1,0:T(8,128)(2,1)S(1)}, u32[]{:S(2)}, u32[]{:S(2)}) collective-permute-start(bf16[192,512]{1,0:T(8,128)(2,1)S(1)} %get-tuple-element.76), channel_id=1, source_target_pairs={{0,2},{2,4},{4,6},{6,7},{7,5},{5,3},{3,1},{1,0},{8,10},{10,12},{12... | collective-permute-start | bytes 589832 | tf_op jit(solution)/shard_map/ppermute | solution.py:210
  22.4 8.4 %collective-permute-start.7 = (bf16[192,512]{1,0:T(8,128)(2,1)S(1)}, bf16[192,512]{1,0:T(8,128)(2,1)S(1)}, u32[]{:S(2)}, u32[]{:S(2)}) collective-permute-start(bf16[192,512]{1,0:T(8,128)(2,1)S(1)} %get-tuple-element.74), channel_id=1, source_target_pairs={{0,1},{2,0},{4,2},{6,4},{7,6},{5,7},{3,5},{1,3},{8,9},{10,8},{12,1... | collective-permute-start | bytes 589832 | tf_op jit(solution)/shard_map/ppermute | solution.py:210
  24.1 8.5 %collective-permute-start.6 = (bf16[192,512]{1,0:T(8,128)(2,1)S(1)}, bf16[192,512]{1,0:T(8,128)(2,1)S(1)}, u32[]{:S(2)}, u32[]{:S(2)}) collective-permute-start(bf16[192,512]{1,0:T(8,128)(2,1)S(1)} %get-tuple-element.72), channel_id=1, source_target_pairs={{0,2},{2,4},{4,6},{6,7},{7,5},{5,3},{3,1},{1,0},{8,10},{10,12},{12... | collective-permute-start | bytes 589832 | tf_op jit(solution)/shard_map/ppermute | solution.py:210
  24.5 13.3 %copy-start = (bf16[192,1024]{1,0:T(8,128)(2,1)S(1)}, bf16[192,1024]{1,0:T(8,128)(2,1)}, u32[]{:S(2)}) copy-start(bf16[192,1024]{1,0:T(8,128)(2,1)} %residual_ref.3) | copy-start | bytes 1179652
  24.6 22.9 %slice-start = ((s8[10485760]{0:T(1024)(128)(4,1)}), s8[4194304]{0:T(1024)(128)(4,1)S(1)}, s32[]{:S(2)}) async-start(s8[10485760]{0:T(1024)(128)(4,1)} %bitcast.1), calls=%async_computation | async-start | bytes 8388608
  24.6 22.9 %slice-start.1 = ((s8[10485760]{0:T(1024)(128)(4,1)}), s8[4194304]{0:T(1024)(128)(4,1)S(1)}, s32[]{:S(2)}) async-start(s8[10485760]{0:T(1024)(128)(4,1)} %bitcast.1), calls=%async_computation.1 | async-start | bytes 8388608
  24.6 22.9 %copy-start.1 = (f32[8192]{0:T(1024)S(1)}, f32[8192]{0:T(1024)}, u32[]{:S(2)}) copy-start(f32[8192]{0:T(1024)} %param.8) | copy-start | bytes 98308
  28.6 11.0 %collective-permute-start.11 = (bf16[192,512]{1,0:T(8,128)(2,1)S(1)}, bf16[192,512]{1,0:T(8,128)(2,1)S(1)}, u32[]{:S(2)}, u32[]{:S(2)}) collective-permute-start(bf16[192,512]{1,0:T(8,128)(2,1)S(1)} %get-tuple-element.85), channel_id=1, source_target_pairs={{0,1},{2,0},{4,2},{6,4},{7,6},{5,7},{3,5},{1,3},{8,9},{10,8},{12,1... | collective-permute-start | bytes 589832 | tf_op jit(solution)/shard_map/ppermute | solution.py:210
  30.3 6.8 %collective-permute-start.12 = (bf16[192,512]{1,0:T(8,128)(2,1)S(1)}, bf16[192,512]{1,0:T(8,128)(2,1)S(1)}, u32[]{:S(2)}, u32[]{:S(2)}) collective-permute-start(bf16[192,512]{1,0:T(8,128)(2,1)S(1)} %get-tuple-element.87), channel_id=1, source_target_pairs={{0,2},{2,4},{4,6},{6,7},{7,5},{5,3},{3,1},{1,0},{8,10},{10,12},{12... | collective-permute-start | bytes 589832 | tf_op jit(solution)/shard_map/ppermute | solution.py:210
  30.8 7.0 %collective-permute-start.13 = (bf16[192,512]{1,0:T(8,128)(2,1)S(1)}, bf16[192,512]{1,0:T(8,128)(2,1)S(1)}, u32[]{:S(2)}, u32[]{:S(2)}) collective-permute-start(bf16[192,512]{1,0:T(8,128)(2,1)S(1)} %get-tuple-element.88), channel_id=1, source_target_pairs={{0,1},{2,0},{4,2},{6,4},{7,6},{5,7},{3,5},{1,3},{8,9},{10,8},{12,1... | collective-permute-start | bytes 589832 | tf_op jit(solution)/shard_map/ppermute | solution.py:210
  32.6 7.0 %collective-permute-start.10 = (bf16[192,512]{1,0:T(8,128)(2,1)S(1)}, bf16[192,512]{1,0:T(8,128)(2,1)S(1)}, u32[]{:S(2)}, u32[]{:S(2)}) collective-permute-start(bf16[192,512]{1,0:T(8,128)(2,1)S(1)} %get-tuple-element.84), channel_id=1, source_target_pairs={{0,2},{2,4},{4,6},{6,7},{7,5},{5,3},{3,1},{1,0},{8,10},{10,12},{12... | collective-permute-start | bytes 589832 | tf_op jit(solution)/shard_map/ppermute | solution.py:210
  33.0 14.5 %slice-start.2 = ((s8[10485760]{0:T(1024)(128)(4,1)}), s8[2097152]{0:T(1024)(128)(4,1)S(1)}, s32[]{:S(2)}) async-start(s8[10485760]{0:T(1024)(128)(4,1)} %bitcast.1), calls=%async_computation.2 | async-start | bytes 4194304
  37.9 7.9 %collective-permute-start.18 = (bf16[192,512]{1,0:T(8,128)(2,1)S(1)}, bf16[192,512]{1,0:T(8,128)(2,1)S(1)}, u32[]{:S(2)}, u32[]{:S(2)}) collective-permute-start(bf16[192,512]{1,0:T(8,128)(2,1)S(1)} %shard_map.84.refs_1_), channel_id=1, source_target_pairs={{0,1},{2,0},{4,2},{6,4},{7,6},{5,7},{3,5},{1,3},{8,9},{10,8},{12,1... | collective-permute-start | bytes 589832 | tf_op jit(solution)/shard_map/ppermute | solution.py:210
  39.7 7.7 %collective-permute-start.21 = (bf16[192,512]{1,0:T(8,128)(2,1)S(1)}, bf16[192,512]{1,0:T(8,128)(2,1)S(1)}, u32[]{:S(2)}, u32[]{:S(2)}) collective-permute-start(bf16[192,512]{1,0:T(8,128)(2,1)S(1)} %shard_map.83.refs_0_), channel_id=1, source_target_pairs={{0,2},{2,4},{4,6},{6,7},{7,5},{5,3},{3,1},{1,0},{8,10},{10,12},{12... | collective-permute-start | bytes 589832 | tf_op jit(solution)/shard_map/ppermute | solution.py:210
  40.2 9.9 %collective-permute-start.14 = (bf16[192,512]{1,0:T(8,128)(2,1)S(1)}, bf16[192,512]{1,0:T(8,128)(2,1)S(1)}, u32[]{:S(2)}, u32[]{:S(2)}) collective-permute-start(bf16[192,512]{1,0:T(8,128)(2,1)S(1)} %shard_map.83.refs_0_), channel_id=1, source_target_pairs={{0,1},{2,0},{4,2},{6,4},{7,6},{5,7},{3,5},{1,3},{8,9},{10,8},{12,1... | collective-permute-start | bytes 589832 | tf_op jit(solution)/shard_map/ppermute | solution.py:210
  41.8 9.9 %collective-permute-start.16 = (bf16[192,512]{1,0:T(8,128)(2,1)S(1)}, bf16[192,512]{1,0:T(8,128)(2,1)S(1)}, u32[]{:S(2)}, u32[]{:S(2)}) collective-permute-start(bf16[192,512]{1,0:T(8,128)(2,1)S(1)} %shard_map.84.refs_1_), channel_id=1, source_target_pairs={{0,2},{2,4},{4,6},{6,7},{7,5},{5,3},{3,1},{1,0},{8,10},{10,12},{12... | collective-permute-start | bytes 589832 | tf_op jit(solution)/shard_map/ppermute | solution.py:210
  45.8 8.4 %collective-permute-start.19 = (bf16[192,512]{1,0:T(8,128)(2,1)S(1)}, bf16[192,512]{1,0:T(8,128)(2,1)S(1)}, u32[]{:S(2)}, u32[]{:S(2)}) collective-permute-start(bf16[192,512]{1,0:T(8,128)(2,1)S(1)} %collective-permute-done.18.refs_0_), channel_id=1, source_target_pairs={{0,1},{2,0},{4,2},{6,4},{7,6},{5,7},{3,5},{1,3},{8,9},{10,8},{12,1... | collective-permute-start | bytes 589832 | tf_op jit(solution)/shard_map/ppermute | solution.py:210
  48.0 7.9 %collective-permute-start.22 = (bf16[192,512]{1,0:T(8,128)(2,1)S(1)}, bf16[192,512]{1,0:T(8,128)(2,1)S(1)}, u32[]{:S(2)}, u32[]{:S(2)}) collective-permute-start(bf16[192,512]{1,0:T(8,128)(2,1)S(1)} %get-tuple-element.89), channel_id=1, source_target_pairs={{0,2},{2,4},{4,6},{6,7},{7,5},{5,3},{3,1},{1,0},{8,10},{10,12},{12... | collective-permute-start | bytes 589832 | tf_op jit(solution)/shard_map/ppermute | solution.py:210
  50.0 8.4 %collective-permute-start.15 = (bf16[192,512]{1,0:T(8,128)(2,1)S(1)}, bf16[192,512]{1,0:T(8,128)(2,1)S(1)}, u32[]{:S(2)}, u32[]{:S(2)}) collective-permute-start(bf16[192,512]{1,0:T(8,128)(2,1)S(1)} %collective-permute-done.14.refs_0_), channel_id=1, source_target_pairs={{0,1},{2,0},{4,2},{6,4},{7,6},{5,7},{3,5},{1,3},{8,9},{10,8},{12,1... | collective-permute-start | bytes 589832 | tf_op jit(solution)/shard_map/ppermute | solution.py:210
  51.7 8.4 %collective-permute-start.17 = (bf16[192,512]{1,0:T(8,128)(2,1)S(1)}, bf16[192,512]{1,0:T(8,128)(2,1)S(1)}, u32[]{:S(2)}, u32[]{:S(2)}) collective-permute-start(bf16[192,512]{1,0:T(8,128)(2,1)S(1)} %collective-permute-done.16.refs_1_), channel_id=1, source_target_pairs={{0,2},{2,4},{4,6},{6,7},{7,5},{5,3},{3,1},{1,0},{8,10},{10,12},{12... | collective-permute-start | bytes 589832 | tf_op jit(solution)/shard_map/ppermute | solution.py:210
  54.3 8.4 %collective-permute-start.20 = (bf16[192,512]{1,0:T(8,128)(2,1)S(1)}, bf16[192,512]{1,0:T(8,128)(2,1)S(1)}, u32[]{:S(2)}, u32[]{:S(2)}) collective-permute-start(bf16[192,512]{1,0:T(8,128)(2,1)S(1)} %collective-permute-done.19.refs_2_), channel_id=1, source_target_pairs={{0,1},{2,0},{4,2},{6,4},{7,6},{5,7},{3,5},{1,3},{8,9},{10,8},{12,1... | collective-permute-start | bytes 589832 | tf_op jit(solution)/shard_map/ppermute | solution.py:210
  56.7 7.9 %collective-permute-start.23 = (bf16[192,512]{1,0:T(8,128)(2,1)S(1)}, bf16[192,512]{1,0:T(8,128)(2,1)S(1)}, u32[]{:S(2)}, u32[]{:S(2)}) collective-permute-start(bf16[192,512]{1,0:T(8,128)(2,1)S(1)} %get-tuple-element.92), channel_id=1, source_target_pairs={{0,2},{2,4},{4,6},{6,7},{7,5},{5,3},{3,1},{1,0},{8,10},{10,12},{12... | collective-permute-start | bytes 589832 | tf_op jit(solution)/shard_map/ppermute | solution.py:210
  58.5 6.8 %collective-permute-start.24 = (bf16[192,512]{1,0:T(8,128)(2,1)S(1)}, bf16[192,512]{1,0:T(8,128)(2,1)S(1)}, u32[]{:S(2)}, u32[]{:S(2)}) collective-permute-start(bf16[192,512]{1,0:T(8,128)(2,1)S(1)} %collective-permute-done.15.refs_0_), channel_id=1, source_target_pairs={{0,1},{2,0},{4,2},{6,4},{7,6},{5,7},{3,5},{1,3},{8,9},{10,8},{12,1... | collective-permute-start | bytes 589832 | tf_op jit(solution)/shard_map/ppermute | solution.py:210
  60.1 6.6 %collective-permute-start.25 = (bf16[192,512]{1,0:T(8,128)(2,1)S(1)}, bf16[192,512]{1,0:T(8,128)(2,1)S(1)}, u32[]{:S(2)}, u32[]{:S(2)}) collective-permute-start(bf16[192,512]{1,0:T(8,128)(2,1)S(1)} %collective-permute-done.17.refs_1_), channel_id=1, source_target_pairs={{0,2},{2,4},{4,6},{6,7},{7,5},{5,3},{3,1},{1,0},{8,10},{10,12},{12... | collective-permute-start | bytes 589832 | tf_op jit(solution)/shard_map/ppermute | solution.py:210
  62.7 6.4 %collective-permute-start.27 = (bf16[192,512]{1,0:T(8,128)(2,1)S(1)}, bf16[192,512]{1,0:T(8,128)(2,1)S(1)}, u32[]{:S(2)}, u32[]{:S(2)}) collective-permute-start(bf16[192,512]{1,0:T(8,128)(2,1)S(1)} %collective-permute-done.20.refs_2_), channel_id=1, source_target_pairs={{0,1},{2,0},{4,2},{6,4},{7,6},{5,7},{3,5},{1,3},{8,9},{10,8},{12,1... | collective-permute-start | bytes 589832 | tf_op jit(solution)/shard_map/ppermute | solution.py:210
  64.6 5.7 %collective-permute-start.26 = (bf16[192,512]{1,0:T(8,128)(2,1)S(1)}, bf16[192,512]{1,0:T(8,128)(2,1)S(1)}, u32[]{:S(2)}, u32[]{:S(2)}) collective-permute-start(bf16[192,512]{1,0:T(8,128)(2,1)S(1)} %collective-permute-done.23.refs_3_), channel_id=1, source_target_pairs={{0,2},{2,4},{4,6},{6,7},{7,5},{5,3},{3,1},{1,0},{8,10},{10,12},{12... | collective-permute-start | bytes 589832 | tf_op jit(solution)/shard_map/ppermute | solution.py:210
